TPU v7x, 32 devices: a whole 2x2x4 slice. The times are simulated.
32 devices in a mesh: row: 8 (over z, core), seq: 4 (over y, x).
Axes of the slice: x: 2, y: 2, z: 4, core: 2. Of those that a mesh axis runs over, the one named last changes fastest.
Arguments:
- frames: bfloat16 [8, 2048, 1536], P('row', 'seq'), may hold values from -6 to 6
- context: bfloat16 [8, 128, 768], P('row'), may hold values from -6 to 6
- seg_lengths: int32 [8, 8], P('row'), may hold values from 1 to 2041, as said below
- bucket_ids: int32 [8], replicated, may hold values from 0 to 4, as said below
- timesteps: int32 [5], replicated, may hold values from 0 to 999
- bucket_weights: float32 [5], replicated, may hold values from 0.5 to 2
- w_time_in: bfloat16 [256, 1536], P(('row', 'seq')), may hold values from -0.5 to 0.5
- w_time_out: bfloat16 [1536, 1536], P(('row', 'seq')), may hold values from -0.15625 to 0.15625
- w_mod: bfloat16 [1536, 9216], P(('row', 'seq')), may hold values from -0.15625 to 0.15625
- w_qkv: bfloat16 [1536, 4608], P(('row', 'seq')), may hold values from -0.15625 to 0.15625
- w_attn_out: bfloat16 [1536, 1536], P(('row', 'seq')), may hold values from -0.875 to 0.875
- cross_gain: bfloat16 [1536], P(('row', 'seq')), may hold values from 0.099609375 to 1.8984375
- w_cross_q: bfloat16 [1536, 1536], P(('row', 'seq')), may hold values from -0.15625 to 0.15625
- w_cross_kv: bfloat16 [768, 3072], P(('row', 'seq')), may hold values from -0.21875 to 0.21875
- w_cross_out: bfloat16 [1536, 1536], P(('row', 'seq')), may hold values from -0.4375 to 0.4375
- w_glu: bfloat16 [1536, 12288], P(('row', 'seq')), may hold values from -0.15625 to 0.15625
- w_down: bfloat16 [6144, 1536], P(('row', 'seq')), may hold values from -0.078125 to 0.078125
- cotangent: bfloat16 [8, 2048, 1536], P('row', 'seq'), may hold values from -6 to 6
Outputs:
- out: bfloat16 [8, 2048, 1536], P('row', 'seq')
- grad_frames: float32 [8, 2048, 1536], P('row', 'seq')
- grad_time_in: float32 [256, 1536], P(('row', 'seq'))
- grad_time_out: float32 [1536, 1536], P(('row', 'seq'))
- grad_mod: float32 [1536, 9216], P(('row', 'seq'))
- grad_qkv: float32 [1536, 4608], P(('row', 'seq'))
- grad_attn_out: float32 [1536, 1536], P(('row', 'seq'))
- grad_cross_gain: float32 [1536], P(('row', 'seq'))
- grad_cross_q: float32 [1536, 1536], P(('row', 'seq'))
- grad_cross_kv: float32 [768, 3072], P(('row', 'seq'))
- grad_cross_out: float32 [1536, 1536], P(('row', 'seq'))
- grad_glu: float32 [1536, 12288], P(('row', 'seq'))
- grad_down: float32 [6144, 1536], P(('row', 'seq'))
Inputs may be any that keep to these rules, and one draw needn't show every extreme that they name: `seg_lengths`: each row's 8 lengths are positive and sum to 2048; some row holds a clip of exactly 2041 frames. `bucket_ids`: never falling along the rows, and each of the 5 buckets holds at least one row.
All inputs are finite; a program needn't handle non-finite values.
Results may differ from a plain program's by a relative error of at most 0.02.
Values may be sent and summed in bfloat16 or wider, within the bound.
No kernel may reach another device: no remote copies, remote signals or barrier semaphores. Data moves between devices by JAX's collectives and lax.ppermute only.
A program may use at most 640 MiB of HBM per device.

v0:
```python
import math

import jax
import jax.numpy as jnp
from jax import lax
from jax.sharding import PartitionSpec as P

D = 1536
HEADS = 24
HEAD_DIM = 64
FF = 6144
TFREQ = 256
LENGTH = 2048
BUCKETS = 5


highest = lax.Precision.HIGHEST


def matmul(left, right):
    return jnp.einsum("...i,ij->...j", left, right, preferred_element_type=jnp.float32)


def matmul_t(left, right):
    return jnp.einsum("...j,ij->...i", left, right, preferred_element_type=jnp.float32)


def outer_sum(left, right):
    return jnp.einsum("rfi,rfj->ij", left, right, preferred_element_type=jnp.float32)


def layer_stats(values):
    center = values - jnp.mean(values, axis=-1, keepdims=True)
    inv_std = lax.rsqrt(jnp.mean(center * center, axis=-1, keepdims=True) + 1e-05)
    return (center * inv_std, inv_std)


def norm_back(grad_normed, normed, inv_std):
    return inv_std * (
        grad_normed
        - jnp.mean(grad_normed, axis=-1, keepdims=True)
        - normed * jnp.mean(grad_normed * normed, axis=-1, keepdims=True)
    )


def silu_slope(values):
    sigmoid_part = jax.nn.sigmoid(values)
    return sigmoid_part * (1.0 + values * (1.0 - sigmoid_part))


def angle_tables(positions):
    half_dim = HEAD_DIM // 2
    inverse = jnp.exp(-math.log(10000.0) * jnp.arange(half_dim, dtype=jnp.float32) / half_dim)
    angles = positions[:, None] * inverse[None, :]
    return (jnp.cos(angles)[:, None, :], jnp.sin(angles)[:, None, :])


def rotate(values, cosine, sine_table):
    half_dim = values.shape[-1] // 2
    first_half = values[..., :half_dim]
    second_half = values[..., half_dim:]
    return jnp.concatenate(
        [
            first_half * cosine - second_half * sine_table,
            second_half * cosine + first_half * sine_table,
        ],
        axis=-1,
    )


def time_features(times):
    half_dim = TFREQ // 2
    freqs = jnp.exp(-math.log(10000.0) * jnp.arange(half_dim, dtype=jnp.float32) / half_dim)
    angles = times[:, None] * freqs[None, :]
    return jnp.concatenate([jnp.cos(angles), jnp.sin(angles)], axis=-1)


def stamp_rows(times, time_in, time_out, modul):
    features = time_features(times).astype(jnp.bfloat16)
    pre_hidden = jnp.dot(features, time_in, preferred_element_type=jnp.float32)
    time_hidden = jax.nn.silu(pre_hidden).astype(jnp.bfloat16)
    time_token = jnp.dot(time_hidden, time_out, preferred_element_type=jnp.float32)
    token_act = jax.nn.silu(time_token).astype(jnp.bfloat16)
    modulation = jnp.dot(token_act, modul, preferred_element_type=jnp.float32)
    return (features, pre_hidden, time_hidden, time_token, token_act, modulation)


def self_forward(row_inputs):
    query_row, key_row, value_row, local_row, whole_row = row_inputs
    allowed = local_row[:, None] == whole_row[None, :]
    scores = (
        jnp.einsum("qhd,khd->hqk", query_row, key_row, preferred_element_type=jnp.float32) * 0.125
    )
    scores = jnp.where(allowed[None], scores, -1e30)
    row_max = jnp.max(scores, axis=-1, keepdims=True)
    shifted = jnp.exp(scores - row_max)
    denominator = jnp.sum(shifted, axis=-1, keepdims=True)
    soft_weights = (shifted / denominator).astype(jnp.bfloat16)
    mixed = jnp.einsum("hqk,khd->qhd", soft_weights, value_row, preferred_element_type=jnp.float32)
    return (mixed.astype(jnp.bfloat16), row_max + jnp.log(denominator))


def self_backward(row_inputs):
    query_row, key_row, value_row, grad_row, log_row, local_row, whole_row = row_inputs
    allowed = local_row[:, None] == whole_row[None, :]
    scores = (
        jnp.einsum("qhd,khd->hqk", query_row, key_row, preferred_element_type=jnp.float32) * 0.125
    )
    soft_again = jnp.exp(jnp.where(allowed[None], scores, -1e30) - log_row)
    grad_soft = jnp.einsum("qhd,khd->hqk", grad_row, value_row, preferred_element_type=jnp.float32)
    grad_scores = (
        soft_again * (grad_soft - jnp.sum(soft_again * grad_soft, axis=-1, keepdims=True))
    ).astype(jnp.bfloat16)
    grad_query = (
        jnp.einsum("hqk,khd->qhd", grad_scores, key_row, preferred_element_type=jnp.float32) * 0.125
    )
    key_part = (
        jnp.einsum("hqk,qhd->khd", grad_scores, query_row, preferred_element_type=jnp.float32)
        * 0.125
    )
    value_part = jnp.einsum(
        "hqk,qhd->khd",
        soft_again.astype(jnp.bfloat16),
        grad_row,
        preferred_element_type=jnp.float32,
    )
    return (grad_query, key_part, value_part)


def on_device(
    frames,
    context,
    seg_lengths,
    bucket_ids,
    timesteps,
    bucket_weights,
    w_time_in,
    w_time_out,
    w_mod,
    w_qkv,
    w_attn_out,
    cross_gain,
    w_cross_q,
    w_cross_kv,
    w_cross_out,
    w_glu,
    w_down,
    cotangent,
):
    fwd_weights = (
        lax.all_gather(w_time_in, ("row", "seq"), axis=0, tiled=True),
        lax.all_gather(w_time_out, ("row", "seq"), axis=0, tiled=True),
        lax.all_gather(w_mod, ("row", "seq"), axis=0, tiled=True),
        lax.all_gather(w_qkv, ("row", "seq"), axis=0, tiled=True),
        lax.all_gather(w_attn_out, ("row", "seq"), axis=0, tiled=True),
        lax.all_gather(cross_gain, ("row", "seq"), axis=0, tiled=True),
        lax.all_gather(w_cross_q, ("row", "seq"), axis=0, tiled=True),
        lax.all_gather(w_cross_kv, ("row", "seq"), axis=0, tiled=True),
        lax.all_gather(w_cross_out, ("row", "seq"), axis=0, tiled=True),
        lax.all_gather(w_glu, ("row", "seq"), axis=0, tiled=True),
        lax.all_gather(w_down, ("row", "seq"), axis=0, tiled=True),
    )
    (
        time_in,
        time_out,
        modul,
        qkv_w,
        attn_w,
        gain_w,
        crossq_w,
        crosskv_w,
        crossout_w,
        glu_w,
        down_w,
    ) = fwd_weights
    rows_here = frames.shape[0]
    frames_here = frames.shape[1]
    text_len = context.shape[1]
    row_start = lax.axis_index("row") * rows_here
    seq_start = lax.axis_index("seq") * frames_here
    my_buckets = lax.dynamic_slice_in_dim(bucket_ids, row_start, rows_here)
    onehot = (my_buckets[:, None] == jnp.arange(BUCKETS, dtype=jnp.int32)[None, :]).astype(
        jnp.float32
    )
    my_times = jnp.dot(onehot, timesteps.astype(jnp.float32), precision=highest)
    features, pre_hidden, time_hidden, time_token, token_act, modulation = stamp_rows(
        my_times, time_in, time_out, modul
    )
    shift_attn = modulation[:, None, 0:D]
    scale_attn = modulation[:, None, D : 2 * D]
    gate_attn = modulation[:, None, 2 * D : 3 * D]
    shift_ffn = modulation[:, None, 3 * D : 4 * D]
    scale_ffn = modulation[:, None, 4 * D : 5 * D]
    gate_ffn = modulation[:, None, 5 * D : 6 * D]
    bounds = jnp.cumsum(seg_lengths, axis=-1)
    all_positions = jnp.arange(LENGTH, dtype=jnp.int32)
    all_ids = jnp.sum(
        (all_positions[None, :, None] >= bounds[:, None, :]).astype(jnp.int32), axis=-1
    )
    local_ids = lax.dynamic_slice_in_dim(all_ids, seq_start, frames_here, 1)
    cosine, sine_table = angle_tables(
        (seq_start + jnp.arange(frames_here, dtype=jnp.int32)).astype(jnp.float32)
    )
    inputs = frames.astype(jnp.float32)
    normed_a, inv_a = layer_stats(inputs)
    attn_in = (normed_a * (1.0 + scale_attn) + shift_attn).astype(jnp.bfloat16)
    projected = matmul(attn_in, qkv_w)
    query_pre = projected[..., :D].reshape(rows_here, frames_here, HEADS, HEAD_DIM)
    key_pre = projected[..., D : 2 * D].reshape(rows_here, frames_here, HEADS, HEAD_DIM)
    value_pre = projected[..., 2 * D :].reshape(rows_here, frames_here, HEADS, HEAD_DIM)
    queries = rotate(query_pre, cosine, sine_table).astype(jnp.bfloat16)
    key_local = rotate(key_pre, cosine, sine_table).astype(jnp.bfloat16)
    value_local = value_pre.astype(jnp.bfloat16)
    key_rows, value_rows = (
        lax.all_gather(key_local, "seq", axis=1, tiled=True),
        lax.all_gather(value_local, "seq", axis=1, tiled=True),
    )
    mixed_rows, log_total = lax.map(
        self_forward, (queries, key_rows, value_rows, local_ids, all_ids)
    )
    attn_mixed = mixed_rows.reshape(rows_here, frames_here, D)
    attn_out = matmul(attn_mixed, attn_w)
    after_attn = inputs + gate_attn * attn_out
    normed_c, inv_c = layer_stats(after_attn)
    gain_values = gain_w.astype(jnp.float32)
    cross_in = (normed_c * gain_values).astype(jnp.bfloat16)
    cross_q = (
        matmul(cross_in, crossq_w)
        .astype(jnp.bfloat16)
        .reshape(rows_here, frames_here, HEADS, HEAD_DIM)
    )
    cross_kv = jnp.einsum(
        "rcm,me->rce", context, crosskv_w, preferred_element_type=jnp.float32
    ).astype(jnp.bfloat16)
    cross_k = cross_kv[..., :D].reshape(rows_here, text_len, HEADS, HEAD_DIM)
    cross_v = cross_kv[..., D:].reshape(rows_here, text_len, HEADS, HEAD_DIM)
    cross_scores = (
        jnp.einsum("rqhd,rchd->rhqc", cross_q, cross_k, preferred_element_type=jnp.float32) * 0.125
    )
    cross_shift = jnp.exp(cross_scores - jnp.max(cross_scores, axis=-1, keepdims=True))
    cross_soft = cross_shift / jnp.sum(cross_shift, axis=-1, keepdims=True)
    cross_soft_low = cross_soft.astype(jnp.bfloat16)
    cross_mixed = (
        jnp.einsum("rhqc,rchd->rqhd", cross_soft_low, cross_v, preferred_element_type=jnp.float32)
        .reshape(rows_here, frames_here, D)
        .astype(jnp.bfloat16)
    )
    cross_out = matmul(cross_mixed, crossout_w)
    after_cross = after_attn + cross_out
    normed_f, inv_f = layer_stats(after_cross)
    ffn_in = (normed_f * (1.0 + scale_ffn) + shift_ffn).astype(jnp.bfloat16)
    gate_up = matmul(ffn_in, glu_w)
    gate_pre = gate_up[..., :FF]
    up_pre = gate_up[..., FF:]
    gate_act = jax.nn.silu(gate_pre)
    hidden = (gate_act * up_pre).astype(jnp.bfloat16)
    ffn_out = matmul(hidden, down_w)
    result = (after_cross + gate_ffn * ffn_out).astype(jnp.bfloat16)
    bwd_weights = (
        lax.all_gather(w_time_in, ("row", "seq"), axis=0, tiled=True),
        lax.all_gather(w_time_out, ("row", "seq"), axis=0, tiled=True),
        lax.all_gather(w_mod, ("row", "seq"), axis=0, tiled=True),
        lax.all_gather(w_qkv, ("row", "seq"), axis=0, tiled=True),
        lax.all_gather(w_attn_out, ("row", "seq"), axis=0, tiled=True),
        lax.all_gather(cross_gain, ("row", "seq"), axis=0, tiled=True),
        lax.all_gather(w_cross_q, ("row", "seq"), axis=0, tiled=True),
        lax.all_gather(w_cross_kv, ("row", "seq"), axis=0, tiled=True),
        lax.all_gather(w_cross_out, ("row", "seq"), axis=0, tiled=True),
        lax.all_gather(w_glu, ("row", "seq"), axis=0, tiled=True),
        lax.all_gather(w_down, ("row", "seq"), axis=0, tiled=True),
    )
    (
        time_in,
        time_out,
        modul,
        qkv_w,
        attn_w,
        gain_w,
        crossq_w,
        crosskv_w,
        crossout_w,
        glu_w,
        down_w,
    ) = bwd_weights
    row_scale = jnp.dot(onehot, bucket_weights, precision=highest)
    grad_out = cotangent.astype(jnp.float32) * row_scale[:, None, None]
    grad_ffn_low = (gate_ffn * grad_out).astype(jnp.bfloat16)
    dgate_ffn = jnp.sum(grad_out * ffn_out, axis=1)
    grad_down = outer_sum(hidden, grad_ffn_low)
    grad_hidden = matmul_t(grad_ffn_low, down_w)
    grad_gate_up = jnp.concatenate(
        [grad_hidden * up_pre * silu_slope(gate_pre), grad_hidden * gate_act], axis=-1
    ).astype(jnp.bfloat16)
    grad_glu = outer_sum(ffn_in, grad_gate_up)
    grad_ffn_in = matmul_t(grad_gate_up, glu_w)
    dshift_ffn = jnp.sum(grad_ffn_in, axis=1)
    dscale_ffn = jnp.sum(grad_ffn_in * normed_f, axis=1)
    grad_cross = grad_out + norm_back(grad_ffn_in * (1.0 + scale_ffn), normed_f, inv_f)
    ffn_grads = (
        lax.psum_scatter(grad_glu, ("row", "seq"), scatter_dimension=0, tiled=True),
        lax.psum_scatter(grad_down, ("row", "seq"), scatter_dimension=0, tiled=True),
    )
    grad_cross_low = grad_cross.astype(jnp.bfloat16)
    grad_crossout = outer_sum(cross_mixed, grad_cross_low)
    grad_cmixed = (
        matmul_t(grad_cross_low, crossout_w)
        .astype(jnp.bfloat16)
        .reshape(rows_here, frames_here, HEADS, HEAD_DIM)
    )
    grad_csoft = jnp.einsum(
        "rqhd,rchd->rhqc", grad_cmixed, cross_v, preferred_element_type=jnp.float32
    )
    grad_cvalue = jnp.einsum(
        "rhqc,rqhd->rchd", cross_soft_low, grad_cmixed, preferred_element_type=jnp.float32
    )
    grad_cscores = (
        cross_soft * (grad_csoft - jnp.sum(cross_soft * grad_csoft, axis=-1, keepdims=True))
    ).astype(jnp.bfloat16)
    grad_cquery = (
        (
            jnp.einsum("rhqc,rchd->rqhd", grad_cscores, cross_k, preferred_element_type=jnp.float32)
            * 0.125
        )
        .reshape(rows_here, frames_here, D)
        .astype(jnp.bfloat16)
    )
    grad_ckey = (
        jnp.einsum("rhqc,rqhd->rchd", grad_cscores, cross_q, preferred_element_type=jnp.float32)
        * 0.125
    )
    grad_ckv = jnp.concatenate(
        [grad_ckey.reshape(rows_here, text_len, D), grad_cvalue.reshape(rows_here, text_len, D)],
        axis=-1,
    )
    grad_crosskv = jnp.einsum(
        "rcm,rce->me", context.astype(jnp.float32), grad_ckv, precision=highest
    )
    grad_crossq = outer_sum(cross_in, grad_cquery)
    grad_cross_in = matmul_t(grad_cquery, crossq_w)
    grad_gain = jnp.sum(grad_cross_in * normed_c, axis=(0, 1))
    grad_attn = grad_cross + norm_back(grad_cross_in * gain_values, normed_c, inv_c)
    grad_attn_low = (gate_attn * grad_attn).astype(jnp.bfloat16)
    dgate_attn = jnp.sum(grad_attn * attn_out, axis=1)
    grad_attnout = outer_sum(attn_mixed, grad_attn_low)
    grad_amixed = (
        matmul_t(grad_attn_low, attn_w)
        .astype(jnp.bfloat16)
        .reshape(rows_here, frames_here, HEADS, HEAD_DIM)
    )
    grad_query, key_part, value_part = lax.map(
        self_backward, (queries, key_rows, value_rows, grad_amixed, log_total, local_ids, all_ids)
    )
    grad_key, grad_value = (
        lax.psum_scatter(
            key_part.astype(jnp.bfloat16), "seq", scatter_dimension=1, tiled=True
        ).astype(jnp.float32),
        lax.psum_scatter(
            value_part.astype(jnp.bfloat16), "seq", scatter_dimension=1, tiled=True
        ).astype(jnp.float32),
    )
    grad_projected = jnp.concatenate(
        [
            rotate(grad_query, cosine, -sine_table).reshape(rows_here, frames_here, D),
            rotate(grad_key, cosine, -sine_table).reshape(rows_here, frames_here, D),
            grad_value.reshape(rows_here, frames_here, D),
        ],
        axis=-1,
    ).astype(jnp.bfloat16)
    grad_qkv = outer_sum(attn_in, grad_projected)
    grad_attn_in = matmul_t(grad_projected, qkv_w)
    dshift_attn = jnp.sum(grad_attn_in, axis=1)
    dscale_attn = jnp.sum(grad_attn_in * normed_a, axis=1)
    grad_frames = grad_attn + norm_back(grad_attn_in * (1.0 + scale_attn), normed_a, inv_a)
    grad_rows = jnp.concatenate(
        [dshift_attn, dscale_attn, dgate_attn, dshift_ffn, dscale_ffn, dgate_ffn], axis=-1
    )
    grad_modul = jnp.dot(token_act.astype(jnp.float32).T, grad_rows, precision=highest)
    grad_token = jnp.dot(grad_rows, modul.astype(jnp.float32).T, precision=highest) * silu_slope(
        time_token
    )
    grad_timeout = jnp.dot(time_hidden.astype(jnp.float32).T, grad_token, precision=highest)
    grad_pre = jnp.dot(grad_token, time_out.astype(jnp.float32).T, precision=highest) * silu_slope(
        pre_hidden
    )
    grad_timein = jnp.dot(features.astype(jnp.float32).T, grad_pre, precision=highest)
    rest_grads = (
        lax.psum_scatter(grad_timein, ("row", "seq"), scatter_dimension=0, tiled=True),
        lax.psum_scatter(grad_timeout, ("row", "seq"), scatter_dimension=0, tiled=True),
        lax.psum_scatter(grad_modul, ("row", "seq"), scatter_dimension=0, tiled=True),
        lax.psum_scatter(grad_qkv, ("row", "seq"), scatter_dimension=0, tiled=True),
        lax.psum_scatter(grad_attnout, ("row", "seq"), scatter_dimension=0, tiled=True),
        lax.psum_scatter(grad_gain, ("row", "seq"), scatter_dimension=0, tiled=True),
        lax.psum_scatter(grad_crossq, ("row", "seq"), scatter_dimension=0, tiled=True),
        lax.psum_scatter(grad_crosskv, ("row", "seq"), scatter_dimension=0, tiled=True),
        lax.psum_scatter(grad_crossout, ("row", "seq"), scatter_dimension=0, tiled=True),
    )
    shard_timein, shard_timeout, shard_modul = (rest_grads[0], rest_grads[1], rest_grads[2])
    block_grads = rest_grads[3:]
    return (
        result,
        grad_frames,
        shard_timein,
        shard_timeout,
        shard_modul,
        block_grads[0],
        block_grads[1],
        block_grads[2],
        block_grads[3],
        block_grads[4],
        block_grads[5],
        ffn_grads[0],
        ffn_grads[1],
    )


def solution(mesh):
    placed = (
        P("row", "seq", None),
        P("row", None, None),
        P("row", None),
        P(),
        P(),
        P(),
        P(("row", "seq"), None),
        P(("row", "seq"), None),
        P(("row", "seq"), None),
        P(("row", "seq"), None),
        P(("row", "seq"), None),
        P(("row", "seq")),
        P(("row", "seq"), None),
        P(("row", "seq"), None),
        P(("row", "seq"), None),
        P(("row", "seq"), None),
        P(("row", "seq"), None),
        P("row", "seq", None),
    )
    return jax.shard_map(
        on_device,
        mesh=mesh,
        in_specs=placed,
        out_specs=(
            P("row", "seq", None),
            P("row", "seq", None),
            P(("row", "seq"), None),
            P(("row", "seq"), None),
            P(("row", "seq"), None),
            P(("row", "seq"), None),
            P(("row", "seq"), None),
            P(("row", "seq")),
            P(("row", "seq"), None),
            P(("row", "seq"), None),
            P(("row", "seq"), None),
            P(("row", "seq"), None),
            P(("row", "seq"), None),
        ),
        check_vma=False,
    )
```

profile of v0, /device:TPU:0, one launch (start us, length us, event | category | flops | bytes accessed | tf_op | source)
XLA Modules:
  0.0 4122.9 jit_solution(8242844012341209597)
XLA Ops:
  14.5 77.1 %all_gather.47 = bf16[256,1536]{1,0:T(8,128)(2,1)S(1)} all-gather(bf16[8,1536]{1,0:T(8,128)(2,1)} %param.24), channel_id=1, replica_groups=mesh['row'=8,'seq'=4] {'row','seq'}, dimensions={0}, use_global_device_ids=true | all-gather | bytes 811008 | tf_op jit(solution)/shard_map/all_gather | solution.py:151
  98.7 154.2 %all-gather.14.cloned.1.call-done = bf16[1536,9216]{1,0:T(8,128)(2,1)} async-done(((bf16[48,9216]{1,0:T(8,128)(2,1)}), bf16[1536,9216]{1,0:T(8,128)(2,1)}) %all-gather.14.cloned.1.call-update) | async-done | bytes 28311568 | tf_op jit(solution)/shard_map/all_gather | solution.py:153
  252.8 11.1 fusion.131
  264.6 92.6 %all-gather.16.cloned.1.call-done = bf16[1536,4608]{1,0:T(8,128)(2,1)} async-done(((bf16[48,4608]{1,0:T(8,128)(2,1)}), bf16[1536,4608]{1,0:T(8,128)(2,1)}) %all-gather.16.cloned.1.call-update) | async-done | bytes 14155792 | tf_op jit(solution)/shard_map/all_gather | solution.py:154
  357.1 10.4 convolution_bitcast_fusion.1
  367.5 3.4 fusion.125
  375.4 3.6 copy.79
  378.9 4.0 fusion.82
  391.9 39.5 all-reduce
  434.2 3.7 fusion.36
  441.6 51.5 %all-gather.20.cloned.1.call-done = bf16[1,2048,24,64]{1,3,2,0:T(8,128)(2,1)} async-done(((bf16[1,512,24,64]{1,3,2,0:T(8,128)(2,1)}), bf16[1,2048,24,64]{1,3,2,0:T(8,128)(2,1)}) %all-gather.20.cloned.1.call-update) | async-done | bytes 6291472 | tf_op jit(solution)/shard_map/all_gather | solution.py:215
  493.1 39.6 fusion.7
  532.7 31.6 fusion.1
  565.4 39.6 fusion.62
  605.0 27.0 all-gather.22.cloned.1.call-done
  632.0 7.8 fusion.124
  640.2 57.0 %all-gather.26.cloned.1.call-done = bf16[1536,1536]{1,0:T(8,128)(2,1)} async-done(((bf16[48,1536]{1,0:T(8,128)(2,1)}), bf16[1536,1536]{1,0:T(8,128)(2,1)}) %all-gather.26.cloned.1.call-update) | async-done | bytes 4718608 | tf_op jit(solution)/shard_map/all_gather | solution.py:157
  697.2 6.2 convolution_convert_fusion.3
  706.0 6.4 fusion.127
  712.5 4.6 convolution_convert_fusion.4
  717.0 45.5 %all-gather.28.cloned.1.call-done = bf16[1536,1536]{1,0:T(8,128)(2,1)} async-done(((bf16[48,1536]{1,0:T(8,128)(2,1)}), bf16[1536,1536]{1,0:T(8,128)(2,1)}) %all-gather.28.cloned.1.call-update) | async-done | bytes 4718608 | tf_op jit(solution)/shard_map/all_gather | solution.py:159
  762.5 6.5 fusion.128
  770.2 208.9 %all-gather.30.cloned.1.call-done = bf16[1536,12288]{1,0:T(8,128)(2,1)} async-done(((bf16[48,12288]{1,0:T(8,128)(2,1)}), bf16[1536,12288]{1,0:T(8,128)(2,1)}) %all-gather.30.cloned.1.call-update) | async-done | bytes 37748752 | tf_op jit(solution)/shard_map/all_gather | solution.py:160
  979.1 29.5 convolution_bitcast_fusion
  1008.6 96.2 %all-gather.32.cloned.1.call-done = bf16[6144,1536]{1,0:T(8,128)(2,1)} async-done(((bf16[192,1536]{1,0:T(8,128)(2,1)}), bf16[6144,1536]{1,0:T(8,128)(2,1)}) %all-gather.32.cloned.1.call-update) | async-done | bytes 18874384 | tf_op jit(solution)/shard_map/all_gather | solution.py:161
  1104.8 29.3 fusion.24
  1134.1 28.3 fusion.48
  1165.4 19.3 fusion.47
  1186.4 3.8 convolution_convert_fusion.2
  1192.3 4.6 multiply_reduce_fusion.1
  1203.1 6.1 fusion.46
  1215.0 3.8 convolution_convert_fusion.1
  1220.7 75.0 %multiply_reduce_fusion = (f32[24,512]{1,0:T(8,128)S(1)}, f32[24,512,2048]{2,1,0:T(8,128)}) fusion(f32[24,512]{1,0:T(8,128)S(1)} %copy-done.39, f32[24,512,2048]{2,1,0:T(8,128)} %get-tuple-element.174, pred[512,2048]{1,0:T(8,128)(4,1)S(1)} %copy-done.2, bf16[512,24,64]{0,2,1:T(8,128)(2,1)S(1)} %bitcast.246, ...), kind=kOutput, calls=%fused_computation.2 | convolution fusion | flops 3347042304 | bytes 210337792 | tf_op jit(solution)/shard_map/while/body/eval_jaxpr/qhd,khd->hqk/dot_general | solution.py:110
  1295.7 78.3 %multiply_convert_fusion = bf16[24,512,2048]{2,1,0:T(8,128)(2,1)} fusion(f32[24,512,2048]{2,1,0:T(8,128)} %get-tuple-element.185, f32[24,512]{1,0:T(8,128)S(1)} %get-tuple-element.184, f32[24,512]{1,0:T(8,128)S(1)} %copy-done.39, f32[24,512,2048]{2,1,0:T(8,128)} %get-tuple-element.174, pred[512,2048]{1,0:T(8,128)(4,1)S(1)} %copy-done.2), kind=kLoop, calls=%fused_computation.1 | loop fusion | flops 150994944 | bytes 252805120 | tf_op jit(solution)/shard_map/while/body/eval_jaxpr/convert_element_type | solution.py:113
  1374.0 21.5 fusion.15
  1397.0 41.2 convert_bitcast_fusion
  1440.0 7.0 fusion.113
  1448.4 6.9 fusion.72
  1457.3 6.4 fusion.86
  1468.3 4.0 fusion.75
  1472.3 6.6 convolution_bitcast_fusion.2
  1478.9 10.0 copy.98
  1488.9 24.2 multiply_bitcast_fusion
  1517.5 19.8 reduce-scatter.17.cloned.1.call-done
  1537.3 15.8 fusion.44
  1553.1 3.1 fusion.119
  1556.3 25.8 convolution_reduce_fusion.3
  1582.2 6.3 convolution_reduce_fusion
  1590.0 4.2 broadcast_multiply_fusion.1
  1595.0 21.6 fusion.78
  1617.2 15.5 fusion.58
  1633.4 18.3 broadcast_multiply_fusion
  1653.8 34.8 fusion.12
  1689.2 40.3 all-reduce.1
  1730.2 5.1 fusion.43
  1735.2 86.0 %reduce-scatter.31.cloned.1.call-done = f32[48,1536]{1,0:T(8,128)} async-done(((f32[1536,1536]{1,0:T(8,128)}), f32[48,1536]{1,0:T(8,128)}) %reduce-scatter.31.cloned.1.call-update) | async-done | bytes 294928 | tf_op jit(solution)/shard_map/reduce_scatter | solution.py:395
  1821.2 140.8 %reduce-scatter.27.cloned.1.call-done = f32[48,1536]{1,0:T(8,128)} async-done(((f32[1536,1536]{1,0:T(8,128)}), f32[48,1536]{1,0:T(8,128)}) %reduce-scatter.27.cloned.1.call-update) | async-done | bytes 294928 | tf_op jit(solution)/shard_map/reduce_scatter | solution.py:391
  1962.0 141.9 %reduce-scatter.37.cloned.1.call-done = f32[24,3072]{1,0:T(8,128)} async-done(((f32[768,3072]{1,0:T(8,128)}), f32[24,3072]{1,0:T(8,128)}) %reduce-scatter.37.cloned.1.call-update) | async-done | bytes 294928
  2103.9 101.8 %reduce-scatter.19.cloned.1.call-done = f32[8,1536]{1,0:T(8,128)} async-done(((f32[256,1536]{1,0:T(8,128)}), f32[8,1536]{1,0:T(8,128)}) %reduce-scatter.19.cloned.1.call-update) | async-done | bytes 49168 | tf_op jit(solution)/shard_map/reduce_scatter | solution.py:387
  2205.8 141.1 %reduce-scatter.21.cloned.1.call-done = f32[48,1536]{1,0:T(8,128)} async-done(((f32[1536,1536]{1,0:T(8,128)}), f32[48,1536]{1,0:T(8,128)}) %reduce-scatter.21.cloned.1.call-update) | async-done | bytes 294928 | tf_op jit(solution)/shard_map/reduce_scatter | solution.py:388
  2346.9 355.4 %reduce-scatter.35.cloned.1.call-done = f32[192,1536]{1,0:T(8,128)} async-done(((f32[6144,1536]{1,0:T(8,128)}), f32[192,1536]{1,0:T(8,128)}) %reduce-scatter.35.cloned.1.call-update) | async-done | bytes 1179664 | tf_op jit(solution)/shard_map/reduce_scatter | solution.py:301
  2702.2 269.9 %reduce-scatter.25.cloned.1.call-done = f32[48,4608]{1,0:T(8,128)} async-done(((f32[1536,4608]{1,0:T(8,128)}), f32[48,4608]{1,0:T(8,128)}) %reduce-scatter.25.cloned.1.call-update) | async-done | bytes 884752 | tf_op jit(solution)/shard_map/reduce_scatter | solution.py:390
  2972.1 480.2 %reduce-scatter.23.cloned.1.call-done = f32[48,9216]{1,0:T(8,128)} async-done(((f32[1536,9216]{1,0:T(8,128)}), f32[48,9216]{1,0:T(8,128)}) %reduce-scatter.23.cloned.1.call-update) | async-done | bytes 1769488 | tf_op jit(solution)/shard_map/reduce_scatter | solution.py:389
  3452.3 663.8 %reduce-scatter.33.cloned.1.call-done = f32[48,12288]{1,0:T(8,128)} async-done(((f32[1536,12288]{1,0:T(8,128)}), f32[48,12288]{1,0:T(8,128)}) %reduce-scatter.33.cloned.1.call-update) | async-done | bytes 2359312 | tf_op jit(solution)/shard_map/reduce_scatter | solution.py:300
  (306 shorter events, 82.7 us)
Async XLA Ops:
  7.2 427.0 %copy-start = (bf16[1,128,768]{2,1,0:T(8,128)(2,1)S(1)}, bf16[1,128,768]{2,1,0:T(8,128)(2,1)}, u32[]{:S(2)}) copy-start(bf16[1,128,768]{2,1,0:T(8,128)(2,1)} %param.19) | copy-start | bytes 589828
  7.2 85.9 %copy-start.13 = (bf16[1,512,1536]{2,1,0:T(8,128)(2,1)S(1)}, bf16[1,512,1536]{2,1,0:T(8,128)(2,1)}, u32[]{:S(2)}) copy-start(bf16[1,512,1536]{2,1,0:T(8,128)(2,1)} %param.18) | copy-start | bytes 4718596
  7.2 87.7 %all-gather.12.cloned.1.call-start = ((), (), s32[]{:S(2)}) async-start(), calls=%async_computation.12 | async-start | bytes 4866048 | tf_op jit(solution)/shard_map/all_gather | solution.py:152
  7.9 244.9 %all-gather.14.cloned.1.call-start = ((), (), s32[]{:S(2)}) async-start(), calls=%async_computation.13 | async-start | bytes 29196288 | tf_op jit(solution)/shard_map/all_gather | solution.py:153
  8.7 348.4 %all-gather.16.cloned.1.call-start = ((), (), s32[]{:S(2)}) async-start(), calls=%async_computation.14 | async-start | bytes 14598144 | tf_op jit(solution)/shard_map/all_gather | solution.py:154
  9.4 424.8 %all-gather.24.cloned.1.call-start = ((), (), s32[]{:S(2)}) async-start(), calls=%async_computation.18 | async-start | bytes 4866048 | tf_op jit(solution)/shard_map/all_gather | solution.py:158
  10.0 483.1 %all-gather.20.cloned.1.call-start = ((), (), s32[]{:S(2)}) async-start(), calls=%async_computation.16 | async-start | bytes 7864320 | tf_op jit(solution)/shard_map/all_gather | solution.py:215
  93.4 263.7 %copy-start.66 = (f32[512]{0:T(512)}, f32[512]{0:T(512)S(1)}, u32[]{:S(2)}) copy-start(f32[512]{0:T(512)S(1)} %broadcast_multiply_fusion.11) | copy-start | bytes 6148
  94.0 263.2 %copy-start.79 = (f32[512]{0:T(512)}, f32[512]{0:T(512)S(1)}, u32[]{:S(2)}) copy-start(f32[512]{0:T(512)S(1)} %add_rsqrt_fusion.2) | copy-start | bytes 6148
  94.9 284.0 %copy-start.40 = (f32[512,32]{0,1:T(8,128)}, f32[512,32]{0,1:T(8,128)S(1)}, u32[]{:S(2)}) copy-start(f32[512,32]{0,1:T(8,128)S(1)} %get-tuple-element.172) | copy-start | bytes 196612
  264.6 102.9 %copy-start.54 = (f32[1536]{0:T(1024)}, f32[1536]{0:T(1024)S(1)}, u32[]{:S(2)}) copy-start(f32[1536]{0:T(1024)S(1)} %get-tuple-element.135) | copy-start | bytes 18436
  264.6 102.9 %copy-start.74 = (f32[1536]{0:T(1024)}, f32[1536]{0:T(1024)S(1)}, u32[]{:S(2)}) copy-start(f32[1536]{0:T(1024)S(1)} %get-tuple-element.134) | copy-start | bytes 18436
  384.2 181.2 %all-gather.18.cloned.1.call-start = ((), (), s32[]{:S(2)}) async-start(), calls=%async_computation.15 | async-start | bytes 7864320 | tf_op jit(solution)/shard_map/all_gather | solution.py:216
  386.3 45.9 %copy-start.86 = (f32[5]{0:T(128)S(1)}, f32[5]{0:T(128)}, u32[]{:S(2)}) copy-start(f32[5]{0:T(128)} %param.23) | copy-start | bytes 64
  387.9 244.0 %all-gather.22.cloned.1.call-start = ((), (), s32[]{:S(2)}) async-start(), calls=%async_computation.17 | async-start | bytes 4866048 | tf_op jit(solution)/shard_map/all_gather | solution.py:155
  388.7 308.6 %all-gather.26.cloned.1.call-start = ((), (), s32[]{:S(2)}) async-start(), calls=%async_computation.19 | async-start | bytes 4866048 | tf_op jit(solution)/shard_map/all_gather | solution.py:157
  389.4 373.1 %all-gather.28.cloned.1.call-start = ((), (), s32[]{:S(2)}) async-start(), calls=%async_computation.20 | async-start | bytes 4866048 | tf_op jit(solution)/shard_map/all_gather | solution.py:159
  390.2 588.9 %all-gather.30.cloned.1.call-start = ((), (), s32[]{:S(2)}) async-start(), calls=%async_computation.21 | async-start | bytes 38928384 | tf_op jit(solution)/shard_map/all_gather | solution.py:160
  390.7 714.1 %all-gather.32.cloned.1.call-start = ((), (), s32[]{:S(2)}) async-start(), calls=%async_computation.22 | async-start | bytes 19464192 | tf_op jit(solution)/shard_map/all_gather | solution.py:161
  391.5 1121.8 %reduce-scatter.15.cloned.1.call-start = ((), (), s32[]{:S(2)}) async-start(), calls=%async_computation.23 | async-start | bytes 7864320 | tf_op jit(solution)/shard_map/reduce_scatter | solution.py:354
  434.2 131.3 %copy-start.1 = (pred[512,2048]{1,0:T(8,128)(4,1)}, pred[512,2048]{1,0:T(8,128)(4,1)S(1)}, u32[]{:S(2)}) copy-start(pred[512,2048]{1,0:T(8,128)(4,1)S(1)} %broadcast_compare_fusion) | copy-start | bytes 3145732
  434.2 58.9 %copy-start.20 = (bf16[512,24,32]{0,2,1:T(8,128)(2,1)S(1)}, bf16[512,24,32]{0,2,1:T(8,128)(2,1)}, u32[]{:S(2)}) copy-start(bf16[512,24,32]{0,2,1:T(8,128)(2,1)} %get-tuple-element.157) | copy-start | bytes 2359300
  434.2 58.9 %copy-start.22 = (bf16[512,24,32]{0,2,1:T(8,128)(2,1)S(1)}, bf16[512,24,32]{0,2,1:T(8,128)(2,1)}, u32[]{:S(2)}) copy-start(bf16[512,24,32]{0,2,1:T(8,128)(2,1)} %get-tuple-element.158) | copy-start | bytes 2359300
  565.4 66.5 %copy-start.44 = (f32[1536]{0:T(1024)S(1)}, f32[1536]{0:T(1024)}, u32[]{:S(2)}) copy-start(f32[1536]{0:T(1024)} %get-tuple-element.136) | copy-start | bytes 18436
  639.7 63.7 %copy-start.5 = (f32[1,512,1536]{2,1,0:T(8,128)}, f32[1,512,1536]{2,1,0:T(8,128)S(1)}, u32[]{:S(2)}) copy-start(f32[1,512,1536]{2,1,0:T(8,128)S(1)} %get-tuple-element.147) | copy-start | bytes 9437188
  639.7 57.5 %copy-start.47 = (f32[1536]{0:T(1024)S(1)}, f32[1536]{0:T(1024)}, u32[]{:S(2)}) copy-start(f32[1536]{0:T(1024)} %convert_element_type.228) | copy-start | bytes 18436
  639.7 63.7 %copy-start.63 = (f32[512]{0:T(512)}, f32[512]{0:T(512)S(1)}, u32[]{:S(2)}) copy-start(f32[512]{0:T(512)S(1)} %broadcast_multiply_fusion.10) | copy-start | bytes 6148
  640.2 63.2 %copy-start.68 = (f32[512]{0:T(512)}, f32[512]{0:T(512)S(1)}, u32[]{:S(2)}) copy-start(f32[512]{0:T(512)S(1)} %add_rsqrt_fusion.1) | copy-start | bytes 6148
  706.0 6.4 copy-start.42
  769.0 396.4 %copy-start.3 = (f32[1,512,1536]{2,1,0:T(8,128)}, f32[1,512,1536]{2,1,0:T(8,128)S(1)}, u32[]{:S(2)}) copy-start(f32[1,512,1536]{2,1,0:T(8,128)S(1)} %get-tuple-element.179) | copy-start | bytes 9437188
  769.0 210.0 %copy-start.27 = (f32[1536]{0:T(1024)S(1)}, f32[1536]{0:T(1024)}, u32[]{:S(2)}) copy-start(f32[1536]{0:T(1024)} %get-tuple-element.133) | copy-start | bytes 18436
  769.1 210.0 %copy-start.35 = (f32[1536]{0:T(1024)S(1)}, f32[1536]{0:T(1024)}, u32[]{:S(2)}) copy-start(f32[1536]{0:T(1024)} %get-tuple-element.137) | copy-start | bytes 18436
  769.1 396.3 %copy-start.33 = (f32[512]{0:T(512)}, f32[512]{0:T(512)S(1)}, u32[]{:S(2)}) copy-start(f32[512]{0:T(512)S(1)} %broadcast_multiply_fusion.9) | copy-start | bytes 6148
  769.6 395.9 %copy-start.37 = (f32[512]{0:T(512)}, f32[512]{0:T(512)S(1)}, u32[]{:S(2)}) copy-start(f32[512]{0:T(512)S(1)} %add_rsqrt_fusion) | copy-start | bytes 6148
  979.1 125.8 %copy-start.76 = (f32[1536]{0:T(1024)S(1)}, f32[1536]{0:T(1024)}, u32[]{:S(2)}) copy-start(f32[1536]{0:T(1024)} %get-tuple-element.132) | copy-start | bytes 18436
  1165.4 20.9 copy-start.15
  1199.5 9.8 copy-start.11
  1200.2 9.1 copy-start.32
  1203.1 6.5 copy-start.19
  1203.1 11.9 slice-start
  1220.6 75.1 %copy-start.25 = (bf16[512,1536]{0,1:T(8,128)(2,1)}, bf16[512,1536]{0,1:T(8,128)(2,1)S(1)}, u32[]{:S(2)}) copy-start(bf16[512,1536]{0,1:T(8,128)(2,1)S(1)} %copy.86) | copy-start | bytes 4718596
  1295.7 78.3 %copy-start.21 = (bf16[512,24,32]{0,2,1:T(8,128)(2,1)S(1)}, bf16[512,24,32]{0,2,1:T(8,128)(2,1)}, u32[]{:S(2)}) copy-start(bf16[512,24,32]{0,2,1:T(8,128)(2,1)} %get-tuple-element.157) | copy-start | bytes 2359300
  1295.7 78.3 %copy-start.23 = (bf16[512,24,32]{0,2,1:T(8,128)(2,1)S(1)}, bf16[512,24,32]{0,2,1:T(8,128)(2,1)}, u32[]{:S(2)}) copy-start(bf16[512,24,32]{0,2,1:T(8,128)(2,1)} %get-tuple-element.158) | copy-start | bytes 2359300
  1395.6 141.8 %reduce-scatter.17.cloned.1.call-start = ((), (), s32[]{:S(2)}) async-start(), calls=%async_computation.24 | async-start | bytes 7864320 | tf_op jit(solution)/shard_map/reduce_scatter | solution.py:357
  1438.1 297.1 %reduce-scatter.29.cloned.1.call-start = ((), (), s32[]{:S(2)}) async-start(), calls=%async_computation.30 | async-start | bytes 9732096 | tf_op jit(solution)/shard_map/reduce_scatter | solution.py:393
  1447.0 374.2 %reduce-scatter.31.cloned.1.call-start = ((), (), s32[]{:S(2)}) async-start(), calls=%async_computation.31 | async-start | bytes 9732096 | tf_op jit(solution)/shard_map/reduce_scatter | solution.py:395
  1455.4 506.7 %reduce-scatter.27.cloned.1.call-start = ((), (), s32[]{:S(2)}) async-start(), calls=%async_computation.29 | async-start | bytes 9732096 | tf_op jit(solution)/shard_map/reduce_scatter | solution.py:391
  1463.7 640.2 %reduce-scatter.37.cloned.1.call-start = ((), (), s32[]{:S(2)}) async-start(), calls=%async_computation.34 | async-start | bytes 9732096
  1488.9 716.9 %reduce-scatter.19.cloned.1.call-start = ((), (), s32[]{:S(2)}) async-start(), calls=%async_computation.25 | async-start | bytes 1622016 | tf_op jit(solution)/shard_map/reduce_scatter | solution.py:387
  1516.1 21.2 copy-start.14
  1516.2 21.2 copy-start.55
  1516.2 21.2 copy-start.67
  1516.2 21.2 copy-start.80
  1556.3 25.8 copy-start.53
  1582.2 6.4 copy-start.81
  1582.2 7.8 copy-start.62
  1590.0 756.9 %reduce-scatter.21.cloned.1.call-start = ((), (), s32[]{:S(2)}) async-start(), calls=%async_computation.26 | async-start | bytes 9732096 | tf_op jit(solution)/shard_map/reduce_scatter | solution.py:388
  1594.3 1108.0 %reduce-scatter.35.cloned.1.call-start = ((), (), s32[]{:S(2)}) async-start(), calls=%async_computation.33 | async-start | bytes 38928384 | tf_op jit(solution)/shard_map/reduce_scatter | solution.py:301
  1616.5 1355.6 %reduce-scatter.25.cloned.1.call-start = ((), (), s32[]{:S(2)}) async-start(), calls=%async_computation.28 | async-start | bytes 29196288 | tf_op jit(solution)/shard_map/reduce_scatter | solution.py:390
  1632.8 1819.5 %reduce-scatter.23.cloned.1.call-start = ((), (), s32[]{:S(2)}) async-start(), calls=%async_computation.27 | async-start | bytes 58392576 | tf_op jit(solution)/shard_map/reduce_scatter | solution.py:389
  1651.8 2464.3 %reduce-scatter.33.cloned.1.call-start = ((), (), s32[]{:S(2)}) async-start(), calls=%async_computation.32 | async-start | bytes 77856768 | tf_op jit(solution)/shard_map/reduce_scatter | solution.py:300
  1688.5 41.6 %copy-start.82 = (f32[512]{0:T(512)S(1)}, f32[512]{0:T(512)}, u32[]{:S(2)}) copy-start(f32[512]{0:T(512)} %get-tuple-element.127) | copy-start | bytes 6148
  1688.5 41.6 %copy-start.78 = (f32[512]{0:T(512)S(1)}, f32[512]{0:T(512)}, u32[]{:S(2)}) copy-start(f32[512]{0:T(512)} %get-tuple-element.131) | copy-start | bytes 6148
  1688.5 41.6 %copy-start.10 = (f32[1,512,1536]{2,1,0:T(8,128)S(1)}, f32[1,512,1536]{2,1,0:T(8,128)}, u32[]{:S(2)}) copy-start(f32[1,512,1536]{2,1,0:T(8,128)} %copy-done.8) | copy-start | bytes 9437188
  (50 other events, 135.4 us)
Sparse Core Ops, SparseCore 0:
  10.9 70.9 all-gather.11
  84.9 167.9 all-gather.13
  255.7 101.3 all-gather.15
  359.9 62.0 all-gather.23
  424.2 68.8 all-gather.19
  495.3 70.0 all-gather.17
  568.3 63.6 all-gather.21
  634.8 62.3 all-gather.25
  700.1 62.3 all-gather.27
  765.3 213.7 all-gather.29
  982.0 122.8 all-gather.31
  1395.7 68.3 reduce-scatter.14
  1467.1 70.2 reduce-scatter.16
  1543.6 135.6 reduce-scatter.28
  1686.7 134.4 reduce-scatter.30
  1827.6 134.4 reduce-scatter.26
  1969.4 134.5 reduce-scatter.36
  2109.6 96.1 reduce-scatter.18
  2212.2 134.5 reduce-scatter.20
  2354.8 347.3 reduce-scatter.34
  2709.3 262.8 reduce-scatter.24
  2979.1 473.1 reduce-scatter.22
  3460.4 655.6 reduce-scatter.32
where the time goes:
time: 4130 us; the launch traced here: 4120 us
  waiting for transfers between devices  3140 us (76%)
  matrix products  580 us (14%)
  other arithmetic  170 us (4%)
  blocking collectives  157 us (4%)
  local copies, waits for them, and re-layouts  59.1 us (1%)
    reduce_scatter x1, waiting for transfers between devices, on_device(): lax.psum_scatter(grad_glu, ('row', 'seq'), scatter_dimension=0, tiled=True)  664 us
    reduce_scatter x1, waiting for transfers between devices, on_device(): lax.psum_scatter(grad_modul, ('row', 'seq'), scatter_dimension=0, tiled=T...  480 us
    reduce_scatter x1, waiting for transfers between devices, on_device(): lax.psum_scatter(grad_down, ('row', 'seq'), scatter_dimension=0, tiled=True)  355 us
    reduce_scatter x1, waiting for transfers between devices, on_device(): lax.psum_scatter(grad_qkv, ('row', 'seq'), scatter_dimension=0, tiled=True)  270 us
    all_gather x1, waiting for transfers between devices, on_device(): lax.all_gather(w_glu, ('row', 'seq'), axis=0, tiled=True)  209 us
    all_gather x1, waiting for transfers between devices, on_device(): lax.all_gather(w_mod, ('row', 'seq'), axis=0, tiled=True)  154 us
    unnamed x24, waiting for transfers between devices  148 us
    reduce_scatter x1, waiting for transfers between devices, on_device(): lax.psum_scatter(grad_timeout, ('row', 'seq'), scatter_dimension=0, tiled...  141 us
  transfers between devices with their start and end apart: 23, of which 19 were waited for; matrix products, arithmetic and copies ran while one was open for 12% of the time, Pallas kernels for 0%

commit v1 on v0

--- a/solution.py
+++ b/solution.py
@@ -1,8 +1,11 @@
+import functools
 import math
 
 import jax
 import jax.numpy as jnp
 from jax import lax
+from jax.experimental import pallas as pl
+from jax.experimental.pallas import tpu as pltpu
 from jax.sharding import PartitionSpec as P
 
 D = 1536
@@ -12,6 +15,236 @@
 TFREQ = 256
 LENGTH = 2048
 BUCKETS = 5
+PAIR = 2 * HEAD_DIM
+VMEM = 50 * 1024 * 1024
+f32 = jnp.float32
+bf16 = jnp.bfloat16
+
+
+def dot_nt(left, right):
+    return lax.dot_general(left, right, (((1,), (1,)), ((), ())), preferred_element_type=f32)
+
+
+def dot_nn(left, right):
+    return lax.dot_general(left, right, (((1,), (0,)), ((), ())), preferred_element_type=f32)
+
+
+def swap_halves(values):
+    lane = lax.broadcasted_iota(jnp.int32, values.shape, 1)
+    ahead = pltpu.roll(values, PAIR - HEAD_DIM // 2, 1)
+    behind = pltpu.roll(values, HEAD_DIM // 2, 1)
+    return jnp.where((lane & (HEAD_DIM // 2)) == 0, ahead, behind)
+
+
+def head_lanes(values, head):
+    lane = lax.broadcasted_iota(jnp.int32, values.shape, 1)
+    return jnp.where((lane // HEAD_DIM) == head, values, 0.0)
+
+
+def project_kernel(x_ref, scale_ref, shift_ref, w_ref, cos_ref, sin_ref, in_ref, out_ref):
+    values = x_ref[...].astype(f32)
+    center = values - jnp.mean(values, axis=-1, keepdims=True)
+    inv_std = lax.rsqrt(jnp.mean(center * center, axis=-1, keepdims=True) + 1e-05)
+    modulated = (center * inv_std * scale_ref[...] + shift_ref[...]).astype(bf16)
+    in_ref[...] = modulated
+    projected = dot_nn(modulated, w_ref[...])
+    cosine = cos_ref[...]
+    sine = sin_ref[...]
+    width = out_ref.shape[1]
+    for start in range(0, width, PAIR):
+        part = projected[:, start : start + PAIR]
+        if start < 2 * width // 3:
+            part = part * cosine + swap_halves(part) * sine
+        out_ref[:, start : start + PAIR] = part.astype(bf16)
+
+
+def project(x, scale, shift, w, cosine, sine, block=256):
+    count, depth = x.shape
+    width = w.shape[1]
+    row_spec = lambda cols: pl.BlockSpec((block, cols), lambda i: (i, 0))
+    whole = lambda a: pl.BlockSpec(a.shape, lambda i: (0, 0))
+    return pl.pallas_call(
+        project_kernel,
+        grid=(count // block,),
+        in_specs=[row_spec(depth), whole(scale), whole(shift), whole(w), row_spec(PAIR), row_spec(PAIR)],
+        out_specs=[row_spec(depth), row_spec(width)],
+        out_shape=[
+            jax.ShapeDtypeStruct((count, depth), bf16),
+            jax.ShapeDtypeStruct((count, width), bf16),
+        ],
+        compiler_params=pltpu.CompilerParams(vmem_limit_bytes=VMEM),
+        cost_estimate=pl.CostEstimate(
+            flops=2 * count * depth * width,
+            bytes_accessed=2 * (2 * count * depth + depth * width + count * width),
+            transcendentals=count,
+        ),
+        name="project",
+    )(x, scale, shift, w, cosine, sine)
+
+
+def attend_kernel(masked, *refs):
+    if masked:
+        q_ref, k_ref, v_ref, qmask_ref, kmask_ref, o_ref, lse_ref, keys, values_t = refs
+    else:
+        q_ref, k_ref, v_ref, o_ref, lse_ref, keys, values_t = refs
+
+    @pl.when(pl.program_id(1) == 0)
+    def _():
+        keys[:, :PAIR] = k_ref[...]
+        if masked:
+            keys[:, PAIR:] = kmask_ref[...]
+        values_t[...] = v_ref[...].astype(f32).T.astype(bf16)
+
+    queries = q_ref[...].astype(f32) * 0.125
+    mixed = []
+    for head in range(2):
+        query = head_lanes(queries, head).astype(bf16)
+        if masked:
+            query = jnp.concatenate([query, qmask_ref[...]], axis=1)
+        scores = dot_nt(keys[...], query)
+        top = jnp.max(scores, axis=0, keepdims=True)
+        shifted = jnp.exp(scores - top)
+        total = jnp.sum(shifted, axis=0, keepdims=True)
+        own = values_t[head * HEAD_DIM : (head + 1) * HEAD_DIM, :]
+        mixed.append(dot_nn(own, shifted.astype(bf16)) / total)
+        lse_ref[0, head : head + 1, :] = top + jnp.log(total)
+    o_ref[...] = jnp.concatenate(mixed, axis=0).T.astype(bf16)
+
+
+def attend(q, k, v, q_col, k_col, v_col, pairs, block, masks=None):
+    count, keys = q.shape[0], k.shape[0]
+    masked = masks is not None
+    in_specs = [
+        pl.BlockSpec((block, PAIR), lambda p, i: (i, q_col + p)),
+        pl.BlockSpec((keys, PAIR), lambda p, i: (0, k_col + p)),
+        pl.BlockSpec((keys, PAIR), lambda p, i: (0, v_col + p)),
+    ]
+    if masked:
+        in_specs += [
+            pl.BlockSpec((block, PAIR), lambda p, i: (i, 0)),
+            pl.BlockSpec((keys, PAIR), lambda p, i: (0, 0)),
+        ]
+    return pl.pallas_call(
+        functools.partial(attend_kernel, masked),
+        grid=(pairs, count // block),
+        in_specs=in_specs,
+        out_specs=[
+            pl.BlockSpec((block, PAIR), lambda p, i: (i, p)),
+            pl.BlockSpec((1, 2, block), lambda p, i: (p, 0, i)),
+        ],
+        out_shape=[
+            jax.ShapeDtypeStruct((count, pairs * PAIR), bf16),
+            jax.ShapeDtypeStruct((pairs, 2, count), f32),
+        ],
+        scratch_shapes=[
+            pltpu.VMEM((keys, (2 if masked else 1) * PAIR), bf16),
+            pltpu.VMEM((PAIR, keys), bf16),
+        ],
+        compiler_params=pltpu.CompilerParams(vmem_limit_bytes=VMEM),
+        cost_estimate=pl.CostEstimate(
+            flops=16 * pairs * PAIR * count * keys,
+            bytes_accessed=2 * pairs * PAIR * (2 * count + 2 * keys),
+            transcendentals=2 * pairs * count * keys,
+        ),
+        name="attend",
+    )(q, k, v, *(masks or ()))
+
+
+def attend_back_kernel(masked, chunk, *refs):
+    if masked:
+        (q_ref, k_ref, v_ref, do_ref, o_ref, lse_ref, qmask_ref, kmask_ref, qcos_ref, qsin_ref,
+         kcos_ref, ksin_ref, dq_ref, dk_ref, dv_ref, keys, keys_t, dk_sum, dv_sum) = refs
+    else:
+        (q_ref, k_ref, v_ref, do_ref, o_ref, lse_ref,
+         dq_ref, dk_ref, dv_ref, keys, keys_t, dk_sum, dv_sum) = refs
+    step = pl.program_id(1)
+    count = k_ref.shape[0]
+
+    @pl.when(step == 0)
+    def _():
+        keys[:, :PAIR] = k_ref[...]
+        if masked:
+            keys[:, PAIR:] = kmask_ref[...]
+        keys_t[...] = k_ref[...].astype(f32).T.astype(bf16)
+        dk_sum[...] = jnp.zeros_like(dk_sum)
+        dv_sum[...] = jnp.zeros_like(dv_sum)
+
+    queries = q_ref[...].astype(f32) * 0.125
+    grads = do_ref[...].astype(f32)
+    rows_t = (grads * o_ref[...].astype(f32)).T
+    parts = []
+    for head in range(2):
+        lanes = slice(head * HEAD_DIM, (head + 1) * HEAD_DIM)
+        delta = jnp.sum(rows_t[lanes, :], axis=0, keepdims=True)
+        log_row = lse_ref[0, head : head + 1, :]
+        query = head_lanes(queries, head).astype(bf16)
+        grad = head_lanes(grads, head).astype(bf16)
+        full = jnp.concatenate([query, qmask_ref[...]], axis=1) if masked else query
+        total = None
+        for start in range(0, count, chunk):
+            here = slice(start, start + chunk)
+            soft = jnp.exp(dot_nt(keys[here, :], full) - log_row)
+            grad_soft = dot_nt(v_ref[here, :], grad)
+            grad_scores = (soft * (grad_soft - delta)).astype(bf16)
+            dv_sum[here, :] += dot_nn(soft.astype(bf16), grad)
+            dk_sum[here, :] += dot_nn(grad_scores, query)
+            part = dot_nn(keys_t[lanes, here], grad_scores)
+            total = part if total is None else total + part
+        parts.append(total)
+    dq = jnp.concatenate(parts, axis=0).T * 0.125
+    if masked:
+        dq = dq * qcos_ref[...] - swap_halves(dq) * qsin_ref[...]
+    dq_ref[...] = dq.astype(dq_ref.dtype)
+
+    @pl.when(step == pl.num_programs(1) - 1)
+    def _():
+        dk = dk_sum[...]
+        if masked:
+            dk = dk * kcos_ref[...] - swap_halves(dk) * ksin_ref[...]
+        dk_ref[...] = dk.astype(dk_ref.dtype)
+        dv_ref[...] = dv_sum[...].astype(dv_ref.dtype)
+
+
+def attend_back(q, k, v, do, o, lse, q_col, k_col, v_col, pairs, block, chunk, masks=None, tables=None):
+    count, keys = q.shape[0], k.shape[0]
+    masked = masks is not None
+    out_type = bf16 if masked else f32
+    rows = lambda col: pl.BlockSpec((block, PAIR), lambda p, i: (i, col + p))
+    whole = lambda col: pl.BlockSpec((keys, PAIR), lambda p, i: (0, col + p))
+    in_specs = [
+        rows(q_col), whole(k_col), whole(v_col), rows(0), rows(0),
+        pl.BlockSpec((1, 2, block), lambda p, i: (p, 0, i)),
+    ]
+    operands = [q, k, v, do, o, lse]
+    if masked:
+        rows_fixed = pl.BlockSpec((block, PAIR), lambda p, i: (i, 0))
+        whole_fixed = pl.BlockSpec((keys, PAIR), lambda p, i: (0, 0))
+        in_specs += [rows_fixed, whole_fixed, rows_fixed, rows_fixed, whole_fixed, whole_fixed]
+        operands += [masks[0], masks[1], tables[0], tables[1], tables[0], tables[1]]
+    return pl.pallas_call(
+        functools.partial(attend_back_kernel, masked, chunk),
+        grid=(pairs, count // block),
+        in_specs=in_specs,
+        out_specs=[rows(0), whole(0), whole(0)],
+        out_shape=[
+            jax.ShapeDtypeStruct((count, pairs * PAIR), bf16),
+            jax.ShapeDtypeStruct((keys, pairs * PAIR), out_type),
+            jax.ShapeDtypeStruct((keys, pairs * PAIR), out_type),
+        ],
+        scratch_shapes=[
+            pltpu.VMEM((keys, (2 if masked else 1) * PAIR), bf16),
+            pltpu.VMEM((PAIR, keys), bf16),
+            pltpu.VMEM((keys, PAIR), f32),
+            pltpu.VMEM((keys, PAIR), f32),
+        ],
+        compiler_params=pltpu.CompilerParams(vmem_limit_bytes=VMEM),
+        cost_estimate=pl.CostEstimate(
+            flops=40 * pairs * PAIR * count * keys,
+            bytes_accessed=2 * pairs * PAIR * (4 * count + 4 * keys),
+            transcendentals=2 * pairs * count * keys,
+        ),
+        name="attend_back",
+    )(*operands)
 
 
 highest = lax.Precision.HIGHEST
@@ -413,6 +646,310 @@
     )
 
 
+def can_split(rows, seqs):
+    power = lambda n: n & (n - 1) == 0
+    return (
+        power(rows)
+        and power(seqs)
+        and HEADS % (2 * seqs) == 0
+        and D % (rows * seqs) == 0
+        and FF % (rows * seqs) == 0
+        and LENGTH % (seqs * 512) == 0
+    )
+
+
+def on_device_split(
+    rows,
+    seqs,
+    frames,
+    context,
+    seg_lengths,
+    bucket_ids,
+    timesteps,
+    bucket_weights,
+    w_time_in,
+    w_time_out,
+    w_mod,
+    w_qkv,
+    w_attn_out,
+    cross_gain,
+    w_cross_q,
+    w_cross_kv,
+    w_cross_out,
+    w_glu,
+    w_down,
+    cotangent,
+):
+    my_row = lax.axis_index("row")
+    my_seq = lax.axis_index("seq")
+    flat = my_row * seqs + my_seq
+    sizes = {"row": rows, "seq": seqs}
+
+    def swap(value, axis, j):
+        return lax.ppermute(value, axis, [(i, i ^ j) for i in range(sizes[axis])])
+
+    def sum_over(value, axis):
+        j = 1
+        while j < sizes[axis]:
+            value = value + swap(value, axis, j)
+            j *= 2
+        return value
+
+    def sum_all(value):
+        return sum_over(sum_over(value, "seq"), "row")
+
+    def pick(stack, axis_name, j, dim=0):
+        me = my_row if axis_name == "row" else my_seq
+        return lax.dynamic_index_in_dim(stack, me ^ j, dim, keepdims=False)
+
+    def natural(slots, axis_name="seq"):
+        stack = jnp.stack(slots)
+        return jnp.stack([pick(stack, axis_name, t) for t in range(len(slots))])
+
+    def exchange(stack, dim=0, axis_name="seq"):
+        pieces = [pick(stack, axis_name, j, dim) for j in range(sizes[axis_name])]
+        return [pieces[0]] + [swap(p, axis_name, j) for j, p in enumerate(pieces) if j]
+
+    def spread(value, axis_name="seq"):
+        return [value] + [swap(value, axis_name, j) for j in range(1, sizes[axis_name])]
+
+    def mine(values, width):
+        return lax.dynamic_slice_in_dim(values, flat * width, width, values.ndim - 1)
+
+    def dot(left, right):
+        return jnp.dot(left, right, preferred_element_type=jnp.float32)
+
+    def dot_right_t(left, right):
+        return jnp.einsum("fj,ij->fi", left, right, preferred_element_type=jnp.float32)
+
+    def dot_left_t(left, right):
+        return jnp.einsum("fi,fj->ij", left, right, preferred_element_type=jnp.float32)
+
+    low = jnp.bfloat16
+    frames_here = frames.shape[1]
+    text_len, ctx_dim = context.shape[1:]
+    local_heads = D // seqs
+    depth = w_qkv.shape[0]
+    part = FF // (rows * seqs)
+    x_own = frames[0]
+
+    x_all = jnp.concatenate(spread(x_own))
+    kv_split = w_cross_kv.reshape(w_cross_kv.shape[0], seqs, -1)
+    qkv_split = w_qkv.reshape(depth, 3, seqs, local_heads)
+    first_pieces = [
+        jnp.concatenate(
+            [
+                pick(qkv_split, "seq", j, 2).reshape(depth, 3 * local_heads),
+                pick(kv_split, "seq", j, 1).reshape(depth, -1),
+            ],
+            axis=1,
+        )
+        for j in range(seqs)
+    ]
+    first_slots = [first_pieces[0]] + [swap(p, "seq", j) for j, p in enumerate(first_pieces) if j]
+    first_w = natural(first_slots).reshape(seqs * depth, -1)
+    first_w = lax.all_gather(first_w, "row", axis=0, tiled=True)
+    qkv_w = first_w[:, : 3 * local_heads]
+    kv_w = first_w[:, 3 * local_heads :].reshape(ctx_dim, -1)
+    wide_w = lax.all_gather(
+        jnp.concatenate([w_attn_out, w_cross_q, w_cross_out], axis=1), ("row", "seq"), axis=0, tiled=True
+    )
+    attn_w, crossq_w, crossout_w = wide_w[:, :D], wide_w[:, D : 2 * D], wide_w[:, 2 * D :]
+    glu_slots = exchange(w_glu.reshape(depth, 2, rows, seqs, part), 3)
+    glu_w = natural([s.reshape(depth, -1) for s in glu_slots]).reshape(seqs * depth, -1)
+    glu_w = lax.all_gather(glu_w, "row", axis=0, tiled=True)
+    down_w = lax.all_gather(w_down, "row", axis=0, tiled=True)
+
+    features = time_features(timesteps.astype(jnp.float32)).astype(low)
+    pre_part = dot(mine(features, w_time_in.shape[0]), w_time_in)
+    gain_part = lax.dynamic_update_slice(
+        jnp.zeros((1, D), jnp.float32), cross_gain.astype(jnp.float32)[None], (0, flat * depth)
+    )
+    pre_hidden = sum_all(jnp.concatenate([pre_part, gain_part]))
+    gain_values = pre_hidden[BUCKETS:]
+    pre_hidden = pre_hidden[:BUCKETS]
+    time_hidden = jax.nn.silu(pre_hidden).astype(low)
+    time_token = sum_all(dot(mine(time_hidden, depth), w_time_out))
+    token_act = jax.nn.silu(time_token).astype(low)
+    mod_part = dot(mine(token_act, depth), w_mod)
+    row_part = lambda j: lax.dynamic_index_in_dim(mod_part, bucket_ids[my_row ^ j], 0)
+    modulation = row_part(0)
+    for j in range(1, rows):
+        modulation = modulation + swap(row_part(j), "row", j)
+    modulation = sum_over(modulation, "seq")
+    shift_attn, scale_attn, gate_attn, shift_ffn, scale_ffn, gate_ffn = jnp.split(modulation, 6, axis=1)
+
+    bounds = jnp.cumsum(seg_lengths[0])
+    slot_seq = my_seq ^ jnp.arange(seqs, dtype=jnp.int32)
+    positions = (slot_seq[:, None] * frames_here + jnp.arange(frames_here, dtype=jnp.int32)).reshape(-1)
+    ids = jnp.sum((positions[:, None] >= bounds[None, :]).astype(jnp.int32), axis=-1)
+    lane = jnp.arange(PAIR, dtype=jnp.int32)[None, :]
+    same = ids[:, None] == lane
+    key_mask = same.astype(low)
+    query_mask = jnp.where((lane < seg_lengths.shape[1]) & ~same, -1e30, 0.0).astype(low)
+    half_dim = HEAD_DIM // 2
+    inverse = jnp.exp(-math.log(10000.0) * jnp.arange(half_dim, dtype=jnp.float32) / half_dim)
+    angles = positions.astype(jnp.float32)[:, None] * inverse[None, :]
+    cosine = jnp.tile(jnp.cos(angles), (1, PAIR // half_dim))
+    sine = jnp.tile(jnp.concatenate([-jnp.sin(angles), jnp.sin(angles)], axis=1), (1, 2))
+    masks, tables = (query_mask, key_mask), (cosine, sine)
+
+    pairs = local_heads // PAIR
+    attn_in, qkv = project(x_all, 1.0 + scale_attn, shift_attn, qkv_w, cosine, sine)
+    mixed_heads, lse = attend(qkv, qkv, qkv, 0, pairs, 2 * pairs, pairs, 512, masks)
+    slots = lambda values: values.reshape(seqs, frames_here, -1)
+    mixed_slots = slots(mixed_heads)
+    mixed_got = [mixed_slots[0]] + [swap(mixed_slots[j], "seq", j) for j in range(1, seqs)]
+    attn_mixed = natural(mixed_got).transpose(1, 0, 2).reshape(frames_here, D)
+    attn_out = dot(attn_mixed, attn_w)
+    inputs = x_own.astype(jnp.float32)
+    after_attn = inputs + gate_attn * attn_out
+
+    normed_c, inv_c = layer_stats(after_attn)
+    cross_in = (normed_c * gain_values).astype(low)
+    cross_q = dot(cross_in, crossq_w).astype(low)
+    kv_mine = dot(context[0], kv_w).astype(low)
+    cross_kv = natural(spread(kv_mine)).transpose(1, 0, 2).reshape(text_len, 2 * D)
+    all_pairs = D // PAIR
+    cross_mixed, cross_lse = attend(cross_q, cross_kv, cross_kv, 0, 0, all_pairs, all_pairs, frames_here)
+    after_cross = after_attn + dot(cross_mixed, crossout_w)
+
+    normed_f, inv_f = layer_stats(after_cross)
+    ffn_in = (normed_f * (1.0 + scale_ffn) + shift_ffn).astype(low)
+    ffn_all = jnp.concatenate(spread(ffn_in))
+    units = FF // seqs
+    gate_up = dot(ffn_all, glu_w)
+    gate_pre, up_pre = gate_up[:, :units], gate_up[:, units:]
+    gate_act = jax.nn.silu(gate_pre)
+    hidden = (gate_act * up_pre).astype(low)
+
+    def return_slots(values):
+        stack = slots(values.astype(low))
+        total = stack[0].astype(jnp.float32)
+        for j in range(1, seqs):
+            total = total + swap(stack[j], "seq", j).astype(jnp.float32)
+        return total
+
+    ffn_out = return_slots(dot(hidden, down_w))
+    result = (after_cross + gate_ffn * ffn_out).astype(low)
+
+    row_scale = lax.dynamic_index_in_dim(bucket_weights, bucket_ids[my_row], 0)
+    grad_out = cotangent[0].astype(jnp.float32) * row_scale
+    grad_ffn_all = jnp.concatenate(spread((gate_ffn * grad_out).astype(low)))
+    dgate_ffn = jnp.sum(grad_out * ffn_out, axis=0)
+    grad_hidden = dot_right_t(grad_ffn_all, down_w)
+    grad_gate_up = jnp.concatenate(
+        [grad_hidden * up_pre * silu_slope(gate_pre), grad_hidden * gate_act], axis=-1
+    ).astype(low)
+    grad_ffn_in = return_slots(dot_right_t(grad_gate_up, glu_w))
+    grad_glu = lax.psum_scatter(
+        dot_left_t(ffn_all, grad_gate_up).astype(low), "row", scatter_dimension=0, tiled=True
+    )
+    grad_down = lax.psum_scatter(
+        dot_left_t(hidden, grad_ffn_all).astype(low), "row", scatter_dimension=0, tiled=True
+    )
+    dshift_ffn = jnp.sum(grad_ffn_in, axis=0)
+    dscale_ffn = jnp.sum(grad_ffn_in * normed_f, axis=0)
+    grad_cross = grad_out + norm_back(grad_ffn_in * (1.0 + scale_ffn), normed_f, inv_f)
+
+    grad_cross_low = grad_cross.astype(low)
+    grad_crossout = dot_left_t(cross_mixed, grad_cross_low)
+    grad_cmixed = dot_right_t(grad_cross_low, crossout_w).astype(low)
+    grad_cquery, grad_ckey, grad_cvalue = attend_back(
+        cross_q, cross_kv, cross_kv, grad_cmixed, cross_mixed, cross_lse,
+        0, 0, all_pairs, all_pairs, frames_here, text_len,
+    )
+    grad_ckv = jnp.concatenate([grad_ckey, grad_cvalue], axis=1).reshape(text_len, seqs, -1)
+    grad_ckv = sum(exchange(grad_ckv, 1))
+    grad_kv = jnp.einsum(
+        "cm,ce->me", context[0].astype(jnp.float32), grad_ckv, precision=highest
+    ).astype(low)
+    kv_got = exchange(grad_kv.reshape(rows, ctx_dim // rows, -1), 0, "row")
+    grad_kv = sum(g.astype(jnp.float32) for g in kv_got)
+    grad_kv = natural(exchange(grad_kv.reshape(seqs, ctx_dim // (rows * seqs), -1)))
+    grad_crosskv = grad_kv.transpose(1, 0, 2).reshape(ctx_dim // (rows * seqs), 2 * D)
+    grad_crossq = dot_left_t(cross_in, grad_cquery)
+    grad_cross_in = dot_right_t(grad_cquery, crossq_w)
+    grad_gain = jnp.sum(grad_cross_in * normed_c, axis=0)
+    grad_attn = grad_cross + norm_back(grad_cross_in * gain_values, normed_c, inv_c)
+
+    grad_attn_low = (gate_attn * grad_attn).astype(low)
+    dgate_attn = jnp.sum(grad_attn * attn_out, axis=0)
+    grad_attnout = dot_left_t(attn_mixed, grad_attn_low)
+    grad_wide = jnp.concatenate([grad_attnout, grad_crossq, grad_crossout], axis=1).astype(low)
+    grad_wide = lax.psum_scatter(grad_wide, ("row", "seq"), scatter_dimension=0, tiled=True)
+    grad_amixed = dot_right_t(grad_attn_low, attn_w).astype(low)
+    grad_heads = jnp.concatenate(exchange(grad_amixed.reshape(frames_here, seqs, local_heads), 1))
+    grad_projected = jnp.concatenate(
+        attend_back(
+            qkv, qkv, qkv, grad_heads, mixed_heads, lse,
+            0, pairs, 2 * pairs, pairs, 512, 512, masks, tables,
+        ),
+        axis=1,
+    )
+    grad_attn_in = return_slots(dot_right_t(grad_projected, qkv_w))
+    grad_qkv = lax.psum_scatter(
+        dot_left_t(attn_in, grad_projected).astype(low), "row", scatter_dimension=0, tiled=True
+    )
+    normed_a, inv_a = layer_stats(inputs)
+    dshift_attn = jnp.sum(grad_attn_in, axis=0)
+    dscale_attn = jnp.sum(grad_attn_in * normed_a, axis=0)
+    grad_frames = grad_attn + norm_back(grad_attn_in * (1.0 + scale_attn), normed_a, inv_a)
+
+    qkv_got = natural(exchange(grad_qkv.reshape(seqs, depth, -1)))
+    grad_qkv = qkv_got.reshape(seqs, depth, 3, local_heads).transpose(1, 2, 0, 3).reshape(depth, 3 * D)
+    glu_got = natural(exchange(grad_glu.reshape(seqs, depth, -1)))
+    grad_glu = (
+        glu_got.reshape(seqs, depth, 2, rows, part).transpose(1, 2, 3, 0, 4).reshape(depth, 2 * FF)
+    )
+
+    own_sums = sum_over(
+        jnp.stack(
+            [dshift_attn, dscale_attn, dgate_attn, dshift_ffn, dscale_ffn, dgate_ffn, grad_gain]
+        ),
+        "seq",
+    )
+    bucket_list = jnp.arange(BUCKETS, dtype=jnp.int32)
+    grad_mods = jnp.zeros((BUCKETS, 6 * D), jnp.float32)
+    gain_total = jnp.zeros((D,), jnp.float32)
+    for j, sums in enumerate(spread(own_sums, "row")):
+        hit = (bucket_list == bucket_ids[my_row ^ j]).astype(jnp.float32)
+        grad_mods = grad_mods + hit[:, None] * sums[:6].reshape(1, 6 * D)
+        gain_total = gain_total + sums[6]
+
+    def outer(left, right):
+        return sum(left[b][:, None] * right[b][None, :] for b in range(BUCKETS))
+
+    def gather_all(own):
+        across = natural(spread(own)).transpose(1, 0, 2).reshape(BUCKETS, -1)
+        return natural(spread(across, "row"), "row").transpose(1, 0, 2).reshape(BUCKETS, -1)
+
+    grad_modul = outer(mine(token_act, depth).astype(jnp.float32), grad_mods)
+    token_own = jnp.dot(grad_mods, w_mod.astype(jnp.float32).T, precision=highest)
+    grad_token = gather_all(token_own * silu_slope(mine(time_token, depth)))
+    grad_timeout = outer(mine(time_hidden, depth).astype(jnp.float32), grad_token)
+    hidden_own = jnp.dot(grad_token, w_time_out.astype(jnp.float32).T, precision=highest)
+    grad_pre = gather_all(hidden_own * silu_slope(mine(pre_hidden, depth)))
+    grad_timein = outer(mine(features, w_time_in.shape[0]).astype(jnp.float32), grad_pre)
+
+    grad_wide = grad_wide.astype(jnp.float32)
+    return (
+        result[None],
+        grad_frames[None],
+        grad_timein,
+        grad_timeout,
+        grad_modul,
+        grad_qkv.astype(jnp.float32),
+        grad_wide[:, :D],
+        mine(gain_total, depth),
+        grad_wide[:, D : 2 * D],
+        grad_crosskv,
+        grad_wide[:, 2 * D :],
+        grad_glu.astype(jnp.float32),
+        grad_down.astype(jnp.float32),
+    )
+
+
 def solution(mesh):
     placed = (
         P("row", "seq", None),
@@ -434,8 +971,10 @@
         P(("row", "seq"), None),
         P("row", "seq", None),
     )
+    rows, seqs = mesh.shape["row"], mesh.shape["seq"]
+    plan = functools.partial(on_device_split, rows, seqs) if can_split(rows, seqs) else on_device
     return jax.shard_map(
-        on_device,
+        plan,
         mesh=mesh,
         in_specs=placed,
         out_specs=(

time: 4130 us -> 1280 us (0.31)
  waiting for transfers between devices: 3140 us -> 523 us
  matrix products: 580 us -> 214 us
  Pallas kernels: 0 us -> 162 us
  blocking collectives: 157 us -> 0 us
  starting transfers between devices: 1.14 us -> 127 us
  other arithmetic: 170 us -> 90.8 us
  local copies, waits for them, and re-layouts: 59.1 us -> 122 us
    reduce_scatter x11 -> x3, waiting for transfers between devices: 2260 us -> 0.02 us  [the longest x1 0.02 us: on_device_split(): lax.psum_scatter(dot_left_t(ffn_all, grad_gate_up).astype(low), 'row', sc...]
    all_gather x11 -> x4, waiting for transfers between devices: 734 us -> 0.01 us  [the longest x1 0.01 us: on_device_split(): first_w = lax.all_gather(first_w, 'row', axis=0, tiled=True)]
    ppermute x0 -> x100, waiting for transfers between devices: none -> 455 us  [swap(): return lax.ppermute(value, axis, [(i, i ^ j) for i in range(sizes[axis])])]
    dot_general x36 -> x24, matrix products: 573 us -> 214 us  [the longest x6 81.4 us: dot_right_t(): jnp.einsum('fj,ij->fi', left, right, preferred_element_type=jnp.float32)]
    pallas_call x0 -> x5, Pallas kernels: none -> 162 us  [the longest x2 87.9 us: attend_back(): pl.pallas_call(functools.partial(attend_back_kernel, masked, chunk), grid...]
    ppermute x0 -> x100, starting transfers between devices: none -> 127 us  [swap(): return lax.ppermute(value, axis, [(i, i ^ j) for i in range(sizes[axis])])]
    unnamed x24 -> x9, waiting for transfers between devices: 148 us -> 68 us
    unnamed x2 -> x0, blocking collectives: 79.8 us -> none
  transfers between devices with their start and end apart: 23 -> 108, of which waited for: 19 -> 49; matrix products, arithmetic and copies ran while one was open for 12% -> 23% of each run, Pallas kernels for 0% -> 6%
where the time goes in v1:
time: 1280 us; the launch traced here: 1270 us
  waiting for transfers between devices  523 us (41%)
  matrix products  214 us (17%)
  Pallas kernels  162 us (13%)
  starting transfers between devices  127 us (10%)
  local copies, waits for them, and re-layouts  122 us (10%)
  other arithmetic  90.8 us (7%)
  between operations  32.3 us (3%)
    ppermute x100, waiting for transfers between devices, swap(): return lax.ppermute(value, axis, [(i, i ^ j) for i in range(sizes[axis])])  455 us
    ppermute x100, starting transfers between devices, swap(): return lax.ppermute(value, axis, [(i, i ^ j) for i in range(sizes[axis])])  127 us
    pallas_call x2, Pallas kernels, attend_back(): pl.pallas_call(functools.partial(attend_back_kernel, masked, chunk), grid...  87.9 us
    dot_general x6, matrix products, dot_right_t(): jnp.einsum('fj,ij->fi', left, right, preferred_element_type=jnp.float32)  81.4 us
    unnamed x9, waiting for transfers between devices  68 us
    dot_general x9, matrix products, dot(): return jnp.dot(left, right, preferred_element_type=jnp.float32)  65.8 us
    dot_general x6, matrix products, dot_left_t(): jnp.einsum('fi,fj->ij', left, right, preferred_element_type=jnp.float32)  62.8 us
    pallas_call x2, Pallas kernels, attend(): pl.pallas_call(functools.partial(attend_kernel, masked), grid=(pairs, cou...  56.8 us
  transfers between devices with their start and end apart: 108, of which 49 were waited for; matrix products, arithmetic and copies ran while one was open for 23% of the time, Pallas kernels for 6%

profile of v1, /device:TPU:0, one launch (start us, length us, event | category | flops | bytes accessed | tf_op | source)
XLA Modules:
  0.0 1271.0 jit_solution(7195049177875389469)
XLA Ops:
  13.3 3.0 collective-permute-start.22
  20.6 4.3 collective-permute-done.23
  29.8 5.1 constant_dynamic-slice_fusion.59
  40.6 6.6 collective-permute-done.34
  48.7 6.8 collective-permute-done.35
  61.7 3.5 collective-permute-done
  66.2 3.2 collective-permute-done.1
  75.2 3.6 collective-permute-start.4
  87.1 3.1 collective-permute-done.6
  92.4 5.2 collective-permute-done.8
  136.0 88.6 %collective-permute-done.17 = f32[1,9216]{1,0:T(1,128)} collective-permute-done((f32[1,9216]{1,0:T(1,128)S(1)}, f32[1,9216]{1,0:T(1,128)}, u32[]{:S(2)}, u32[]{:S(2)}) %collective-permute-start.17) | collective-permute-done | bytes 36896 | tf_op jit(solution)/shard_map/ppermute | solution.py:689
  230.2 6.6 pad_maximum_fusion.6.x_ref
  239.3 3.0 reshape.441
  247.6 4.2 slice.326.w_ref
  251.9 16.8 %project.1 = (bf16[2048,1536]{1,0:T(8,128)(2,1)}, bf16[2048,1152]{1,0:T(8,128)(2,1)}) custom-call(bf16[2048,1536]{1,0:T(8,128)(2,1)} %pad_maximum_fusion.6.x_ref, f32[1,1536]{1,0:T(1,128)S(1)} %get-tuple-element.239.scale_ref, f32[1,1536]{1,0:T(1,128)S(1)} %get-tuple-element.238.shift_ref, bf16[1536,1152]{1,0:T(8,128)(2,1)} %slice.326.w_ref, ...), custom_call_target="tpu_custom_call" | custom-call | flops 7247757312 | bytes 20840448 | tf_op jit(solution)/shard_map/project/pallas_call | solution.py:66
  268.7 47.1 %attend.2 = (bf16[2048,384]{1,0:T(8,128)(2,1)S(1)}, f32[3,2,2048]{2,1,0:T(2,128)S(1)}) custom-call(bf16[2048,1152]{1,0:T(8,128)(2,1)} %get-tuple-element.25.refs_0_.refs_1_.refs_2_, bf16[2048,1152]{1,0:T(8,128)(2,1)} %get-tuple-element.25.refs_0_.refs_1_.refs_2_, bf16[2048,1152]{1,0:T(8,128)(2,1)} %get-tuple-element.25.refs_0_.refs_1_.refs_2_, ...), custom_call_target="tpu_custom_call" | custom-call | flops 25769803776 | bytes 6291456 | tf_op jit(solution)/shard_map/attend/pallas_call | solution.py:127
  324.1 5.4 collective-permute-done.25
  329.5 5.6 collective-permute-done.26
  340.9 9.2 fusion.87
  351.6 5.1 fusion.35.refs_0_
  356.8 9.7 attend.3
  366.5 5.2 fusion.94
  382.9 29.0 %collective-permute-done.31 = bf16[512,1536]{1,0:T(8,128)(2,1)} collective-permute-done((bf16[512,1536]{1,0:T(8,128)(2,1)}, bf16[512,1536]{1,0:T(8,128)(2,1)}, u32[]{:S(2)}, u32[]{:S(2)}) %collective-permute-start.31) | collective-permute-done | bytes 1572896 | tf_op jit(solution)/shard_map/ppermute | solution.py:689
  413.6 33.5 %collective-permute-done.32 = bf16[512,1536]{1,0:T(8,128)(2,1)} collective-permute-done((bf16[512,1536]{1,0:T(8,128)(2,1)}, bf16[512,1536]{1,0:T(8,128)(2,1)}, u32[]{:S(2)}, u32[]{:S(2)}) %collective-permute-start.32) | collective-permute-done | bytes 1572896 | tf_op jit(solution)/shard_map/ppermute | solution.py:689
  447.1 30.4 %fusion.43 = f32[2048,3072]{1,0:T(8,128)} fusion(bf16[1536,3072]{1,0:T(8,128)(2,1)} %all-gather.9.cloned.1.call-done, bf16[512,1536]{1,0:T(8,128)(2,1)} %collective-permute-done.33, bf16[512,1536]{1,0:T(8,128)(2,1)} %collective-permute-done.32, bf16[512,1536]{1,0:T(8,128)(2,1)} %collective-permute-done.31, bf16[512,1536]{1,0:T(8,128)(2,1)} %add_convert_fusion.1), kind=kOutput, calls=%fused_computation.91 | convolution fusion | flops 19352518656 | bytes 40894464 | tf_op jit(solution)/shard_map/dot_general | solution.py:720
  479.3 30.9 %collective-permute-done.41 = bf16[512,1536]{1,0:T(8,128)(2,1)} collective-permute-done((bf16[512,1536]{1,0:T(8,128)(2,1)}, bf16[512,1536]{1,0:T(8,128)(2,1)}, u32[]{:S(2)}, u32[]{:S(2)}) %collective-permute-start.41) | collective-permute-done | bytes 1572896 | tf_op jit(solution)/shard_map/ppermute | solution.py:689
  510.2 25.2 %multiply_convert_fusion.1 = (bf16[2048,1536]{1,0:T(8,128)(2,1)}, bf16[2048,1536]{1,0:T(8,128)(2,1)}, bf16[2048,1536]{1,0:T(8,128)(2,1)}) fusion(f32[2048,3072]{1,0:T(8,128)} %fusion.43, bf16[1536,1536]{1,0:T(8,128)(2,1)} %all-gather.11.cloned.1.call-done, bf16[512,1536]{1,0:T(8,128)(2,1)} %collective-permute-done.42, ...), kind=kOutput, calls=%fused_computation.3 | convolution fusion | flops 9736028160 | bytes 55050240 | tf_op jit(solution)/shard_map/fj,ij->fi/dot_general | solution.py:723
  535.4 25.4 %fusion.2 = bf16[2048,1536]{1,0:T(8,128)(2,1)S(1)} fusion(bf16[1536,3072]{1,0:T(8,128)(2,1)} %all-gather.9.cloned.1.call-done, bf16[2048,1536]{1,0:T(8,128)(2,1)} %get-tuple-element.143, bf16[2048,1536]{1,0:T(8,128)(2,1)} %get-tuple-element.142), kind=kOutput, calls=%fused_computation.9 | convolution fusion | flops 19355664384 | bytes 28311552 | tf_op jit(solution)/shard_map/fj,ij->fi/dot_general | solution.py:723
  565.7 13.4 %convolution_convert_fusion.6 = bf16[2048,1536]{1,0:T(8,128)(2,1)S(1)} fusion(bf16[2048,1536]{1,0:T(8,128)(2,1)} %get-tuple-element.144, bf16[1536,1536]{1,0:T(8,128)(2,1)} %all-gather.11.cloned.1.call-done), kind=kOutput, calls=%fused_computation.15 | convolution fusion | flops 9666822144 | bytes 17301504 | tf_op jit(solution)/shard_map/dot_general | solution.py:720
  581.3 18.5 %collective-permute-done.43 = bf16[512,1536]{1,0:T(8,128)(2,1)S(1)} collective-permute-done((bf16[512,1536]{1,0:T(8,128)(2,1)}, bf16[512,1536]{1,0:T(8,128)(2,1)S(1)}, u32[]{:S(2)}, u32[]{:S(2)}) %collective-permute-start.43) | collective-permute-done | bytes 1572896 | tf_op jit(solution)/shard_map/ppermute | solution.py:689
  601.0 33.2 %collective-permute-done.44 = bf16[512,1536]{1,0:T(8,128)(2,1)S(1)} collective-permute-done((bf16[512,1536]{1,0:T(8,128)(2,1)S(1)}, bf16[512,1536]{1,0:T(8,128)(2,1)S(1)}, u32[]{:S(2)}, u32[]{:S(2)}) %collective-permute-start.44) | collective-permute-done | bytes 1572896 | tf_op jit(solution)/shard_map/ppermute | solution.py:689
  637.1 30.2 %collective-permute-done.37 = bf16[512,1536]{1,0:T(8,128)(2,1)S(1)} collective-permute-done((bf16[512,1536]{1,0:T(8,128)(2,1)S(1)}, bf16[512,1536]{1,0:T(8,128)(2,1)S(1)}, u32[]{:S(2)}, u32[]{:S(2)}) %collective-permute-start.37) | collective-permute-done | bytes 1572896 | tf_op jit(solution)/shard_map/ppermute | solution.py:689
  667.2 27.5 %collective-permute-done.38 = bf16[512,1536]{1,0:T(8,128)(2,1)S(1)} collective-permute-done((bf16[512,1536]{1,0:T(8,128)(2,1)S(1)}, bf16[512,1536]{1,0:T(8,128)(2,1)S(1)}, u32[]{:S(2)}, u32[]{:S(2)}) %collective-permute-start.38) | collective-permute-done | bytes 1572896 | tf_op jit(solution)/shard_map/ppermute | solution.py:689
  697.6 6.5 fusion.31
  704.1 7.2 fusion.38.refs_3_
  711.4 12.2 attend_back.2
  723.7 7.1 multiply_reduce_fusion
  734.6 6.1 fusion.32
  740.6 3.9 reshape.445
  744.6 6.3 constant_dynamic-slice_fusion.54
  754.8 7.0 collective-permute-done.46
  761.8 4.4 collective-permute-done.47
  767.6 75.7 %attend_back.3 = (bf16[2048,384]{1,0:T(8,128)(2,1)}, bf16[2048,384]{1,0:T(8,128)(2,1)}, bf16[2048,384]{1,0:T(8,128)(2,1)}) custom-call(bf16[2048,1152]{1,0:T(8,128)(2,1)} %get-tuple-element.25.refs_0_.refs_1_.refs_2_, bf16[2048,1152]{1,0:T(8,128)(2,1)} %get-tuple-element.25.refs_0_.refs_1_.refs_2_, ...), custom_call_target="tpu_custom_call" | custom-call | flops 64424509440 | bytes 12582912 | tf_op jit(solution)/shard_map/attend_back/pallas_call | solution.py:224
  848.2 10.1 convolution_convert_fusion.4
  858.3 27.9 %convolution_convert_fusion = bf16[1536,3072]{1,0:T(8,128)(2,1)} fusion(bf16[2048,1536]{1,0:T(8,128)(2,1)} %get-tuple-element.143, bf16[2048,1536]{1,0:T(8,128)(2,1)} %get-tuple-element.142, bf16[512,1536]{1,0:T(8,128)(2,1)} %collective-permute-done.33, bf16[512,1536]{1,0:T(8,128)(2,1)} %collective-permute-done.32, ...), kind=kOutput, calls=%fused_computation.7 | convolution fusion | flops 19382403072 | bytes 28311552 | tf_op jit(solution)/shard_map/fi,fj->ij/dot_general | solution.py:726
  886.3 15.7 %convolution_convert_fusion.7 = bf16[1536,1536]{1,0:T(8,128)(2,1)} fusion(bf16[2048,1536]{1,0:T(8,128)(2,1)} %get-tuple-element.144, bf16[512,1536]{1,0:T(8,128)(2,1)} %collective-permute-done.42, bf16[512,1536]{1,0:T(8,128)(2,1)} %collective-permute-done.41, bf16[512,1536]{1,0:T(8,128)(2,1)} %collective-permute-done.40, bf16[512,1536]{1,0:T(8,128)(2,1)} %fusion.30), kind=kOutput, calls=%fused_computation.16 | convolution fusion | flops 9691201536 | bytes 17301504 | tf_op jit(solution)/shard_map/fi,fj->ij/dot_general | solution.py:726
  917.0 3.3 convolution_convert_fusion.2
  925.3 7.0 collective-permute-done.85
  941.2 4.1 collective-permute-done.88
  945.3 10.4 convolution_convert_fusion.5
  957.8 14.6 %collective-permute-done.91 = bf16[96,768]{1,0:T(8,128)(2,1)S(1)} collective-permute-done((bf16[96,768]{1,0:T(8,128)(2,1)S(1)}, bf16[96,768]{1,0:T(8,128)(2,1)S(1)}, u32[]{:S(2)}, u32[]{:S(2)}) %collective-permute-start.91) | collective-permute-done | bytes 147488 | tf_op jit(solution)/shard_map/ppermute | solution.py:689
  982.0 24.1 %pad_maximum_fusion = bf16[1536,4608]{0,1:T(8,128)(2,1)} fusion(bf16[1536,1536]{0,1:T(8,128)(2,1)S(1)} %convolution_convert_fusion.1, bf16[1536,1536]{0,1:T(8,128)(2,1)S(1)} %convolution_convert_fusion.2, bf16[1536,1536]{0,1:T(8,128)(2,1)S(1)} %convolution_convert_fusion.3), kind=kLoop, calls=%fused_computation | loop fusion | flops 42467328 | bytes 28311552 | tf_op jit(solution)/shard_map/concatenate | solution.py:879
  1006.3 18.8 %copy.177 = bf16[1536,4608]{1,0:T(8,128)(2,1)} copy(bf16[1536,4608]{0,1:T(8,128)(2,1)} %pad_maximum_fusion) | data formatting | bytes 28311552
  1025.3 25.5 %collective-permute-done.95 = f32[24,768]{1,0:T(8,128)S(1)} collective-permute-done((f32[24,768]{1,0:T(8,128)S(1)}, f32[24,768]{1,0:T(8,128)S(1)}, u32[]{:S(2)}, u32[]{:S(2)}) %collective-permute-start.95) | collective-permute-done | bytes 73760 | tf_op jit(solution)/shard_map/ppermute | solution.py:689
  1051.6 5.7 fusion.28
  1061.9 3.8 collective-permute-done.53
  1065.8 19.2 %collective-permute-start.55 = (f32[7,1536]{1,0:T(8,128)S(1)}, f32[7,1536]{1,0:T(8,128)S(1)}, u32[]{:S(2)}, u32[]{:S(2)}) collective-permute-start(f32[7,1536]{1,0:T(8,128)S(1)} %add.588), channel_id=1, source_target_pairs={{0,8},{4,12},{8,0},{12,4},{16,24},{20,28},{24,16},{28,20},{1,9},{5... | collective-permute-start | bytes 129032 | tf_op jit(solution)/shard_map/ppermute | solution.py:689
  1091.3 6.4 fusion.27
  1128.8 3.0 collective-permute-start.79
  1156.9 8.3 collective-permute-done.97
  1165.8 5.8 collective-permute-done.99
  1176.0 6.4 copy.220
  1182.5 5.2 reshape.459
  1187.7 67.9 %reduce-scatter.13.cloned.1.call-done = bf16[48,4608]{1,0:T(8,128)(2,1)} async-done(((bf16[1536,4608]{1,0:T(8,128)(2,1)}), bf16[48,4608]{1,0:T(8,128)(2,1)}) %reduce-scatter.13.cloned.1.call-update) | async-done | bytes 442384
  (628 shorter events, 260.9 us)
Async XLA Ops:
  7.2 229.5 %all-gather.5.cloned.1.call-start = ((), (), s32[]{:S(2)}) async-start(), calls=%async_computation.4 | async-start | bytes 5308416 | tf_op jit(solution)/shard_map/all_gather | solution.py:751
  26.0 314.9 %all-gather.7.cloned.1.call-start = ((), (), s32[]{:S(2)}) async-start(), calls=%async_computation.5 | async-start | bytes 14598144 | tf_op jit(solution)/shard_map/all_gather | solution.py:754
  26.9 386.7 %all-gather.9.cloned.1.call-start = ((), (), s32[]{:S(2)}) async-start(), calls=%async_computation.6 | async-start | bytes 10616832 | tf_op jit(solution)/shard_map/all_gather | solution.py:760
  35.0 12.2 collective-permute-start.34
  37.0 18.4 %collective-permute-start.35 = (bf16[48,2,8,192]{3,2,1,0:T(8,128)(2,1)}, bf16[48,2,8,192]{3,2,1,0:T(8,128)(2,1)}, u32[]{:S(2)}, u32[]{:S(2)}) collective-permute-start(bf16[48,2,8,192]{3,2,1,0:T(8,128)(2,1)} %bitcast.276), channel_id=1, source_target_pairs={{0,2},{1,3},{2,0},{3,1},{4,6},{5,7},{6,4},{7,5},{8,10},{9,11},{10,... | collective-permute-start | bytes 884744 | tf_op jit(solution)/shard_map/ppermute | solution.py:689
  38.8 18.1 %collective-permute-start.36 = (bf16[48,2,8,192]{3,2,1,0:T(8,128)(2,1)}, bf16[48,2,8,192]{3,2,1,0:T(8,128)(2,1)}, u32[]{:S(2)}, u32[]{:S(2)}) collective-permute-start(bf16[48,2,8,192]{3,2,1,0:T(8,128)(2,1)} %bitcast.275), channel_id=1, source_target_pairs={{0,3},{1,2},{2,1},{3,0},{4,7},{5,6},{6,5},{7,4},{8,11},{9,10},{10,... | collective-permute-start | bytes 884744 | tf_op jit(solution)/shard_map/ppermute | solution.py:689
  59.8 450.4 %all-gather.11.cloned.1.call-start = ((), (), s32[]{:S(2)}) async-start(), calls=%async_computation.7 | async-start | bytes 5308416 | tf_op jit(solution)/shard_map/all_gather | solution.py:761
  65.9 1071.3 %reduce-scatter.7.cloned.1.call-start = ((), (), s32[]{:S(2)}) async-start(), calls=%async_computation.8 | async-start | bytes 3981312 | tf_op jit(solution)/shard_map/reduce_scatter | solution.py:891
  97.7 16.8 %collective-permute-start.9 = (f32[5,1536]{1,0:T(8,128)S(1)}, f32[5,1536]{1,0:T(8,128)S(1)}, u32[]{:S(2)}, u32[]{:S(2)}) collective-permute-start(f32[5,1536]{1,0:T(8,128)S(1)} %add.526), channel_id=1, source_target_pairs={{0,16},{4,20},{8,24},{12,28},{16,0},{20,4},{24,8},{28,12},{1,17},{... | collective-permute-start | bytes 92168 | tf_op jit(solution)/shard_map/ppermute | solution.py:689
  116.6 11.3 collective-permute-start.12
  117.1 11.2 collective-permute-start.13
  118.5 11.1 collective-permute-start.14
  119.7 11.8 collective-permute-start.15
  127.9 102.3 %collective-permute-start.19 = (bf16[512,1536]{1,0:T(8,128)(2,1)}, bf16[512,1536]{1,0:T(8,128)(2,1)}, u32[]{:S(2)}, u32[]{:S(2)}) collective-permute-start(bf16[512,1536]{1,0:T(8,128)(2,1)} %bitcast), channel_id=1, source_target_pairs={{0,1},{1,0},{2,3},{3,2},{4,5},{5,4},{6,7},{7,6},{8,9},{9,8},{10,11... | collective-permute-start | bytes 4718600 | tf_op jit(solution)/shard_map/ppermute | solution.py:689
  128.3 101.9 %collective-permute-start.20 = (bf16[512,1536]{1,0:T(8,128)(2,1)}, bf16[512,1536]{1,0:T(8,128)(2,1)}, u32[]{:S(2)}, u32[]{:S(2)}) collective-permute-start(bf16[512,1536]{1,0:T(8,128)(2,1)} %bitcast), channel_id=1, source_target_pairs={{0,2},{1,3},{2,0},{3,1},{4,6},{5,7},{6,4},{7,5},{8,10},{9,11},{10,... | collective-permute-start | bytes 4718600 | tf_op jit(solution)/shard_map/ppermute | solution.py:689
  129.6 100.6 %collective-permute-start.21 = (bf16[512,1536]{1,0:T(8,128)(2,1)}, bf16[512,1536]{1,0:T(8,128)(2,1)}, u32[]{:S(2)}, u32[]{:S(2)}) collective-permute-start(bf16[512,1536]{1,0:T(8,128)(2,1)} %bitcast), channel_id=1, source_target_pairs={{0,3},{1,2},{2,1},{3,0},{4,7},{5,6},{6,5},{7,4},{8,11},{9,10},{10,... | collective-permute-start | bytes 4718600 | tf_op jit(solution)/shard_map/ppermute | solution.py:689
  131.6 93.0 %collective-permute-start.17 = (f32[1,9216]{1,0:T(1,128)S(1)}, f32[1,9216]{1,0:T(1,128)}, u32[]{:S(2)}, u32[]{:S(2)}) collective-permute-start(f32[1,9216]{1,0:T(1,128)S(1)} %add_add_fusion), channel_id=1, source_target_pairs={{0,1},{1,0},{2,3},{3,2},{4,5},{5,4},{6,7},{7,6},{8,9},{9,8},{10,11... | collective-permute-start | bytes 110600 | tf_op jit(solution)/shard_map/ppermute | solution.py:689
  244.1 75.0 %collective-permute-start.28 = (bf16[128,768]{0,1:T(8,128)(2,1)S(1)}, bf16[128,768]{0,1:T(8,128)(2,1)S(1)}, u32[]{:S(2)}, u32[]{:S(2)}) collective-permute-start(bf16[128,768]{0,1:T(8,128)(2,1)S(1)} %bitcast.304), channel_id=1, source_target_pairs={{0,1},{1,0},{2,3},{3,2},{4,5},{5,4},{6,7},{7,6},{8,9},{9,8},{10,11... | collective-permute-start | bytes 589832 | tf_op jit(solution)/shard_map/ppermute | solution.py:689
  244.3 76.3 %collective-permute-start.29 = (bf16[128,768]{0,1:T(8,128)(2,1)S(1)}, bf16[128,768]{0,1:T(8,128)(2,1)S(1)}, u32[]{:S(2)}, u32[]{:S(2)}) collective-permute-start(bf16[128,768]{0,1:T(8,128)(2,1)S(1)} %bitcast.305), channel_id=1, source_target_pairs={{0,2},{1,3},{2,0},{3,1},{4,6},{5,7},{6,4},{7,5},{8,10},{9,11},{10,... | collective-permute-start | bytes 589832 | tf_op jit(solution)/shard_map/ppermute | solution.py:689
  246.3 74.3 %collective-permute-start.30 = (bf16[128,768]{0,1:T(8,128)(2,1)S(1)}, bf16[128,768]{0,1:T(8,128)(2,1)S(1)}, u32[]{:S(2)}, u32[]{:S(2)}) collective-permute-start(bf16[128,768]{0,1:T(8,128)(2,1)S(1)} %bitcast.306), channel_id=1, source_target_pairs={{0,3},{1,2},{2,1},{3,0},{4,7},{5,6},{6,5},{7,4},{8,11},{9,10},{10,... | collective-permute-start | bytes 589832 | tf_op jit(solution)/shard_map/ppermute | solution.py:689
  317.1 12.4 collective-permute-start.25
  317.1 18.0 %collective-permute-start.26 = (bf16[512,384]{1,0:T(8,128)(2,1)}, bf16[512,384]{1,0:T(8,128)(2,1)}, u32[]{:S(2)}, u32[]{:S(2)}) collective-permute-start(bf16[512,384]{1,0:T(8,128)(2,1)} %get-tuple-element.176), channel_id=1, source_target_pairs={{0,2},{1,3},{2,0},{3,1},{4,6},{5,7},{6,4},{7,5},{8,10},{9,11},{10,... | collective-permute-start | bytes 1179656 | tf_op jit(solution)/shard_map/ppermute | solution.py:689
  319.1 16.0 %collective-permute-start.27 = (bf16[512,384]{1,0:T(8,128)(2,1)}, bf16[512,384]{1,0:T(8,128)(2,1)}, u32[]{:S(2)}, u32[]{:S(2)}) collective-permute-start(bf16[512,384]{1,0:T(8,128)(2,1)} %get-tuple-element.175), channel_id=1, source_target_pairs={{0,3},{1,2},{2,1},{3,0},{4,7},{5,6},{6,5},{7,4},{8,11},{9,10},{10,... | collective-permute-start | bytes 1179656 | tf_op jit(solution)/shard_map/ppermute | solution.py:689
  374.2 37.6 %collective-permute-start.31 = (bf16[512,1536]{1,0:T(8,128)(2,1)}, bf16[512,1536]{1,0:T(8,128)(2,1)}, u32[]{:S(2)}, u32[]{:S(2)}) collective-permute-start(bf16[512,1536]{1,0:T(8,128)(2,1)} %add_convert_fusion.1), channel_id=1, source_target_pairs={{0,1},{1,0},{2,3},{3,2},{4,5},{5,4},{6,7},{7,6},{8,9},{9,8},{10,11... | collective-permute-start | bytes 4718600 | tf_op jit(solution)/shard_map/ppermute | solution.py:689
  375.7 71.4 %collective-permute-start.32 = (bf16[512,1536]{1,0:T(8,128)(2,1)}, bf16[512,1536]{1,0:T(8,128)(2,1)}, u32[]{:S(2)}, u32[]{:S(2)}) collective-permute-start(bf16[512,1536]{1,0:T(8,128)(2,1)} %add_convert_fusion.1), channel_id=1, source_target_pairs={{0,2},{1,3},{2,0},{3,1},{4,6},{5,7},{6,4},{7,5},{8,10},{9,11},{10,... | collective-permute-start | bytes 4718600 | tf_op jit(solution)/shard_map/ppermute | solution.py:689
  376.5 70.6 %collective-permute-start.33 = (bf16[512,1536]{1,0:T(8,128)(2,1)}, bf16[512,1536]{1,0:T(8,128)(2,1)}, u32[]{:S(2)}, u32[]{:S(2)}) collective-permute-start(bf16[512,1536]{1,0:T(8,128)(2,1)} %add_convert_fusion.1), channel_id=1, source_target_pairs={{0,3},{1,2},{2,1},{3,0},{4,7},{5,6},{6,5},{7,4},{8,11},{9,10},{10,... | collective-permute-start | bytes 4718600 | tf_op jit(solution)/shard_map/ppermute | solution.py:689
  380.6 98.7 %collective-permute-start.40 = (bf16[512,1536]{1,0:T(8,128)(2,1)}, bf16[512,1536]{1,0:T(8,128)(2,1)}, u32[]{:S(2)}, u32[]{:S(2)}) collective-permute-start(bf16[512,1536]{1,0:T(8,128)(2,1)} %fusion.30), channel_id=1, source_target_pairs={{0,1},{1,0},{2,3},{3,2},{4,5},{5,4},{6,7},{7,6},{8,9},{9,8},{10,11... | collective-permute-start | bytes 4718600 | tf_op jit(solution)/shard_map/ppermute | solution.py:689
  382.1 128.1 %collective-permute-start.41 = (bf16[512,1536]{1,0:T(8,128)(2,1)}, bf16[512,1536]{1,0:T(8,128)(2,1)}, u32[]{:S(2)}, u32[]{:S(2)}) collective-permute-start(bf16[512,1536]{1,0:T(8,128)(2,1)} %fusion.30), channel_id=1, source_target_pairs={{0,2},{1,3},{2,0},{3,1},{4,6},{5,7},{6,4},{7,5},{8,10},{9,11},{10,... | collective-permute-start | bytes 4718600 | tf_op jit(solution)/shard_map/ppermute | solution.py:689
  411.9 98.3 %collective-permute-start.42 = (bf16[512,1536]{1,0:T(8,128)(2,1)}, bf16[512,1536]{1,0:T(8,128)(2,1)}, u32[]{:S(2)}, u32[]{:S(2)}) collective-permute-start(bf16[512,1536]{1,0:T(8,128)(2,1)} %fusion.30), channel_id=1, source_target_pairs={{0,3},{1,2},{2,1},{3,0},{4,7},{5,6},{6,5},{7,4},{8,11},{9,10},{10,... | collective-permute-start | bytes 4718600 | tf_op jit(solution)/shard_map/ppermute | solution.py:689
  562.2 37.5 %collective-permute-start.43 = (bf16[512,1536]{1,0:T(8,128)(2,1)}, bf16[512,1536]{1,0:T(8,128)(2,1)S(1)}, u32[]{:S(2)}, u32[]{:S(2)}) collective-permute-start(bf16[512,1536]{1,0:T(8,128)(2,1)} %get-tuple-element.150), channel_id=1, source_target_pairs={{0,1},{1,0},{2,3},{3,2},{4,5},{5,4},{6,7},{7,6},{8,9},{9,8},{10,11... | collective-permute-start | bytes 4718600 | tf_op jit(solution)/shard_map/ppermute | solution.py:689
  563.1 71.0 %collective-permute-start.44 = (bf16[512,1536]{1,0:T(8,128)(2,1)S(1)}, bf16[512,1536]{1,0:T(8,128)(2,1)S(1)}, u32[]{:S(2)}, u32[]{:S(2)}) collective-permute-start(bf16[512,1536]{1,0:T(8,128)(2,1)S(1)} %get-tuple-element.152), channel_id=1, source_target_pairs={{0,2},{1,3},{2,0},{3,1},{4,6},{5,7},{6,4},{7,5},{8,10},{9,11},{10,... | collective-permute-start | bytes 4718600 | tf_op jit(solution)/shard_map/ppermute | solution.py:689
  564.0 70.2 %collective-permute-start.45 = (bf16[512,1536]{1,0:T(8,128)(2,1)S(1)}, bf16[512,1536]{1,0:T(8,128)(2,1)S(1)}, u32[]{:S(2)}, u32[]{:S(2)}) collective-permute-start(bf16[512,1536]{1,0:T(8,128)(2,1)S(1)} %get-tuple-element.151), channel_id=1, source_target_pairs={{0,3},{1,2},{2,1},{3,0},{4,7},{5,6},{6,5},{7,4},{8,11},{9,10},{10,... | collective-permute-start | bytes 4718600 | tf_op jit(solution)/shard_map/ppermute | solution.py:689
  579.4 87.8 %collective-permute-start.37 = (bf16[512,1536]{1,0:T(8,128)(2,1)S(1)}, bf16[512,1536]{1,0:T(8,128)(2,1)S(1)}, u32[]{:S(2)}, u32[]{:S(2)}) collective-permute-start(bf16[512,1536]{1,0:T(8,128)(2,1)S(1)} %get-tuple-element.153), channel_id=1, source_target_pairs={{0,1},{1,0},{2,3},{3,2},{4,5},{5,4},{6,7},{7,6},{8,9},{9,8},{10,11... | collective-permute-start | bytes 4718600 | tf_op jit(solution)/shard_map/ppermute | solution.py:689
  580.4 114.3 %collective-permute-start.38 = (bf16[512,1536]{1,0:T(8,128)(2,1)S(1)}, bf16[512,1536]{1,0:T(8,128)(2,1)S(1)}, u32[]{:S(2)}, u32[]{:S(2)}) collective-permute-start(bf16[512,1536]{1,0:T(8,128)(2,1)S(1)} %get-tuple-element.155), channel_id=1, source_target_pairs={{0,2},{1,3},{2,0},{3,1},{4,6},{5,7},{6,4},{7,5},{8,10},{9,11},{10,... | collective-permute-start | bytes 4718600 | tf_op jit(solution)/shard_map/ppermute | solution.py:689
  599.8 96.7 %collective-permute-start.39 = (bf16[512,1536]{1,0:T(8,128)(2,1)S(1)}, bf16[512,1536]{1,0:T(8,128)(2,1)S(1)}, u32[]{:S(2)}, u32[]{:S(2)}) collective-permute-start(bf16[512,1536]{1,0:T(8,128)(2,1)S(1)} %get-tuple-element.154), channel_id=1, source_target_pairs={{0,3},{1,2},{2,1},{3,0},{4,7},{5,6},{6,5},{7,4},{8,11},{9,10},{10,... | collective-permute-start | bytes 4718600 | tf_op jit(solution)/shard_map/ppermute | solution.py:689
  751.0 10.9 collective-permute-start.46
  751.8 14.4 %collective-permute-start.47 = (bf16[512,384]{1,0:T(8,128)(2,1)S(1)}, bf16[512,384]{1,0:T(8,128)(2,1)S(1)}, u32[]{:S(2)}, u32[]{:S(2)}) collective-permute-start(bf16[512,384]{1,0:T(8,128)(2,1)S(1)} %bitcast.322), channel_id=1, source_target_pairs={{0,2},{1,3},{2,0},{3,1},{4,6},{5,7},{6,4},{7,5},{8,10},{9,11},{10,... | collective-permute-start | bytes 1179656 | tf_op jit(solution)/shard_map/ppermute | solution.py:689
  753.8 12.4 collective-permute-start.48
  858.2 288.2 %reduce-scatter.9.cloned.1.call-start = ((), (), s32[]{:S(2)}) async-start(), calls=%async_computation.9 | async-start | bytes 10616832 | tf_op jit(solution)/shard_map/reduce_scatter | solution.py:845
  886.3 268.5 %reduce-scatter.11.cloned.1.call-start = ((), (), s32[]{:S(2)}) async-start(), calls=%async_computation.10 | async-start | bytes 5308416 | tf_op jit(solution)/shard_map/reduce_scatter | solution.py:848
  902.0 353.5 %reduce-scatter.13.cloned.1.call-start = ((), (), s32[]{:S(2)}) async-start(), calls=%async_computation.11 | async-start | bytes 14598144
  913.2 12.1 collective-permute-start.84
  915.0 17.3 %collective-permute-start.85 = (f32[128,768]{1,0:T(8,128)S(1)}, f32[128,768]{1,0:T(8,128)S(1)}, u32[]{:S(2)}, u32[]{:S(2)}) collective-permute-start(f32[128,768]{1,0:T(8,128)S(1)} %bitcast.318), channel_id=1, source_target_pairs={{0,2},{1,3},{2,0},{3,1},{4,6},{5,7},{6,4},{7,5},{8,10},{9,11},{10,... | collective-permute-start | bytes 1179656 | tf_op jit(solution)/shard_map/ppermute | solution.py:689
  915.5 16.8 %collective-permute-start.86 = (f32[128,768]{1,0:T(8,128)S(1)}, f32[128,768]{1,0:T(8,128)S(1)}, u32[]{:S(2)}, u32[]{:S(2)}) collective-permute-start(f32[128,768]{1,0:T(8,128)S(1)} %bitcast.319), channel_id=1, source_target_pairs={{0,3},{1,2},{2,1},{3,0},{4,7},{5,6},{6,5},{7,4},{8,11},{9,10},{10,... | collective-permute-start | bytes 1179656 | tf_op jit(solution)/shard_map/ppermute | solution.py:689
  933.7 11.6 collective-permute-start.88
  936.7 19.1 %collective-permute-start.89 = (bf16[96,768]{1,0:T(8,128)(2,1)S(1)}, bf16[96,768]{1,0:T(8,128)(2,1)S(1)}, u32[]{:S(2)}, u32[]{:S(2)}) collective-permute-start(bf16[96,768]{1,0:T(8,128)(2,1)S(1)} %get-tuple-element.194), channel_id=1, source_target_pairs={{0,12},{4,8},{8,4},{12,0},{16,28},{20,24},{24,20},{28,16},{1,13},{... | collective-permute-start | bytes 442376 | tf_op jit(solution)/shard_map/ppermute | solution.py:689
  938.5 19.3 %collective-permute-start.90 = (bf16[96,768]{1,0:T(8,128)(2,1)S(1)}, bf16[96,768]{1,0:T(8,128)(2,1)S(1)}, u32[]{:S(2)}, u32[]{:S(2)}) collective-permute-start(bf16[96,768]{1,0:T(8,128)(2,1)S(1)} %get-tuple-element.193), channel_id=1, source_target_pairs={{0,16},{4,20},{8,24},{12,28},{16,0},{20,4},{24,8},{28,12},{1,17},{... | collective-permute-start | bytes 442376 | tf_op jit(solution)/shard_map/ppermute | solution.py:689
  938.5 33.9 %collective-permute-start.91 = (bf16[96,768]{1,0:T(8,128)(2,1)S(1)}, bf16[96,768]{1,0:T(8,128)(2,1)S(1)}, u32[]{:S(2)}, u32[]{:S(2)}) collective-permute-start(bf16[96,768]{1,0:T(8,128)(2,1)S(1)} %get-tuple-element.192), channel_id=1, source_target_pairs={{0,20},{4,16},{8,28},{12,24},{16,4},{20,0},{24,12},{28,8},{1,21},{... | collective-permute-start | bytes 442376 | tf_op jit(solution)/shard_map/ppermute | solution.py:689
  941.1 31.3 %collective-permute-start.92 = (bf16[96,768]{1,0:T(8,128)(2,1)S(1)}, bf16[96,768]{1,0:T(8,128)(2,1)S(1)}, u32[]{:S(2)}, u32[]{:S(2)}) collective-permute-start(bf16[96,768]{1,0:T(8,128)(2,1)S(1)} %get-tuple-element.191), channel_id=1, source_target_pairs={{0,24},{4,28},{8,16},{12,20},{16,8},{20,12},{24,0},{28,4},{1,25},{... | collective-permute-start | bytes 442376 | tf_op jit(solution)/shard_map/ppermute | solution.py:689
  945.3 27.4 %collective-permute-start.93 = (bf16[96,768]{1,0:T(8,128)(2,1)S(1)}, bf16[96,768]{1,0:T(8,128)(2,1)S(1)}, u32[]{:S(2)}, u32[]{:S(2)}) collective-permute-start(bf16[96,768]{1,0:T(8,128)(2,1)S(1)} %get-tuple-element.190), channel_id=1, source_target_pairs={{0,28},{4,24},{8,20},{12,16},{16,12},{20,8},{24,4},{28,0},{1,29},{... | collective-permute-start | bytes 442376 | tf_op jit(solution)/shard_map/ppermute | solution.py:689
  975.2 76.3 %collective-permute-start.49 = (bf16[512,1536]{1,0:T(8,128)(2,1)}, bf16[512,1536]{1,0:T(8,128)(2,1)}, u32[]{:S(2)}, u32[]{:S(2)}) collective-permute-start(bf16[512,1536]{1,0:T(8,128)(2,1)} %get-tuple-element.147), channel_id=1, source_target_pairs={{0,1},{1,0},{2,3},{3,2},{4,5},{5,4},{6,7},{7,6},{8,9},{9,8},{10,11... | collective-permute-start | bytes 4718600 | tf_op jit(solution)/shard_map/ppermute | solution.py:689
  977.0 74.5 %collective-permute-start.50 = (bf16[512,1536]{1,0:T(8,128)(2,1)}, bf16[512,1536]{1,0:T(8,128)(2,1)}, u32[]{:S(2)}, u32[]{:S(2)}) collective-permute-start(bf16[512,1536]{1,0:T(8,128)(2,1)} %get-tuple-element.149), channel_id=1, source_target_pairs={{0,2},{1,3},{2,0},{3,1},{4,6},{5,7},{6,4},{7,5},{8,10},{9,11},{10,... | collective-permute-start | bytes 4718600 | tf_op jit(solution)/shard_map/ppermute | solution.py:689
  977.3 74.3 %collective-permute-start.51 = (bf16[512,1536]{1,0:T(8,128)(2,1)S(1)}, bf16[512,1536]{1,0:T(8,128)(2,1)}, u32[]{:S(2)}, u32[]{:S(2)}) collective-permute-start(bf16[512,1536]{1,0:T(8,128)(2,1)S(1)} %get-tuple-element.148), channel_id=1, source_target_pairs={{0,3},{1,2},{2,1},{3,0},{4,7},{5,6},{6,5},{7,4},{8,11},{9,10},{10,... | collective-permute-start | bytes 4718600 | tf_op jit(solution)/shard_map/ppermute | solution.py:689
  978.7 72.1 %collective-permute-start.95 = (f32[24,768]{1,0:T(8,128)S(1)}, f32[24,768]{1,0:T(8,128)S(1)}, u32[]{:S(2)}, u32[]{:S(2)}) collective-permute-start(f32[24,768]{1,0:T(8,128)S(1)} %get-tuple-element.222), channel_id=1, source_target_pairs={{0,2},{1,3},{2,0},{3,1},{4,6},{5,7},{6,4},{7,5},{8,10},{9,11},{10,... | collective-permute-start | bytes 221192 | tf_op jit(solution)/shard_map/ppermute | solution.py:689
  980.1 70.8 %collective-permute-start.96 = (f32[24,768]{1,0:T(8,128)S(1)}, f32[24,768]{1,0:T(8,128)S(1)}, u32[]{:S(2)}, u32[]{:S(2)}) collective-permute-start(f32[24,768]{1,0:T(8,128)S(1)} %get-tuple-element.221), channel_id=1, source_target_pairs={{0,3},{1,2},{2,1},{3,0},{4,7},{5,6},{6,5},{7,4},{8,11},{9,10},{10,... | collective-permute-start | bytes 221192 | tf_op jit(solution)/shard_map/ppermute | solution.py:689
  1065.7 21.8 %collective-permute-start.54 = (f32[7,1536]{1,0:T(8,128)S(1)}, f32[7,1536]{1,0:T(8,128)S(1)}, u32[]{:S(2)}, u32[]{:S(2)}) collective-permute-start(f32[7,1536]{1,0:T(8,128)S(1)} %add.588), channel_id=1, source_target_pairs={{0,4},{4,0},{8,12},{12,8},{16,20},{20,16},{24,28},{28,24},{1,5},{5... | collective-permute-start | bytes 129032 | tf_op jit(solution)/shard_map/ppermute | solution.py:689
  1065.8 23.4 %collective-permute-start.55 = (f32[7,1536]{1,0:T(8,128)S(1)}, f32[7,1536]{1,0:T(8,128)S(1)}, u32[]{:S(2)}, u32[]{:S(2)}) collective-permute-start(f32[7,1536]{1,0:T(8,128)S(1)} %add.588), channel_id=1, source_target_pairs={{0,8},{4,12},{8,0},{12,4},{16,24},{20,28},{24,16},{28,20},{1,9},{5... | collective-permute-start | bytes 129032 | tf_op jit(solution)/shard_map/ppermute | solution.py:689
  1085.0 12.7 collective-permute-start.56
  1085.1 12.6 collective-permute-start.57
  1085.1 12.7 collective-permute-start.58
  1087.5 10.3 collective-permute-start.59
  1148.6 16.6 %collective-permute-start.97 = (bf16[48,3072]{1,0:T(8,128)(2,1)}, bf16[48,3072]{1,0:T(8,128)(2,1)S(1)}, u32[]{:S(2)}, u32[]{:S(2)}) collective-permute-start(bf16[48,3072]{1,0:T(8,128)(2,1)} %get-tuple-element.185), channel_id=1, source_target_pairs={{0,1},{1,0},{2,3},{3,2},{4,5},{5,4},{6,7},{7,6},{8,9},{9,8},{10,11... | collective-permute-start | bytes 884744 | tf_op jit(solution)/shard_map/ppermute | solution.py:689
  1150.9 14.9 %collective-permute-start.98 = (bf16[48,3072]{1,0:T(8,128)(2,1)}, bf16[48,3072]{1,0:T(8,128)(2,1)}, u32[]{:S(2)}, u32[]{:S(2)}) collective-permute-start(bf16[48,3072]{1,0:T(8,128)(2,1)} %get-tuple-element.184), channel_id=1, source_target_pairs={{0,2},{1,3},{2,0},{3,1},{4,6},{5,7},{6,4},{7,5},{8,10},{9,11},{10,... | collective-permute-start | bytes 884744 | tf_op jit(solution)/shard_map/ppermute | solution.py:689
  1152.4 19.3 %collective-permute-start.99 = (bf16[48,3072]{1,0:T(8,128)(2,1)}, bf16[48,3072]{1,0:T(8,128)(2,1)}, u32[]{:S(2)}, u32[]{:S(2)}) collective-permute-start(bf16[48,3072]{1,0:T(8,128)(2,1)} %get-tuple-element.183), channel_id=1, source_target_pairs={{0,3},{1,2},{2,1},{3,0},{4,7},{5,6},{6,5},{7,4},{8,11},{9,10},{10,... | collective-permute-start | bytes 884744 | tf_op jit(solution)/shard_map/ppermute | solution.py:689
  (132 other events, 2157.8 us)
Sparse Core Ops, SparseCore 0:
  26.1 52.0 all-gather.4
  81.6 158.3 all-gather.6
  242.2 91.6 all-gather.8
  335.4 50.1 all-gather.10
  858.4 42.7 reduce-scatter.6
  903.4 116.9 reduce-scatter.8
  1022.9 58.9 reduce-scatter.10
  1088.8 166.6 reduce-scatter.12

commit v2 on v1

--- a/solution.py
+++ b/solution.py
@@ -41,32 +41,59 @@
     return jnp.where((lane // HEAD_DIM) == head, values, 0.0)
 
 
-def project_kernel(x_ref, scale_ref, shift_ref, w_ref, cos_ref, sin_ref, in_ref, out_ref):
+def norm_block(x_ref):
     values = x_ref[...].astype(f32)
     center = values - jnp.mean(values, axis=-1, keepdims=True)
-    inv_std = lax.rsqrt(jnp.mean(center * center, axis=-1, keepdims=True) + 1e-05)
-    modulated = (center * inv_std * scale_ref[...] + shift_ref[...]).astype(bf16)
-    in_ref[...] = modulated
-    projected = dot_nn(modulated, w_ref[...])
-    cosine = cos_ref[...]
-    sine = sin_ref[...]
-    width = out_ref.shape[1]
-    for start in range(0, width, PAIR):
-        part = projected[:, start : start + PAIR]
-        if start < 2 * width // 3:
-            part = part * cosine + swap_halves(part) * sine
-        out_ref[:, start : start + PAIR] = part.astype(bf16)
-
-
-def project(x, scale, shift, w, cosine, sine, block=256):
-    count, depth = x.shape
-    width = w.shape[1]
+    return center * lax.rsqrt(jnp.mean(center * center, axis=-1, keepdims=True) + 1e-05)
+
+
+def project_kernel(per_slot, *refs):
+    x_refs, (scale_ref, shift_ref, w_ref, cos_ref, sin_ref, in_ref, out_ref) = refs[:-7], refs[-7:]
+
+    def run(x_ref):
+        modulated = (norm_block(x_ref) * scale_ref[...] + shift_ref[...]).astype(bf16)
+        in_ref[...] = modulated
+        projected = dot_nn(modulated, w_ref[...])
+        cosine = cos_ref[...]
+        sine = sin_ref[...]
+        width = out_ref.shape[1]
+        for start in range(0, width, PAIR):
+            part = projected[:, start : start + PAIR]
+            if start < 2 * width // 3:
+                part = part * cosine + swap_halves(part) * sine
+            out_ref[:, start : start + PAIR] = part.astype(bf16)
+
+    for slot, x_ref in enumerate(x_refs):
+        pl.when(pl.program_id(0) // per_slot == slot)(functools.partial(run, x_ref))
+
+
+def slot_specs(x_slots, block):
+    per_slot, depth = x_slots[0].shape[0] // block, x_slots[0].shape[1]
+
+    def one(slot):
+        return pl.BlockSpec((block, depth), lambda i: (jnp.clip(i - slot * per_slot, 0, per_slot - 1), 0))
+
+    return per_slot, [one(slot) for slot in range(len(x_slots))]
+
+
+def project(x_slots, scale, shift, w, width, cosine, sine, block=256):
+    per_slot, x_specs = slot_specs(x_slots, block)
+    depth = x_slots[0].shape[1]
+    count = len(x_slots) * x_slots[0].shape[0]
     row_spec = lambda cols: pl.BlockSpec((block, cols), lambda i: (i, 0))
     whole = lambda a: pl.BlockSpec(a.shape, lambda i: (0, 0))
+
     return pl.pallas_call(
-        project_kernel,
+        functools.partial(project_kernel, per_slot),
         grid=(count // block,),
-        in_specs=[row_spec(depth), whole(scale), whole(shift), whole(w), row_spec(PAIR), row_spec(PAIR)],
+        in_specs=x_specs
+        + [
+            whole(scale),
+            whole(shift),
+            pl.BlockSpec((depth, width), lambda i: (0, 0)),
+            row_spec(PAIR),
+            row_spec(PAIR),
+        ],
         out_specs=[row_spec(depth), row_spec(width)],
         out_shape=[
             jax.ShapeDtypeStruct((count, depth), bf16),
@@ -79,7 +106,54 @@
             transcendentals=count,
         ),
         name="project",
-    )(x, scale, shift, w, cosine, sine)
+    )(*x_slots, scale, shift, w, cosine, sine)
+
+
+def project_back_kernel(per_slot, *refs):
+    x_refs, (grad_ref, w_ref, out_ref, sums_ref) = refs[:-4], refs[-4:]
+
+    @pl.when(pl.program_id(0) == 0)
+    def _():
+        sums_ref[...] = jnp.zeros_like(sums_ref)
+
+    def run(x_ref):
+        part = dot_nt(grad_ref[...], w_ref[...])
+        out_ref[...] = part.astype(bf16)
+        sums_ref[0:1, :] += jnp.sum(part, axis=0, keepdims=True)
+        sums_ref[1:2, :] += jnp.sum(part * norm_block(x_ref), axis=0, keepdims=True)
+
+    for slot, x_ref in enumerate(x_refs):
+        pl.when(pl.program_id(0) // per_slot == slot)(functools.partial(run, x_ref))
+
+
+def project_back(grad, w, x_slots, block=256):
+    per_slot, x_specs = slot_specs(x_slots, block)
+    count, width = grad.shape
+    depth = x_slots[0].shape[1]
+    return pl.pallas_call(
+        functools.partial(project_back_kernel, per_slot),
+        grid=(count // block,),
+        in_specs=x_specs
+        + [
+            pl.BlockSpec((block, width), lambda i: (i, 0)),
+            pl.BlockSpec((depth, width), lambda i: (0, 0)),
+        ],
+        out_specs=[
+            pl.BlockSpec((block, depth), lambda i: (i, 0)),
+            pl.BlockSpec((2, depth), lambda i: (0, 0)),
+        ],
+        out_shape=[
+            jax.ShapeDtypeStruct((count, depth), bf16),
+            jax.ShapeDtypeStruct((2, depth), f32),
+        ],
+        compiler_params=pltpu.CompilerParams(vmem_limit_bytes=VMEM),
+        cost_estimate=pl.CostEstimate(
+            flops=2 * count * depth * width,
+            bytes_accessed=2 * (2 * count * depth + depth * width + count * width),
+            transcendentals=count,
+        ),
+        name="project_back",
+    )(*x_slots, grad, w)
 
 
 def attend_kernel(masked, *refs):
@@ -245,6 +319,46 @@
         ),
         name="attend_back",
     )(*operands)
+def split_units_kernel(seqs, part, w_ref, out_ref):
+    block = seqs * part
+    for pair in range(w_ref.shape[1] // (2 * block)):
+        groups = [
+            w_ref[:, (2 * pair + k) * block : (2 * pair + k + 1) * block].astype(f32) for k in range(2)
+        ]
+        for t in range(seqs):
+            both = [g[:, t * part : (t + 1) * part] for g in groups]
+            out_ref[t, :, 2 * pair * part : 2 * (pair + 1) * part] = jnp.concatenate(both, axis=1).astype(bf16)
+
+
+def split_units(w, seqs, part):
+    depth, width = w.shape
+    return pl.pallas_call(
+        functools.partial(split_units_kernel, seqs, part),
+        out_shape=jax.ShapeDtypeStruct((seqs, depth, width // seqs), bf16),
+        compiler_params=pltpu.CompilerParams(vmem_limit_bytes=VMEM),
+        cost_estimate=pl.CostEstimate(flops=0, bytes_accessed=4 * depth * width, transcendentals=0),
+        name="split_units",
+    )(w)
+
+
+def join_units_kernel(seqs, part, in_ref, out_ref):
+    block = seqs * part
+    for pair in range(out_ref.shape[1] // (2 * block)):
+        both = [in_ref[t, :, 2 * pair * part : 2 * (pair + 1) * part].astype(f32) for t in range(seqs)]
+        for k in range(2):
+            group = [b[:, k * part : (k + 1) * part] for b in both]
+            out_ref[:, (2 * pair + k) * block : (2 * pair + k + 1) * block] = jnp.concatenate(group, axis=1)
+
+
+def join_units(stack, part):
+    seqs, depth, width = stack.shape
+    return pl.pallas_call(
+        functools.partial(join_units_kernel, seqs, part),
+        out_shape=jax.ShapeDtypeStruct((depth, width * seqs), f32),
+        compiler_params=pltpu.CompilerParams(vmem_limit_bytes=VMEM),
+        cost_estimate=pl.CostEstimate(flops=0, bytes_accessed=6 * depth * width * seqs, transcendentals=0),
+        name="join_units",
+    )(stack)
 
 
 highest = lax.Precision.HIGHEST
@@ -706,12 +820,40 @@
         stack = jnp.stack(slots)
         return jnp.stack([pick(stack, axis_name, t) for t in range(len(slots))])
 
+    def exchange_lines(stack, dim):
+        pieces = [
+            lax.dynamic_index_in_dim(stack, (my_row // 2) ^ j, dim, keepdims=False)
+            for j in range(rows // 2)
+        ]
+        return [pieces[0]] + [swap(p, "row", 2 * j) for j, p in enumerate(pieces) if j]
+
     def exchange(stack, dim=0, axis_name="seq"):
         pieces = [pick(stack, axis_name, j, dim) for j in range(sizes[axis_name])]
         return [pieces[0]] + [swap(p, axis_name, j) for j, p in enumerate(pieces) if j]
 
     def spread(value, axis_name="seq"):
         return [value] + [swap(value, axis_name, j) for j in range(1, sizes[axis_name])]
+
+    def after(value, *others):
+        return lax.optimization_barrier((value,) + others)[0]
+
+    def spread_two(value):
+        if seqs != 4:
+            return spread(value), None
+        near = [swap(value, "seq", 1), swap(value, "seq", 2)]
+        return [value] + near, near
+
+    def opposite(near):
+        half = near[0].shape[0] // 2
+        return jnp.concatenate([swap(near[1][:half], "seq", 1), swap(near[0][half:], "seq", 2)])
+
+    def columns(values, axis_name, j, width, start=0):
+        me = my_row if axis_name == "row" else my_seq
+        return lax.dynamic_slice_in_dim(values, start + (me ^ j) * width, width, 1)
+
+    def side_by_side(slots):
+        stack = jnp.stack(slots)
+        return jnp.concatenate([pick(stack, "seq", t) for t in range(seqs)], axis=1)
 
     def mine(values, width):
         return lax.dynamic_slice_in_dim(values, flat * width, width, values.ndim - 1)
@@ -733,14 +875,17 @@
     part = FF // (rows * seqs)
     x_own = frames[0]
 
-    x_all = jnp.concatenate(spread(x_own))
-    kv_split = w_cross_kv.reshape(w_cross_kv.shape[0], seqs, -1)
-    qkv_split = w_qkv.reshape(depth, 3, seqs, local_heads)
+    kv_width = 2 * D // seqs
     first_pieces = [
         jnp.concatenate(
-            [
-                pick(qkv_split, "seq", j, 2).reshape(depth, 3 * local_heads),
-                pick(kv_split, "seq", j, 1).reshape(depth, -1),
+            [columns(w_qkv, "seq", j, local_heads, k * D) for k in range(3)]
+            + [
+                jnp.concatenate(
+                    [
+                        columns(w_cross_kv, "seq", j, kv_width)[:, : kv_width // 2],
+                        columns(w_cross_kv, "seq", j, kv_width)[:, kv_width // 2 :],
+                    ]
+                )
             ],
             axis=1,
         )
@@ -749,34 +894,38 @@
     first_slots = [first_pieces[0]] + [swap(p, "seq", j) for j, p in enumerate(first_pieces) if j]
     first_w = natural(first_slots).reshape(seqs * depth, -1)
     first_w = lax.all_gather(first_w, "row", axis=0, tiled=True)
-    qkv_w = first_w[:, : 3 * local_heads]
-    kv_w = first_w[:, 3 * local_heads :].reshape(ctx_dim, -1)
-    wide_w = lax.all_gather(
-        jnp.concatenate([w_attn_out, w_cross_q, w_cross_out], axis=1), ("row", "seq"), axis=0, tiled=True
-    )
-    attn_w, crossq_w, crossout_w = wide_w[:, :D], wide_w[:, D : 2 * D], wide_w[:, 2 * D :]
-    glu_slots = exchange(w_glu.reshape(depth, 2, rows, seqs, part), 3)
-    glu_w = natural([s.reshape(depth, -1) for s in glu_slots]).reshape(seqs * depth, -1)
-    glu_w = lax.all_gather(glu_w, "row", axis=0, tiled=True)
-    down_w = lax.all_gather(w_down, "row", axis=0, tiled=True)
+    kv_w = first_w[:, 3 * local_heads :].reshape(rows * seqs, 2, depth // 2, -1)
+    kv_w = jnp.concatenate([kv_w[:, h].reshape(ctx_dim, -1) for h in range(2)], axis=1)
 
     features = time_features(timesteps.astype(jnp.float32)).astype(low)
     pre_part = dot(mine(features, w_time_in.shape[0]), w_time_in)
     gain_part = lax.dynamic_update_slice(
         jnp.zeros((1, D), jnp.float32), cross_gain.astype(jnp.float32)[None], (0, flat * depth)
     )
-    pre_hidden = sum_all(jnp.concatenate([pre_part, gain_part]))
+    pre_hidden = sum_over(after(jnp.concatenate([pre_part, gain_part]), *first_slots), "seq")
+    x_slots, near = spread_two(after(x_own, pre_hidden))
+    pre_hidden = sum_over(pre_hidden, "row")
     gain_values = pre_hidden[BUCKETS:]
     pre_hidden = pre_hidden[:BUCKETS]
     time_hidden = jax.nn.silu(pre_hidden).astype(low)
-    time_token = sum_all(dot(mine(time_hidden, depth), w_time_out))
+    time_token = sum_over(dot(mine(time_hidden, depth), w_time_out), "row")
+    if near is not None:
+        time_token, *near = lax.optimization_barrier((time_token, *near))
+        x_slots = [x_own, *near, opposite(near)]
+    time_token = sum_over(time_token, "seq")
     token_act = jax.nn.silu(time_token).astype(low)
     mod_part = dot(mine(token_act, depth), w_mod)
+    mod_part, *x_slots = lax.optimization_barrier((mod_part, *x_slots))
     row_part = lambda j: lax.dynamic_index_in_dim(mod_part, bucket_ids[my_row ^ j], 0)
     modulation = row_part(0)
     for j in range(1, rows):
         modulation = modulation + swap(row_part(j), "row", j)
     modulation = sum_over(modulation, "seq")
+    wide_w = lax.all_gather(
+        after(jnp.concatenate([w_attn_out, w_cross_q, w_cross_out], axis=1), time_token), ("row", "seq"), axis=0, tiled=True
+    )
+    attn_w, crossq_w, crossout_w = wide_w[:, :D], wide_w[:, D : 2 * D], wide_w[:, 2 * D :]
+
     shift_attn, scale_attn, gate_attn, shift_ffn, scale_ffn, gate_ffn = jnp.split(modulation, 6, axis=1)
 
     bounds = jnp.cumsum(seg_lengths[0])
@@ -795,12 +944,29 @@
     masks, tables = (query_mask, key_mask), (cosine, sine)
 
     pairs = local_heads // PAIR
-    attn_in, qkv = project(x_all, 1.0 + scale_attn, shift_attn, qkv_w, cosine, sine)
+    slots = lambda values: values.reshape(seqs, frames_here, -1)
+    attn_in, qkv = project(x_slots, 1.0 + scale_attn, shift_attn, first_w, 3 * local_heads, cosine, sine)
+    row_scale = lax.dynamic_index_in_dim(bucket_weights, bucket_ids[my_row], 0)
+    grad_out = cotangent[0].astype(jnp.float32) * row_scale
+    w_glu, w_down, grad_ffn_own, qkv = lax.optimization_barrier(
+        (w_glu, w_down, (gate_ffn * grad_out).astype(low), qkv)
+    )
+    glu_slots = exchange(split_units(w_glu, seqs, part))
+    down_lines = [w_down] + [swap(w_down, "row", 2 * j) for j in range(1, rows // 2)]
+    grad_ffn_slots, near = spread_two(grad_ffn_own)
     mixed_heads, lse = attend(qkv, qkv, qkv, 0, pairs, 2 * pairs, pairs, 512, masks)
-    slots = lambda values: values.reshape(seqs, frames_here, -1)
+    mixed_heads, *got = lax.optimization_barrier(
+        (mixed_heads, *grad_ffn_slots, *glu_slots, *down_lines)
+    )
+    grad_ffn_slots = got[: len(grad_ffn_slots)]
+    glu_slots, down_lines = got[len(grad_ffn_slots) : -len(down_lines)], got[-len(down_lines) :]
+    glu_w = lax.all_gather(natural(glu_slots).reshape(seqs * depth, -1), "row", axis=0, tiled=True)
+    down_other = swap(jnp.stack(down_lines), "row", 1)
+    down_w = [w for j in range(rows // 2) for w in (down_lines[j], down_other[j])]
+    down_w = jnp.concatenate(natural(down_w, "row"))
     mixed_slots = slots(mixed_heads)
     mixed_got = [mixed_slots[0]] + [swap(mixed_slots[j], "seq", j) for j in range(1, seqs)]
-    attn_mixed = natural(mixed_got).transpose(1, 0, 2).reshape(frames_here, D)
+    attn_mixed = side_by_side(mixed_got)
     attn_out = dot(attn_mixed, attn_w)
     inputs = x_own.astype(jnp.float32)
     after_attn = inputs + gate_attn * attn_out
@@ -809,77 +975,134 @@
     cross_in = (normed_c * gain_values).astype(low)
     cross_q = dot(cross_in, crossq_w).astype(low)
     kv_mine = dot(context[0], kv_w).astype(low)
-    cross_kv = natural(spread(kv_mine)).transpose(1, 0, 2).reshape(text_len, 2 * D)
+    cross_kv = side_by_side(spread(kv_mine))
     all_pairs = D // PAIR
     cross_mixed, cross_lse = attend(cross_q, cross_kv, cross_kv, 0, 0, all_pairs, all_pairs, frames_here)
     after_cross = after_attn + dot(cross_mixed, crossout_w)
 
     normed_f, inv_f = layer_stats(after_cross)
     ffn_in = (normed_f * (1.0 + scale_ffn) + shift_ffn).astype(low)
-    ffn_all = jnp.concatenate(spread(ffn_in))
     units = FF // seqs
-    gate_up = dot(ffn_all, glu_w)
-    gate_pre, up_pre = gate_up[:, :units], gate_up[:, units:]
-    gate_act = jax.nn.silu(gate_pre)
-    hidden = (gate_act * up_pre).astype(low)
-
-    def return_slots(values):
-        stack = slots(values.astype(low))
-        total = stack[0].astype(jnp.float32)
-        for j in range(1, seqs):
-            total = total + swap(stack[j], "seq", j).astype(jnp.float32)
-        return total
-
-    ffn_out = return_slots(dot(hidden, down_w))
-    result = (after_cross + gate_ffn * ffn_out).astype(low)
-
-    row_scale = lax.dynamic_index_in_dim(bucket_weights, bucket_ids[my_row], 0)
-    grad_out = cotangent[0].astype(jnp.float32) * row_scale
-    grad_ffn_all = jnp.concatenate(spread((gate_ffn * grad_out).astype(low)))
-    dgate_ffn = jnp.sum(grad_out * ffn_out, axis=0)
-    grad_hidden = dot_right_t(grad_ffn_all, down_w)
-    grad_gate_up = jnp.concatenate(
-        [grad_hidden * up_pre * silu_slope(gate_pre), grad_hidden * gate_act], axis=-1
-    ).astype(low)
-    grad_ffn_in = return_slots(dot_right_t(grad_gate_up, glu_w))
-    grad_glu = lax.psum_scatter(
-        dot_left_t(ffn_all, grad_gate_up).astype(low), "row", scatter_dimension=0, tiled=True
-    )
-    grad_down = lax.psum_scatter(
-        dot_left_t(hidden, grad_ffn_all).astype(low), "row", scatter_dimension=0, tiled=True
-    )
-    dshift_ffn = jnp.sum(grad_ffn_in, axis=0)
-    dscale_ffn = jnp.sum(grad_ffn_in * normed_f, axis=0)
+    ffn_slots, near = spread_two(ffn_in)
+    if near is not None:
+        ffn_slots.append(opposite(near))
+        grad_ffn_slots = lax.optimization_barrier((*grad_ffn_slots, ffn_in))[:-1]
+        grad_ffn_slots = [*grad_ffn_slots, opposite(grad_ffn_slots[1:])]
+    gate_up = [dot(values, glu_w) for values in ffn_slots]
+    gate_pre = [values[:, :units] for values in gate_up]
+    up_pre = [values[:, units:] for values in gate_up]
+    gate_act = [jax.nn.silu(values) for values in gate_pre]
+    hidden = [(a * u).astype(low) for a, u in zip(gate_act, up_pre)]
+
+    grad_hidden = [dot_right_t(values, down_w) for values in grad_ffn_slots]
+    grad_gate_up = [
+        jnp.concatenate([g * u * silu_slope(p), g * a], axis=-1).astype(low)
+        for g, u, p, a in zip(grad_hidden, up_pre, gate_pre, gate_act)
+    ]
+    far_first = list(range(seqs - 1, -1, -1))
+
+    def returned_near(parts):
+        if seqs != 4:
+            return [parts[0]] + [swap(parts[j], "seq", j) for j in range(1, seqs)]
+        half = frames_here // 2
+        return [
+            swap(parts[3][:half], "seq", 1),
+            swap(parts[3][half:], "seq", 2),
+            swap(parts[1][:half], "seq", 1),
+            swap(parts[2][half:], "seq", 2),
+        ]
+
+    def returned_far(parts, near):
+        if seqs != 4:
+            return near[1:], near[:1]
+        half = frames_here // 2
+        both = lambda left, right: left.astype(jnp.float32) + right.astype(jnp.float32)
+        far = [
+            swap(both(parts[2][:half], near[0]).astype(low), "seq", 2),
+            swap(both(parts[1][half:], near[1]).astype(low), "seq", 1),
+        ]
+        return far, [both(parts[0][:half], near[2]), both(parts[0][half:], near[3])]
+
+    def returned_total(far, near):
+        if seqs != 4:
+            return sum(term.astype(jnp.float32) for term in near + far)
+        return jnp.concatenate([n + f.astype(jnp.float32) for n, f in zip(near, far)])
+
+    ffn_back = {j: dot_right_t(grad_gate_up[j], glu_w).astype(low) for j in far_first}
+    ffn_back_near = returned_near(ffn_back)
+    ffn_all, hidden_all = jnp.concatenate(ffn_slots), jnp.concatenate(hidden)
+    grad_glu = dot_left_t(ffn_all, jnp.concatenate(grad_gate_up)).astype(low)
+    grad_down = dot_left_t(hidden_all, jnp.concatenate(grad_ffn_slots)).astype(low)
+    ffn_parts = [dot(values, down_w).astype(low) for values in hidden]
+    grad_glu, *ffn_back_near = lax.optimization_barrier((grad_glu, *ffn_back_near))
+    ffn_back_far = returned_far(ffn_back, ffn_back_near)
+    grad_ffn_in, grad_glu, grad_down, *ffn_parts = lax.optimization_barrier(
+        (returned_total(*ffn_back_far), grad_glu, grad_down, *ffn_parts)
+    )
+    grad_glu = lax.psum_scatter(grad_glu, "row", scatter_dimension=0, tiled=True)
+    grad_down = lax.psum_scatter(grad_down, "row", scatter_dimension=0, tiled=True)
+    ffn_near = returned_near(ffn_parts)
+    dshift_ffn = jnp.sum(grad_ffn_in, axis=0, keepdims=True)
+    dscale_ffn = jnp.sum(grad_ffn_in * normed_f, axis=0, keepdims=True)
     grad_cross = grad_out + norm_back(grad_ffn_in * (1.0 + scale_ffn), normed_f, inv_f)
 
     grad_cross_low = grad_cross.astype(low)
-    grad_crossout = dot_left_t(cross_mixed, grad_cross_low)
     grad_cmixed = dot_right_t(grad_cross_low, crossout_w).astype(low)
     grad_cquery, grad_ckey, grad_cvalue = attend_back(
         cross_q, cross_kv, cross_kv, grad_cmixed, cross_mixed, cross_lse,
         0, 0, all_pairs, all_pairs, frames_here, text_len,
     )
-    grad_ckv = jnp.concatenate([grad_ckey, grad_cvalue], axis=1).reshape(text_len, seqs, -1)
-    grad_ckv = sum(exchange(grad_ckv, 1))
-    grad_kv = jnp.einsum(
-        "cm,ce->me", context[0].astype(jnp.float32), grad_ckv, precision=highest
-    ).astype(low)
-    kv_got = exchange(grad_kv.reshape(rows, ctx_dim // rows, -1), 0, "row")
-    grad_kv = sum(g.astype(jnp.float32) for g in kv_got)
-    grad_kv = natural(exchange(grad_kv.reshape(seqs, ctx_dim // (rows * seqs), -1)))
-    grad_crosskv = grad_kv.transpose(1, 0, 2).reshape(ctx_dim // (rows * seqs), 2 * D)
-    grad_crossq = dot_left_t(cross_in, grad_cquery)
     grad_cross_in = dot_right_t(grad_cquery, crossq_w)
-    grad_gain = jnp.sum(grad_cross_in * normed_c, axis=0)
+    grad_gain = jnp.sum(grad_cross_in * normed_c, axis=0, keepdims=True)
     grad_attn = grad_cross + norm_back(grad_cross_in * gain_values, normed_c, inv_c)
 
     grad_attn_low = (gate_attn * grad_attn).astype(low)
-    dgate_attn = jnp.sum(grad_attn * attn_out, axis=0)
-    grad_attnout = dot_left_t(attn_mixed, grad_attn_low)
-    grad_wide = jnp.concatenate([grad_attnout, grad_crossq, grad_crossout], axis=1).astype(low)
-    grad_wide = lax.psum_scatter(grad_wide, ("row", "seq"), scatter_dimension=0, tiled=True)
+    dgate_attn = jnp.sum(grad_attn * attn_out, axis=0, keepdims=True)
     grad_amixed = dot_right_t(grad_attn_low, attn_w).astype(low)
-    grad_heads = jnp.concatenate(exchange(grad_amixed.reshape(frames_here, seqs, local_heads), 1))
+    grad_amixed, *ffn_near = lax.optimization_barrier((grad_amixed, *ffn_near))
+    head_pieces = [columns(grad_amixed, "seq", j, local_heads) for j in range(seqs)]
+    grad_heads = jnp.concatenate(
+        [head_pieces[0]] + [swap(p, "seq", j) for j, p in enumerate(head_pieces) if j]
+    )
+    cross_mixed, cross_in, attn_mixed, grad_ckey, grad_amixed = lax.optimization_barrier(
+        (cross_mixed, cross_in, attn_mixed, grad_ckey, grad_amixed)
+    )
+
+    core = my_row % 2
+    wide_own = [
+        dot_left_t(left, right).astype(low).reshape(rows // 2, 2, seqs, depth, D)
+        for left, right in (
+            (attn_mixed, grad_attn_low),
+            (cross_in, grad_cquery),
+            (cross_mixed, grad_cross_low),
+        )
+    ]
+    half_of = lambda g, c: lax.dynamic_index_in_dim(g, c, 1, keepdims=False)
+    wide_got = [swap(half_of(g, 1 - core), "row", 1) for g in wide_own]
+    ffn_out = returned_total(*returned_far(ffn_parts, ffn_near))
+
+    grad_ckv = jnp.concatenate([grad_ckey, grad_cvalue], axis=1)
+    ckv_pieces = [columns(grad_ckv, "seq", j, kv_width) for j in range(seqs)]
+    grad_ckv = ckv_pieces[0] + sum(swap(p, "seq", j) for j, p in enumerate(ckv_pieces) if j)
+    grad_kv = dot_left_t(context[0], grad_ckv.astype(low)).astype(low)
+    result = (after_cross + gate_ffn * ffn_out).astype(low)
+    dgate_ffn = jnp.sum(grad_out * ffn_out, axis=0, keepdims=True)
+    grad_heads, grad_kv, result, dgate_ffn, grad_glu, *wide_got = lax.optimization_barrier(
+        (grad_heads, grad_kv, result, dgate_ffn, grad_glu, *wide_got)
+    )
+    glu_got = exchange(grad_glu.reshape(seqs, depth, -1))
+    grad_kv = lax.psum_scatter(grad_kv, "row", scatter_dimension=0, tiled=True)
+    wide_both = [(half_of(own, core), got) for own, got in zip(wide_own, wide_got)]
+
+    def wide_piece(j):
+        both = [
+            pick(own, "seq", j, 1).astype(jnp.float32) + pick(got, "seq", j, 1).astype(jnp.float32)
+            for own, got in wide_both
+        ]
+        return jnp.stack(both, axis=1).astype(low)
+
+    wide_got = [wide_piece(j) for j in range(seqs)]
+    wide_got = [wide_got[0]] + [swap(piece, "seq", j) for j, piece in enumerate(wide_got) if j]
     grad_projected = jnp.concatenate(
         attend_back(
             qkv, qkv, qkv, grad_heads, mixed_heads, lse,
@@ -887,28 +1110,27 @@
         ),
         axis=1,
     )
-    grad_attn_in = return_slots(dot_right_t(grad_projected, qkv_w))
-    grad_qkv = lax.psum_scatter(
-        dot_left_t(attn_in, grad_projected).astype(low), "row", scatter_dimension=0, tiled=True
-    )
-    normed_a, inv_a = layer_stats(inputs)
-    dshift_attn = jnp.sum(grad_attn_in, axis=0)
-    dscale_attn = jnp.sum(grad_attn_in * normed_a, axis=0)
-    grad_frames = grad_attn + norm_back(grad_attn_in * (1.0 + scale_attn), normed_a, inv_a)
-
-    qkv_got = natural(exchange(grad_qkv.reshape(seqs, depth, -1)))
-    grad_qkv = qkv_got.reshape(seqs, depth, 3, local_heads).transpose(1, 2, 0, 3).reshape(depth, 3 * D)
-    glu_got = natural(exchange(grad_glu.reshape(seqs, depth, -1)))
-    grad_glu = (
-        glu_got.reshape(seqs, depth, 2, rows, part).transpose(1, 2, 3, 0, 4).reshape(depth, 2 * FF)
-    )
-
-    own_sums = sum_over(
-        jnp.stack(
-            [dshift_attn, dscale_attn, dgate_attn, dshift_ffn, dscale_ffn, dgate_ffn, grad_gain]
-        ),
-        "seq",
-    )
+    grad_projected, grad_down, grad_kv, *got = lax.optimization_barrier(
+        (grad_projected, grad_down, grad_kv, *glu_got, *wide_got)
+    )
+    glu_got, wide_got = got[:seqs], got[seqs:]
+    wide = sum(g.astype(jnp.float32) for g in wide_got).astype(low)
+    grad_wide = lax.psum_scatter(
+        wide,
+        "row",
+        scatter_dimension=0,
+        axis_index_groups=[list(range(c, rows, 2)) for c in range(2)],
+        tiled=True,
+    )[0].astype(jnp.float32)
+    grad_qkv = dot_left_t(attn_in, grad_projected).astype(low)
+    grad_projected, grad_qkv = lax.optimization_barrier((grad_projected, grad_qkv))
+    grad_qkv = lax.psum_scatter(grad_qkv, "row", scatter_dimension=0, tiled=True)
+    attn_back, attn_sums = project_back(grad_projected, first_w, x_slots)
+    own_sums = jnp.concatenate([attn_sums, dgate_attn, dshift_ffn, dscale_ffn, dgate_ffn, grad_gain])
+    own_sums = sum_over(own_sums, "seq")
+    attn_back = slots(after(attn_back, own_sums))
+    attn_near = returned_near(attn_back)
+
     bucket_list = jnp.arange(BUCKETS, dtype=jnp.int32)
     grad_mods = jnp.zeros((BUCKETS, 6 * D), jnp.float32)
     gain_total = jnp.zeros((D,), jnp.float32)
@@ -920,19 +1142,44 @@
     def outer(left, right):
         return sum(left[b][:, None] * right[b][None, :] for b in range(BUCKETS))
 
-    def gather_all(own):
-        across = natural(spread(own)).transpose(1, 0, 2).reshape(BUCKETS, -1)
-        return natural(spread(across, "row"), "row").transpose(1, 0, 2).reshape(BUCKETS, -1)
+    def gather_row(own):
+        return natural(spread(own, "row"), "row").transpose(1, 0, 2).reshape(BUCKETS, -1)
+
+    def gather_seq(own):
+        return natural(spread(own)).transpose(1, 0, 2).reshape(BUCKETS, -1)
 
     grad_modul = outer(mine(token_act, depth).astype(jnp.float32), grad_mods)
     token_own = jnp.dot(grad_mods, w_mod.astype(jnp.float32).T, precision=highest)
-    grad_token = gather_all(token_own * silu_slope(mine(time_token, depth)))
+    token_own = token_own * silu_slope(mine(time_token, depth))
+    token_own, *attn_near = lax.optimization_barrier((token_own, *attn_near))
+    token_seq = gather_seq(token_own)
+    token_seq, *attn_near = lax.optimization_barrier((token_seq, *attn_near))
+    attn_far, attn_own = returned_far(attn_back, attn_near)
+    grad_token = gather_row(token_seq)
     grad_timeout = outer(mine(time_hidden, depth).astype(jnp.float32), grad_token)
     hidden_own = jnp.dot(grad_token, w_time_out.astype(jnp.float32).T, precision=highest)
-    grad_pre = gather_all(hidden_own * silu_slope(mine(pre_hidden, depth)))
+    hidden_own = hidden_own * silu_slope(mine(pre_hidden, depth))
+    hidden_own, grad_qkv, *attn_far = lax.optimization_barrier((hidden_own, grad_qkv, *attn_far))
+    qkv_got = exchange(grad_qkv.reshape(seqs, depth, -1))
+    grad_attn_in = returned_total(attn_far, attn_own)
+    hidden_seq, *qkv_got = lax.optimization_barrier((gather_seq(hidden_own), *qkv_got))
+    grad_pre = gather_row(hidden_seq)
     grad_timein = outer(mine(features, w_time_in.shape[0]).astype(jnp.float32), grad_pre)
-
-    grad_wide = grad_wide.astype(jnp.float32)
+    normed_a, inv_a = layer_stats(inputs)
+    grad_frames = grad_attn + norm_back(grad_attn_in * (1.0 + scale_attn), normed_a, inv_a)
+
+    qkv_got = jnp.stack(qkv_got)
+    grad_qkv = jnp.concatenate(
+        [
+            pick(qkv_got, "seq", t)[:, k * local_heads : (k + 1) * local_heads]
+            for k in range(3)
+            for t in range(seqs)
+        ],
+        axis=1,
+    )
+    grad_glu = join_units(natural(glu_got), part)
+    grad_crosskv = side_by_side(exchange(grad_kv.reshape(seqs, ctx_dim // (rows * seqs), -1)))
+
     return (
         result[None],
         grad_frames[None],
@@ -940,12 +1187,12 @@
         grad_timeout,
         grad_modul,
         grad_qkv.astype(jnp.float32),
-        grad_wide[:, :D],
+        grad_wide[0],
         mine(gain_total, depth),
-        grad_wide[:, D : 2 * D],
-        grad_crosskv,
-        grad_wide[:, 2 * D :],
-        grad_glu.astype(jnp.float32),
+        grad_wide[1],
+        grad_crosskv.astype(jnp.float32),
+        grad_wide[2],
+        grad_glu,
         grad_down.astype(jnp.float32),
     )
 

time: 1280 us -> 971 us (0.76)
  waiting for transfers between devices: 523 us -> 198 us
  local copies, waits for them, and re-layouts: 122 us -> 103 us
  Pallas kernels: 162 us -> 180 us
  other arithmetic: 90.8 us -> 107 us
    ppermute x100 -> x115, waiting for transfers between devices: 455 us -> 198 us  [swap(): return lax.ppermute(value, axis, [(i, i ^ j) for i in range(sizes[axis])])]
    unnamed x9, waiting for transfers between devices: 68 us -> 0.13 us
    pallas_call x1 -> x4, Pallas kernels: 16.8 us -> 35 us  [the longest x1 17.4 us: project(): pl.pallas_call(functools.partial(project_kernel, per_slot), grid=(count /...]
    convert_element_type x3 -> x10, other arithmetic: 4.15 us -> 22.2 us  [the longest x3 6.92 us: returned_far(): both(parts[1][half:], near[1]).astype(low)]
    concatenate x8 -> x10, other arithmetic: 33.3 us -> 15.4 us  [the longest x2 5 us: side_by_side(): return jnp.concatenate([pick(stack, 'seq', t) for t in range(seqs)], axis=1)]
    another operation x2 -> x13, other arithmetic: 0.29 us -> 17.2 us
    convert_element_type x6 -> x0, local copies, waits for them, and re-layouts: 16.8 us -> none  [the longest x3 14.6 us: on_device_split(): grad_glu.astype(jnp.float32)]
    reshape x14 -> x3, local copies, waits for them, and re-layouts: 16.8 us -> 0.24 us  [the longest x2 0.16 us: gather_seq(): return natural(spread(own)).transpose(1, 0, 2).reshape(BUCKETS, -1)]
  transfers between devices with their start and end apart: 108 -> 123, of which waited for: 49 -> 46; matrix products, arithmetic and copies ran while one was open for 23% -> 41% of each run, Pallas kernels for 6% -> 19%
where the time goes in v2:
time: 971 us; the launch traced here: 962 us
  matrix products  216 us (22%)
  waiting for transfers between devices  198 us (20%)
  Pallas kernels  180 us (19%)
  starting transfers between devices  127 us (13%)
  other arithmetic  107 us (11%)
  local copies, waits for them, and re-layouts  103 us (11%)
  between operations  32.3 us (3%)
    ppermute x115, waiting for transfers between devices, swap(): return lax.ppermute(value, axis, [(i, i ^ j) for i in range(sizes[axis])])  198 us
    ppermute x115, starting transfers between devices, swap(): return lax.ppermute(value, axis, [(i, i ^ j) for i in range(sizes[axis])])  126 us
    pallas_call x2, Pallas kernels, attend_back(): pl.pallas_call(functools.partial(attend_back_kernel, masked, chunk), grid...  87.9 us
    dot_general x11, matrix products, dot_right_t(): jnp.einsum('fj,ij->fi', left, right, preferred_element_type=jnp.float32)  73.7 us
    dot_general x15, matrix products, dot(): return jnp.dot(left, right, preferred_element_type=jnp.float32)  71.5 us
    dot_general x7, matrix products, dot_left_t(): jnp.einsum('fi,fj->ij', left, right, preferred_element_type=jnp.float32)  67.9 us
    pallas_call x2, Pallas kernels, attend(): pl.pallas_call(functools.partial(attend_kernel, masked), grid=(pairs, cou...  56.8 us
    unnamed x353, local copies, waits for them, and re-layouts  40.5 us
  transfers between devices with their start and end apart: 123, of which 46 were waited for; matrix products, arithmetic and copies ran while one was open for 41% of the time, Pallas kernels for 19%

profile of v2, /device:TPU:0, one launch (start us, length us, event | category | flops | bytes accessed | tf_op | source)
XLA Modules:
  0.0 962.1 jit_solution(4893571209866485830)
XLA Ops:
  17.1 5.3 collective-permute-done.1
  24.9 3.4 collective-permute-done.3
  30.0 3.0 collective-permute-done.4
  38.1 6.6 collective-permute-done.6
  45.8 7.9 collective-permute-done.7
  55.3 8.0 collective-permute-done.9
  63.7 8.3 collective-permute-done.10
  104.4 15.1 %collective-permute-done.16 = bf16[256,1536]{1,0:T(8,128)(2,1)S(1)} collective-permute-done((bf16[256,1536]{1,0:T(8,128)(2,1)S(1)}, bf16[256,1536]{1,0:T(8,128)(2,1)S(1)}, u32[]{:S(2)}, u32[]{:S(2)}) %collective-permute-start.16) | collective-permute-done | bytes 786464 | tf_op jit(solution)/shard_map/ppermute | solution.py:803
  119.5 6.0 collective-permute-done.15
  127.7 3.4 collective-permute-start.22
  159.0 3.5 fusion.67
  163.7 17.4 %project.1 = (bf16[2048,1536]{1,0:T(8,128)(2,1)}, bf16[2048,1152]{1,0:T(8,128)(2,1)}) custom-call(bf16[512,1536]{1,0:T(8,128)(2,1)S(1)} %bitcast.364, bf16[512,1536]{1,0:T(8,128)(2,1)} %copy-done.12, bf16[512,1536]{1,0:T(8,128)(2,1)} %copy-done.71, bf16[512,1536]{1,0:T(8,128)(2,1)} %pad_maximum_fusion.8.refs_3_, f32[1,1536]{1,0:T(1,128)S(1)} %get-tuple-element.393.refs_4_, ...), custom_call_target="tpu_custom_call" | custom-call | flops 7247757312 | bytes 20840448 | tf_op jit(solution)/shard_map/project/pallas_call | solution.py:86
  188.4 3.3 collective-permute-done.28
  192.5 7.0 collective-permute-done.29
  203.1 46.7 %attend.2 = (bf16[2048,384]{1,0:T(8,128)(2,1)S(1)}, f32[3,2,2048]{2,1,0:T(2,128)S(1)}) custom-call(bf16[2048,1152]{1,0:T(8,128)(2,1)} %get-tuple-element.130.refs_0_.refs_1_.refs_2_, bf16[2048,1152]{1,0:T(8,128)(2,1)} %get-tuple-element.130.refs_0_.refs_1_.refs_2_, bf16[2048,1152]{1,0:T(8,128)(2,1)} %get-tuple-element.130.refs_0_.refs_1_.refs_2_, ...), custom_call_target="tpu_custom_call" | custom-call | flops 25769803776 | bytes 6291456 | tf_op jit(solution)/shard_map/attend/pallas_call | solution.py:201
  261.6 4.3 collective-permute-done.39
  266.0 3.8 collective-permute-done.38
  285.7 9.4 collective-permute-done.36
  295.1 7.2 collective-permute-done.35
  315.5 8.0 fusion.170
  326.7 5.0 fusion.88.refs_0_
  331.8 10.1 %attend.3 = (bf16[512,1536]{1,0:T(8,128)(2,1)S(1)}, f32[12,2,512]{2,1,0:T(2,128)S(1)}) custom-call(bf16[512,1536]{1,0:T(8,128)(2,1)S(1)} %fusion.88.refs_0_, bf16[128,3072]{1,0:T(8,128)(2,1)S(1)} %copy-done.6, bf16[128,3072]{1,0:T(8,128)(2,1)S(1)} %copy-done.6), custom_call_target="tpu_custom_call" | custom-call | flops 1610612736 | bytes 3932160 | tf_op jit(solution)/shard_map/attend/pallas_call | solution.py:201
  341.9 5.2 fusion.178
  357.5 8.2 fusion.179
  365.7 6.0 multiply_convert_fusion.12
  372.9 6.2 fusion.82
  382.4 6.1 convolution_convert_fusion.8
  388.6 15.3 %collective-permute-done.45 = bf16[256,1536]{1,0:T(8,128)(2,1)} collective-permute-done((bf16[256,1536]{1,0:T(8,128)(2,1)}, bf16[256,1536]{1,0:T(8,128)(2,1)}, u32[]{:S(2)}, u32[]{:S(2)}) %collective-permute-start.45) | collective-permute-done | bytes 786464 | tf_op jit(solution)/shard_map/ppermute | solution.py:803
  412.3 6.4 fusion.181
  418.8 7.3 multiply_convert_fusion.8
  426.1 6.4 fusion.180
  432.6 7.1 multiply_convert_fusion.10
  439.7 7.6 fusion.79
  449.1 5.1 fusion.76
  456.7 6.0 convolution_convert_fusion.7
  468.1 6.4 convolution_convert_fusion.6
  474.6 5.0 fusion.99
  479.6 8.1 multiply_convert_fusion.6
  487.7 7.0 fusion.73
  499.7 29.0 %fusion.16 = bf16[1536,3072]{1,0:T(8,128)(2,1)} fusion(bf16[2048,1536]{1,0:T(8,128)(2,1)} %constant_dynamic-update-slice_fusion.4, bf16[512,1536]{1,0:T(8,128)(2,1)} %get-tuple-element.262, bf16[512,1536]{1,0:T(8,128)(2,1)} %copy-done.141, bf16[512,1536]{1,0:T(8,128)(2,1)} %get-tuple-element.260, bf16[512,1536]{1,0:T(8,128)(2,1)} %get-tuple-element.259, ...), kind=kOutput, calls=%fused_computation.16 | convolution fusion | flops 19432734720 | bytes 28311552 | tf_op jit(solution)/shard_map/fi,fj->ij/dot_general | solution.py:868
  536.0 14.9 %convolution_convert_fusion.4 = bf16[1536,1536]{1,0:T(8,128)(2,1)} fusion(bf16[2048,1536]{1,0:T(8,128)(2,1)} %constant_dynamic-update-slice_fusion.9, bf16[512,1536]{1,0:T(8,128)(2,1)} %get-tuple-element.286, bf16[512,1536]{1,0:T(8,128)(2,1)S(1)} %copy-done.133, bf16[512,1536]{1,0:T(8,128)(2,1)S(1)} %copy-done.135, bf16[512,1536]{1,0:T(8,128)(2,1)S(1)} %copy-done.131), kind=kOutput, calls=%fused_computation.21 | convolution fusion | flops 9691201536 | bytes 17301504 | tf_op jit(solution)/shard_map/fi,fj->ij/dot_general | solution.py:868
  551.0 6.7 convolution_convert_fusion.5
  576.8 7.3 fusion.91.refs_3_
  584.1 12.2 %attend_back.2 = (bf16[512,1536]{1,0:T(8,128)(2,1)S(1)}, f32[128,1536]{1,0:T(8,128)S(1)}, f32[128,1536]{1,0:T(8,128)S(1)}) custom-call(bf16[512,1536]{1,0:T(8,128)(2,1)} %copy-done.16, bf16[128,3072]{1,0:T(8,128)(2,1)S(1)} %copy-done.7, bf16[128,3072]{1,0:T(8,128)(2,1)S(1)} %copy-done.7, bf16[512,1536]{1,0:T(8,128)(2,1)} %fusion.91.refs_3_, ...), custom_call_target="tpu_custom_call" | custom-call | flops 4026531840 | bytes 7864320 | tf_op jit(solution)/shard_map/attend_back/pallas_call | solution.py:298
  596.4 5.9 multiply_reduce_fusion
  603.9 6.2 fusion.85
  616.1 3.0 convolution_convert_fusion.3
  626.0 3.3 convolution_convert_fusion.1
  633.5 6.0 collective-permute-done.62
  647.9 13.0 %collective-permute-done.63 = bf16[256,1536]{1,0:T(8,128)(2,1)S(1)} collective-permute-done((bf16[256,1536]{1,0:T(8,128)(2,1)S(1)}, bf16[256,1536]{1,0:T(8,128)(2,1)S(1)}, u32[]{:S(2)}, u32[]{:S(2)}) %collective-permute-start.63) | collective-permute-done | bytes 786464 | tf_op jit(solution)/shard_map/ppermute | solution.py:803
  683.8 3.0 fusion.110
  686.8 5.6 fusion.108
  700.1 75.7 %attend_back.3 = (bf16[2048,384]{1,0:T(8,128)(2,1)}, bf16[2048,384]{1,0:T(8,128)(2,1)}, bf16[2048,384]{1,0:T(8,128)(2,1)}) custom-call(bf16[2048,1152]{1,0:T(8,128)(2,1)} %get-tuple-element.130.refs_0_.refs_1_.refs_2_, bf16[2048,1152]{1,0:T(8,128)(2,1)} %get-tuple-element.130.refs_0_.refs_1_.refs_2_, ...), custom_call_target="tpu_custom_call" | custom-call | flops 64424509440 | bytes 12582912 | tf_op jit(solution)/shard_map/attend_back/pallas_call | solution.py:298
  777.4 4.0 pad_maximum_fusion.refs_4_
  784.0 5.5 add_convert_fusion
  789.6 13.4 %convolution_convert_fusion = bf16[1536,1152]{1,0:T(8,128)(2,1)} fusion(bf16[2048,1536]{1,0:T(8,128)(2,1)} %get-tuple-element.189, bf16[2048,1152]{1,0:T(8,128)(2,1)} %pad_maximum_fusion.refs_4_), kind=kOutput, calls=%fused_computation.17 | convolution fusion | flops 7249526784 | bytes 14548992 | tf_op jit(solution)/shard_map/fi,fj->ij/dot_general | solution.py:868
  804.4 15.6 %project_back.1 = (bf16[2048,1536]{1,0:T(8,128)(2,1)}, f32[2,1536]{1,0:T(2,128)S(1)}) custom-call(bf16[512,1536]{1,0:T(8,128)(2,1)S(1)} %bitcast.365, bf16[512,1536]{1,0:T(8,128)(2,1)S(1)} %copy-done.13, bf16[512,1536]{1,0:T(8,128)(2,1)} %copy-done.71, bf16[512,1536]{1,0:T(8,128)(2,1)} %pad_maximum_fusion.8.refs_3_, ...), custom_call_target="tpu_custom_call" | custom-call | flops 7247757312 | bytes 20840448 | tf_op jit(solution)/shard_map/project_back/pallas_call | solution.py:133
  830.3 3.1 collective-permute-done.75
  836.8 3.6 collective-permute-start.79
  842.7 3.6 fusion.171
  869.3 14.2 %collective-permute-done.85 = bf16[256,1536]{1,0:T(8,128)(2,1)} collective-permute-done((bf16[256,1536]{1,0:T(8,128)(2,1)}, bf16[256,1536]{1,0:T(8,128)(2,1)}, u32[]{:S(2)}, u32[]{:S(2)}) %collective-permute-start.85) | collective-permute-done | bytes 786464 | tf_op jit(solution)/shard_map/ppermute | solution.py:803
  893.3 3.1 add_convert_fusion.3
  910.0 12.2 %collective-permute-done.97 = bf16[256,1536]{1,0:T(8,128)(2,1)S(1)} collective-permute-done((bf16[256,1536]{1,0:T(8,128)(2,1)}, bf16[256,1536]{1,0:T(8,128)(2,1)S(1)}, u32[]{:S(2)}, u32[]{:S(2)}) %collective-permute-start.97) | collective-permute-done | bytes 786464 | tf_op jit(solution)/shard_map/ppermute | solution.py:803
  937.2 4.2 collective-permute-done.104
  (807 shorter events, 343.3 us)
Async XLA Ops:
  7.2 155.3 %all-gather.4.cloned.1.call-start = ((), (), s32[]{:S(2)}) async-start(), calls=%async_computation.5 | async-start | bytes 5308416 | tf_op jit(solution)/shard_map/all_gather | solution.py:896
  23.5 292.0 %all-gather.6.cloned.1.call-start = ((), (), s32[]{:S(2)}) async-start(), calls=%async_computation.6 | async-start | bytes 14598144 | tf_op jit(solution)/shard_map/all_gather | solution.py:924
  33.0 39.0 %collective-permute-start.11 = (bf16[512,1536]{1,0:T(8,128)(2,1)S(1)}, bf16[512,1536]{1,0:T(8,128)(2,1)S(1)}, u32[]{:S(2)}, u32[]{:S(2)}) collective-permute-start(bf16[512,1536]{1,0:T(8,128)(2,1)S(1)} %bitcast.362), channel_id=1, source_target_pairs={{0,1},{1,0},{2,3},{3,2},{4,5},{5,4},{6,7},{7,6},{8,9},{9,8},{10,11... | collective-permute-start | bytes 4718600 | tf_op jit(solution)/shard_map/ppermute | solution.py:803
  33.5 38.5 %collective-permute-start.12 = (bf16[512,1536]{1,0:T(8,128)(2,1)S(1)}, bf16[512,1536]{1,0:T(8,128)(2,1)S(1)}, u32[]{:S(2)}, u32[]{:S(2)}) collective-permute-start(bf16[512,1536]{1,0:T(8,128)(2,1)S(1)} %bitcast.363), channel_id=1, source_target_pairs={{0,2},{1,3},{2,0},{3,1},{4,6},{5,7},{6,4},{7,5},{8,10},{9,11},{10,... | collective-permute-start | bytes 4718600 | tf_op jit(solution)/shard_map/ppermute | solution.py:803
  82.0 275.4 %all-gather.8.cloned.1.call-start = ((), (), s32[]{:S(2)}) async-start(), calls=%async_computation.7 | async-start | bytes 10616832 | tf_op jit(solution)/shard_map/all_gather | solution.py:963
  98.1 21.5 %collective-permute-start.16 = (bf16[256,1536]{1,0:T(8,128)(2,1)S(1)}, bf16[256,1536]{1,0:T(8,128)(2,1)S(1)}, u32[]{:S(2)}, u32[]{:S(2)}) collective-permute-start(bf16[256,1536]{1,0:T(8,128)(2,1)S(1)} %slice.422), channel_id=1, source_target_pairs={{0,2},{1,3},{2,0},{3,1},{4,6},{5,7},{6,4},{7,5},{8,10},{9,11},{10,... | collective-permute-start | bytes 2359304 | tf_op jit(solution)/shard_map/ppermute | solution.py:803
  100.8 24.7 %collective-permute-start.15 = (bf16[256,1536]{1,0:T(8,128)(2,1)S(1)}, bf16[256,1536]{1,0:T(8,128)(2,1)S(1)}, u32[]{:S(2)}, u32[]{:S(2)}) collective-permute-start(bf16[256,1536]{1,0:T(8,128)(2,1)S(1)} %slice.421), channel_id=1, source_target_pairs={{0,1},{1,0},{2,3},{3,2},{4,5},{5,4},{6,7},{7,6},{8,9},{9,8},{10,11... | collective-permute-start | bytes 2359304 | tf_op jit(solution)/shard_map/ppermute | solution.py:803
  183.3 16.3 %collective-permute-start.29 = (bf16[48,3072]{1,0:T(8,128)(2,1)S(1)}, bf16[48,3072]{1,0:T(8,128)(2,1)S(1)}, u32[]{:S(2)}, u32[]{:S(2)}) collective-permute-start(bf16[48,3072]{1,0:T(8,128)(2,1)S(1)} %get-tuple-element.328), channel_id=1, source_target_pairs={{0,2},{1,3},{2,0},{3,1},{4,6},{5,7},{6,4},{7,5},{8,10},{9,11},{10,... | collective-permute-start | bytes 884744 | tf_op jit(solution)/shard_map/ppermute | solution.py:803
  184.5 17.6 %collective-permute-start.30 = (bf16[48,3072]{1,0:T(8,128)(2,1)S(1)}, bf16[48,3072]{1,0:T(8,128)(2,1)S(1)}, u32[]{:S(2)}, u32[]{:S(2)}) collective-permute-start(bf16[48,3072]{1,0:T(8,128)(2,1)S(1)} %get-tuple-element.327), channel_id=1, source_target_pairs={{0,3},{1,2},{2,1},{3,0},{4,7},{5,6},{6,5},{7,4},{8,11},{9,10},{10,... | collective-permute-start | bytes 884744 | tf_op jit(solution)/shard_map/ppermute | solution.py:803
  185.5 64.4 %collective-permute-start.26 = (bf16[512,1536]{1,0:T(8,128)(2,1)S(1)}, bf16[512,1536]{1,0:T(8,128)(2,1)S(1)}, u32[]{:S(2)}, u32[]{:S(2)}) collective-permute-start(bf16[512,1536]{1,0:T(8,128)(2,1)S(1)} %copy-done.30), channel_id=1, source_target_pairs={{0,1},{1,0},{2,3},{3,2},{4,5},{5,4},{6,7},{7,6},{8,9},{9,8},{10,11... | collective-permute-start | bytes 4718600 | tf_op jit(solution)/shard_map/ppermute | solution.py:803
  187.2 62.8 %collective-permute-start.27 = (bf16[512,1536]{1,0:T(8,128)(2,1)S(1)}, bf16[512,1536]{1,0:T(8,128)(2,1)S(1)}, u32[]{:S(2)}, u32[]{:S(2)}) collective-permute-start(bf16[512,1536]{1,0:T(8,128)(2,1)S(1)} %copy-done.30), channel_id=1, source_target_pairs={{0,2},{1,3},{2,0},{3,1},{4,6},{5,7},{6,4},{7,5},{8,10},{9,11},{10,... | collective-permute-start | bytes 4718600 | tf_op jit(solution)/shard_map/ppermute | solution.py:803
  191.6 58.2 %collective-permute-start.31 = (bf16[192,1536]{1,0:T(8,128)(2,1)S(1)}, bf16[192,1536]{1,0:T(8,128)(2,1)S(1)}, u32[]{:S(2)}, u32[]{:S(2)}) collective-permute-start(bf16[192,1536]{1,0:T(8,128)(2,1)S(1)} %copy-done.43), channel_id=1, source_target_pairs={{0,8},{4,12},{8,0},{12,4},{16,24},{20,28},{24,16},{28,20},{1,9},{5... | collective-permute-start | bytes 1769480 | tf_op jit(solution)/shard_map/ppermute | solution.py:803
  199.5 50.4 %collective-permute-start.32 = (bf16[192,1536]{1,0:T(8,128)(2,1)S(1)}, bf16[192,1536]{1,0:T(8,128)(2,1)S(1)}, u32[]{:S(2)}, u32[]{:S(2)}) collective-permute-start(bf16[192,1536]{1,0:T(8,128)(2,1)S(1)} %copy-done.43), channel_id=1, source_target_pairs={{0,16},{4,20},{8,24},{12,28},{16,0},{20,4},{24,8},{28,12},{1,17},{... | collective-permute-start | bytes 1769480 | tf_op jit(solution)/shard_map/ppermute | solution.py:803
  202.1 47.9 %collective-permute-start.33 = (bf16[192,1536]{1,0:T(8,128)(2,1)S(1)}, bf16[192,1536]{1,0:T(8,128)(2,1)S(1)}, u32[]{:S(2)}, u32[]{:S(2)}) collective-permute-start(bf16[192,1536]{1,0:T(8,128)(2,1)S(1)} %copy-done.43), channel_id=1, source_target_pairs={{0,24},{4,28},{8,16},{12,20},{16,8},{20,12},{24,0},{28,4},{1,25},{... | collective-permute-start | bytes 1769480 | tf_op jit(solution)/shard_map/ppermute | solution.py:803
  253.0 413.2 %reduce-scatter.8.cloned.1.call-start = ((), (), s32[]{:S(2)}) async-start(), calls=%async_computation.8 | async-start | bytes 10616832 | tf_op jit(solution)/shard_map/reduce_scatter | solution.py:1042
  256.6 47.2 %collective-permute-start.40 = (bf16[4,192,1536]{2,1,0:T(8,128)(2,1)}, bf16[4,192,1536]{2,1,0:T(8,128)(2,1)}, u32[]{:S(2)}, u32[]{:S(2)}) collective-permute-start(bf16[4,192,1536]{2,1,0:T(8,128)(2,1)} %pad_maximum_fusion.3), channel_id=1, source_target_pairs={{0,4},{4,0},{8,12},{12,8},{16,20},{20,16},{24,28},{28,24},{1,5},{5... | collective-permute-start | bytes 7077896 | tf_op jit(solution)/shard_map/ppermute | solution.py:803
  282.1 13.0 %collective-permute-start.36 = (bf16[512,384]{1,0:T(8,128)(2,1)S(1)}, bf16[512,384]{1,0:T(8,128)(2,1)S(1)}, u32[]{:S(2)}, u32[]{:S(2)}) collective-permute-start(bf16[512,384]{1,0:T(8,128)(2,1)S(1)} %get-tuple-element.310), channel_id=1, source_target_pairs={{0,3},{1,2},{2,1},{3,0},{4,7},{5,6},{6,5},{7,4},{8,11},{9,10},{10,... | collective-permute-start | bytes 1179656 | tf_op jit(solution)/shard_map/ppermute | solution.py:803
  283.1 19.3 %collective-permute-start.35 = (bf16[512,384]{1,0:T(8,128)(2,1)S(1)}, bf16[512,384]{1,0:T(8,128)(2,1)S(1)}, u32[]{:S(2)}, u32[]{:S(2)}) collective-permute-start(bf16[512,384]{1,0:T(8,128)(2,1)S(1)} %get-tuple-element.311), channel_id=1, source_target_pairs={{0,2},{1,3},{2,0},{3,1},{4,6},{5,7},{6,4},{7,5},{8,10},{9,11},{10,... | collective-permute-start | bytes 1179656 | tf_op jit(solution)/shard_map/ppermute | solution.py:803
  283.8 18.5 %collective-permute-start.34 = (bf16[512,384]{1,0:T(8,128)(2,1)S(1)}, bf16[512,384]{1,0:T(8,128)(2,1)S(1)}, u32[]{:S(2)}, u32[]{:S(2)}) collective-permute-start(bf16[512,384]{1,0:T(8,128)(2,1)S(1)} %get-tuple-element.312), channel_id=1, source_target_pairs={{0,1},{1,0},{2,3},{3,2},{4,5},{5,4},{6,7},{7,6},{8,9},{9,8},{10,11... | collective-permute-start | bytes 1179656 | tf_op jit(solution)/shard_map/ppermute | solution.py:803
  350.2 59.6 %collective-permute-start.41 = (bf16[512,1536]{1,0:T(8,128)(2,1)}, bf16[512,1536]{1,0:T(8,128)(2,1)}, u32[]{:S(2)}, u32[]{:S(2)}) collective-permute-start(bf16[512,1536]{1,0:T(8,128)(2,1)} %get-tuple-element.252), channel_id=1, source_target_pairs={{0,1},{1,0},{2,3},{3,2},{4,5},{5,4},{6,7},{7,6},{8,9},{9,8},{10,11... | collective-permute-start | bytes 4718600 | tf_op jit(solution)/shard_map/ppermute | solution.py:803
  350.7 57.3 %collective-permute-start.42 = (bf16[512,1536]{1,0:T(8,128)(2,1)}, bf16[512,1536]{1,0:T(8,128)(2,1)}, u32[]{:S(2)}, u32[]{:S(2)}) collective-permute-start(bf16[512,1536]{1,0:T(8,128)(2,1)} %get-tuple-element.252), channel_id=1, source_target_pairs={{0,2},{1,3},{2,0},{3,1},{4,6},{5,7},{6,4},{7,5},{8,10},{9,11},{10,... | collective-permute-start | bytes 4718600 | tf_op jit(solution)/shard_map/ppermute | solution.py:803
  353.0 53.0 %collective-permute-start.46 = (bf16[256,1536]{1,0:T(8,128)(2,1)}, bf16[256,1536]{1,0:T(8,128)(2,1)}, u32[]{:S(2)}, u32[]{:S(2)}) collective-permute-start(bf16[256,1536]{1,0:T(8,128)(2,1)} %slice.449), channel_id=1, source_target_pairs={{0,2},{1,3},{2,0},{3,1},{4,6},{5,7},{6,4},{7,5},{8,10},{9,11},{10,... | collective-permute-start | bytes 2359304 | tf_op jit(solution)/shard_map/ppermute | solution.py:803
  354.6 49.3 %collective-permute-start.45 = (bf16[256,1536]{1,0:T(8,128)(2,1)}, bf16[256,1536]{1,0:T(8,128)(2,1)}, u32[]{:S(2)}, u32[]{:S(2)}) collective-permute-start(bf16[256,1536]{1,0:T(8,128)(2,1)} %slice.448), channel_id=1, source_target_pairs={{0,1},{1,0},{2,3},{3,2},{4,5},{5,4},{6,7},{7,6},{8,9},{9,8},{10,11... | collective-permute-start | bytes 2359304 | tf_op jit(solution)/shard_map/ppermute | solution.py:803
  409.2 65.3 %collective-permute-start.43 = (bf16[256,1536]{1,0:T(8,128)(2,1)S(1)}, bf16[256,1536]{1,0:T(8,128)(2,1)S(1)}, u32[]{:S(2)}, u32[]{:S(2)}) collective-permute-start(bf16[256,1536]{1,0:T(8,128)(2,1)S(1)} %slice.551), channel_id=1, source_target_pairs={{0,1},{1,0},{2,3},{3,2},{4,5},{5,4},{6,7},{7,6},{8,9},{9,8},{10,11... | collective-permute-start | bytes 2359304 | tf_op jit(solution)/shard_map/ppermute | solution.py:803
  411.0 63.6 %collective-permute-start.44 = (bf16[256,1536]{1,0:T(8,128)(2,1)S(1)}, bf16[256,1536]{1,0:T(8,128)(2,1)S(1)}, u32[]{:S(2)}, u32[]{:S(2)}) collective-permute-start(bf16[256,1536]{1,0:T(8,128)(2,1)S(1)} %slice.552), channel_id=1, source_target_pairs={{0,2},{1,3},{2,0},{3,1},{4,6},{5,7},{6,4},{7,5},{8,10},{9,11},{10,... | collective-permute-start | bytes 2359304 | tf_op jit(solution)/shard_map/ppermute | solution.py:803
  448.3 80.4 %collective-permute-start.49 = (bf16[256,1536]{1,0:T(8,128)(2,1)}, bf16[256,1536]{1,0:T(8,128)(2,1)}, u32[]{:S(2)}, u32[]{:S(2)}) collective-permute-start(bf16[256,1536]{1,0:T(8,128)(2,1)} %slice.561), channel_id=1, source_target_pairs={{0,1},{1,0},{2,3},{3,2},{4,5},{5,4},{6,7},{7,6},{8,9},{9,8},{10,11... | collective-permute-start | bytes 2359304 | tf_op jit(solution)/shard_map/ppermute | solution.py:803
  455.2 73.4 %collective-permute-start.50 = (bf16[256,1536]{1,0:T(8,128)(2,1)}, bf16[256,1536]{1,0:T(8,128)(2,1)}, u32[]{:S(2)}, u32[]{:S(2)}) collective-permute-start(bf16[256,1536]{1,0:T(8,128)(2,1)} %slice.562), channel_id=1, source_target_pairs={{0,2},{1,3},{2,0},{3,1},{4,6},{5,7},{6,4},{7,5},{8,10},{9,11},{10,... | collective-permute-start | bytes 2359304 | tf_op jit(solution)/shard_map/ppermute | solution.py:803
  496.0 32.7 %collective-permute-start.47 = (bf16[256,1536]{1,0:T(8,128)(2,1)}, bf16[256,1536]{1,0:T(8,128)(2,1)}, u32[]{:S(2)}, u32[]{:S(2)}) collective-permute-start(bf16[256,1536]{1,0:T(8,128)(2,1)} %get-tuple-element.304), channel_id=1, source_target_pairs={{0,1},{1,0},{2,3},{3,2},{4,5},{5,4},{6,7},{7,6},{8,9},{9,8},{10,11... | collective-permute-start | bytes 2359304 | tf_op jit(solution)/shard_map/ppermute | solution.py:803
  496.4 32.2 %collective-permute-start.48 = (bf16[256,1536]{1,0:T(8,128)(2,1)}, bf16[256,1536]{1,0:T(8,128)(2,1)}, u32[]{:S(2)}, u32[]{:S(2)}) collective-permute-start(bf16[256,1536]{1,0:T(8,128)(2,1)} %get-tuple-element.303), channel_id=1, source_target_pairs={{0,2},{1,3},{2,0},{3,1},{4,6},{5,7},{6,4},{7,5},{8,10},{9,11},{10,... | collective-permute-start | bytes 2359304 | tf_op jit(solution)/shard_map/ppermute | solution.py:803
  531.3 26.4 %collective-permute-start.51 = (bf16[256,1536]{1,0:T(8,128)(2,1)}, bf16[256,1536]{1,0:T(8,128)(2,1)}, u32[]{:S(2)}, u32[]{:S(2)}) collective-permute-start(bf16[256,1536]{1,0:T(8,128)(2,1)} %add_convert_fusion.8), channel_id=1, source_target_pairs={{0,2},{1,3},{2,0},{3,1},{4,6},{5,7},{6,4},{7,5},{8,10},{9,11},{10,... | collective-permute-start | bytes 2359304 | tf_op jit(solution)/shard_map/ppermute | solution.py:803
  534.5 23.2 %collective-permute-start.52 = (bf16[256,1536]{1,0:T(8,128)(2,1)}, bf16[256,1536]{1,0:T(8,128)(2,1)}, u32[]{:S(2)}, u32[]{:S(2)}) collective-permute-start(bf16[256,1536]{1,0:T(8,128)(2,1)} %add_convert_fusion.7), channel_id=1, source_target_pairs={{0,1},{1,0},{2,3},{3,2},{4,5},{5,4},{6,7},{7,6},{8,9},{9,8},{10,11... | collective-permute-start | bytes 2359304 | tf_op jit(solution)/shard_map/ppermute | solution.py:803
  561.9 221.0 %reduce-scatter.16.cloned.1.call-start = ((), (), s32[]{:S(2)}) async-start(), calls=%async_computation.12 | async-start | bytes 1327104
  566.0 44.0 %collective-permute-start.53 = (bf16[256,1536]{1,0:T(8,128)(2,1)}, bf16[256,1536]{1,0:T(8,128)(2,1)}, u32[]{:S(2)}, u32[]{:S(2)}) collective-permute-start(bf16[256,1536]{1,0:T(8,128)(2,1)} %get-tuple-element.300), channel_id=1, source_target_pairs={{0,1},{1,0},{2,3},{3,2},{4,5},{5,4},{6,7},{7,6},{8,9},{9,8},{10,11... | collective-permute-start | bytes 2359304 | tf_op jit(solution)/shard_map/ppermute | solution.py:803
  566.5 43.5 %collective-permute-start.54 = (bf16[256,1536]{1,0:T(8,128)(2,1)}, bf16[256,1536]{1,0:T(8,128)(2,1)}, u32[]{:S(2)}, u32[]{:S(2)}) collective-permute-start(bf16[256,1536]{1,0:T(8,128)(2,1)} %get-tuple-element.299), channel_id=1, source_target_pairs={{0,2},{1,3},{2,0},{3,1},{4,6},{5,7},{6,4},{7,5},{8,10},{9,11},{10,... | collective-permute-start | bytes 2359304 | tf_op jit(solution)/shard_map/ppermute | solution.py:803
  567.8 42.2 %collective-permute-start.55 = (bf16[256,1536]{1,0:T(8,128)(2,1)S(1)}, bf16[256,1536]{1,0:T(8,128)(2,1)}, u32[]{:S(2)}, u32[]{:S(2)}) collective-permute-start(bf16[256,1536]{1,0:T(8,128)(2,1)S(1)} %slice.461), channel_id=1, source_target_pairs={{0,1},{1,0},{2,3},{3,2},{4,5},{5,4},{6,7},{7,6},{8,9},{9,8},{10,11... | collective-permute-start | bytes 2359304 | tf_op jit(solution)/shard_map/ppermute | solution.py:803
  570.8 39.2 %collective-permute-start.56 = (bf16[256,1536]{1,0:T(8,128)(2,1)}, bf16[256,1536]{1,0:T(8,128)(2,1)}, u32[]{:S(2)}, u32[]{:S(2)}) collective-permute-start(bf16[256,1536]{1,0:T(8,128)(2,1)} %slice.462), channel_id=1, source_target_pairs={{0,2},{1,3},{2,0},{3,1},{4,6},{5,7},{6,4},{7,5},{8,10},{9,11},{10,... | collective-permute-start | bytes 2359304 | tf_op jit(solution)/shard_map/ppermute | solution.py:803
  610.3 21.2 %collective-permute-start.59 = (bf16[512,384]{1,0:T(8,128)(2,1)S(1)}, bf16[512,384]{1,0:T(8,128)(2,1)S(1)}, u32[]{:S(2)}, u32[]{:S(2)}) collective-permute-start(bf16[512,384]{1,0:T(8,128)(2,1)S(1)} %get-tuple-element.296), channel_id=1, source_target_pairs={{0,3},{1,2},{2,1},{3,0},{4,7},{5,6},{6,5},{7,4},{8,11},{9,10},{10,... | collective-permute-start | bytes 1179656 | tf_op jit(solution)/shard_map/ppermute | solution.py:803
  611.4 21.6 %collective-permute-start.58 = (bf16[512,384]{1,0:T(8,128)(2,1)S(1)}, bf16[512,384]{1,0:T(8,128)(2,1)S(1)}, u32[]{:S(2)}, u32[]{:S(2)}) collective-permute-start(bf16[512,384]{1,0:T(8,128)(2,1)S(1)} %get-tuple-element.297), channel_id=1, source_target_pairs={{0,2},{1,3},{2,0},{3,1},{4,6},{5,7},{6,4},{7,5},{8,10},{9,11},{10,... | collective-permute-start | bytes 1179656 | tf_op jit(solution)/shard_map/ppermute | solution.py:803
  612.3 20.7 %collective-permute-start.57 = (bf16[512,384]{1,0:T(8,128)(2,1)S(1)}, bf16[512,384]{1,0:T(8,128)(2,1)S(1)}, u32[]{:S(2)}, u32[]{:S(2)}) collective-permute-start(bf16[512,384]{1,0:T(8,128)(2,1)S(1)} %get-tuple-element.298), channel_id=1, source_target_pairs={{0,1},{1,0},{2,3},{3,2},{4,5},{5,4},{6,7},{7,6},{8,9},{9,8},{10,11... | collective-permute-start | bytes 1179656 | tf_op jit(solution)/shard_map/ppermute | solution.py:803
  614.0 25.5 %collective-permute-start.62 = (f32[128,768]{1,0:T(8,128)S(1)}, f32[128,768]{1,0:T(8,128)S(1)}, u32[]{:S(2)}, u32[]{:S(2)}) collective-permute-start(f32[128,768]{1,0:T(8,128)S(1)} %get-tuple-element.293), channel_id=1, source_target_pairs={{0,3},{1,2},{2,1},{3,0},{4,7},{5,6},{6,5},{7,4},{8,11},{9,10},{10,... | collective-permute-start | bytes 1179656 | tf_op jit(solution)/shard_map/ppermute | solution.py:803
  615.2 28.0 %collective-permute-start.60 = (f32[128,768]{1,0:T(8,128)S(1)}, f32[128,768]{1,0:T(8,128)S(1)}, u32[]{:S(2)}, u32[]{:S(2)}) collective-permute-start(f32[128,768]{1,0:T(8,128)S(1)} %get-tuple-element.294), channel_id=1, source_target_pairs={{0,1},{1,0},{2,3},{3,2},{4,5},{5,4},{6,7},{7,6},{8,9},{9,8},{10,11... | collective-permute-start | bytes 1179656 | tf_op jit(solution)/shard_map/ppermute | solution.py:803
  631.5 12.7 %collective-permute-start.61 = (f32[128,768]{1,0:T(8,128)S(1)}, f32[128,768]{1,0:T(8,128)S(1)}, u32[]{:S(2)}, u32[]{:S(2)}) collective-permute-start(f32[128,768]{1,0:T(8,128)S(1)} %get-tuple-element.292), channel_id=1, source_target_pairs={{0,2},{1,3},{2,0},{3,1},{4,6},{5,7},{6,4},{7,5},{8,10},{9,11},{10,... | collective-permute-start | bytes 1179656 | tf_op jit(solution)/shard_map/ppermute | solution.py:803
  633.0 33.2 %collective-permute-start.65 = (bf16[4,4,48,1536]{3,2,1,0:T(8,128)(2,1)S(1)}, bf16[4,4,48,1536]{3,2,1,0:T(8,128)(2,1)}, u32[]{:S(2)}, u32[]{:S(2)}) collective-permute-start(bf16[4,4,48,1536]{3,2,1,0:T(8,128)(2,1)S(1)} %dynamic-slice_bitcast_fusion.2), channel_id=1, source_target_pairs={{0,4},{4,0},{8,12},{12,8},{16,20},{20,16},{24,28},{28,24},{1,5},{5... | collective-permute-start | bytes 7077896 | tf_op jit(solution)/shard_map/ppermute | solution.py:803
  633.0 33.2 %collective-permute-start.66 = (bf16[4,4,48,1536]{3,2,1,0:T(8,128)(2,1)S(1)}, bf16[4,4,48,1536]{3,2,1,0:T(8,128)(2,1)}, u32[]{:S(2)}, u32[]{:S(2)}) collective-permute-start(bf16[4,4,48,1536]{3,2,1,0:T(8,128)(2,1)S(1)} %dynamic-slice_bitcast_fusion.1), channel_id=1, source_target_pairs={{0,4},{4,0},{8,12},{12,8},{16,20},{20,16},{24,28},{28,24},{1,5},{5... | collective-permute-start | bytes 7077896 | tf_op jit(solution)/shard_map/ppermute | solution.py:803
  639.5 26.7 %collective-permute-start.67 = (bf16[4,4,48,1536]{3,2,1,0:T(8,128)(2,1)S(1)}, bf16[4,4,48,1536]{3,2,1,0:T(8,128)(2,1)}, u32[]{:S(2)}, u32[]{:S(2)}) collective-permute-start(bf16[4,4,48,1536]{3,2,1,0:T(8,128)(2,1)S(1)} %dynamic-slice_bitcast_fusion), channel_id=1, source_target_pairs={{0,4},{4,0},{8,12},{12,8},{16,20},{20,16},{24,28},{28,24},{1,5},{5... | collective-permute-start | bytes 7077896 | tf_op jit(solution)/shard_map/ppermute | solution.py:803
  643.2 17.7 %collective-permute-start.63 = (bf16[256,1536]{1,0:T(8,128)(2,1)S(1)}, bf16[256,1536]{1,0:T(8,128)(2,1)S(1)}, u32[]{:S(2)}, u32[]{:S(2)}) collective-permute-start(bf16[256,1536]{1,0:T(8,128)(2,1)S(1)} %add_convert_fusion.6), channel_id=1, source_target_pairs={{0,2},{1,3},{2,0},{3,1},{4,6},{5,7},{6,4},{7,5},{8,10},{9,11},{10,... | collective-permute-start | bytes 2359304 | tf_op jit(solution)/shard_map/ppermute | solution.py:803
  644.2 17.4 %collective-permute-start.64 = (bf16[256,1536]{1,0:T(8,128)(2,1)S(1)}, bf16[256,1536]{1,0:T(8,128)(2,1)S(1)}, u32[]{:S(2)}, u32[]{:S(2)}) collective-permute-start(bf16[256,1536]{1,0:T(8,128)(2,1)S(1)} %add_convert_fusion.5), channel_id=1, source_target_pairs={{0,1},{1,0},{2,3},{3,2},{4,5},{5,4},{6,7},{7,6},{8,9},{9,8},{10,11... | collective-permute-start | bytes 2359304 | tf_op jit(solution)/shard_map/ppermute | solution.py:803
  668.7 115.3 %reduce-scatter.10.cloned.1.call-start = ((), (), s32[]{:S(2)}) async-start(), calls=%async_computation.9 | async-start | bytes 5308416 | tf_op jit(solution)/shard_map/reduce_scatter | solution.py:1043
  677.4 230.5 %reduce-scatter.14.cloned.1.call-start = ((), (), s32[]{:S(2)}) async-start(), calls=%async_computation.11 | async-start | bytes 2211840 | tf_op jit(solution)/shard_map/reduce_scatter | solution.py:1118
  681.8 94.0 %collective-permute-start.68 = (bf16[48,3072]{1,0:T(8,128)(2,1)S(1)}, bf16[48,3072]{1,0:T(8,128)(2,1)S(1)}, u32[]{:S(2)}, u32[]{:S(2)}) collective-permute-start(bf16[48,3072]{1,0:T(8,128)(2,1)S(1)} %get-tuple-element.319), channel_id=1, source_target_pairs={{0,1},{1,0},{2,3},{3,2},{4,5},{5,4},{6,7},{7,6},{8,9},{9,8},{10,11... | collective-permute-start | bytes 884744 | tf_op jit(solution)/shard_map/ppermute | solution.py:803
  682.5 101.4 %collective-permute-start.69 = (bf16[48,3072]{1,0:T(8,128)(2,1)}, bf16[48,3072]{1,0:T(8,128)(2,1)}, u32[]{:S(2)}, u32[]{:S(2)}) collective-permute-start(bf16[48,3072]{1,0:T(8,128)(2,1)} %get-tuple-element.318), channel_id=1, source_target_pairs={{0,2},{1,3},{2,0},{3,1},{4,6},{5,7},{6,4},{7,5},{8,10},{9,11},{10,... | collective-permute-start | bytes 884744 | tf_op jit(solution)/shard_map/ppermute | solution.py:803
  693.8 90.2 %collective-permute-start.71 = (bf16[4,3,48,1536]{3,2,1,0:T(8,128)(2,1)}, bf16[4,3,48,1536]{3,2,1,0:T(8,128)(2,1)}, u32[]{:S(2)}, u32[]{:S(2)}) collective-permute-start(bf16[4,3,48,1536]{3,2,1,0:T(8,128)(2,1)} %pad_maximum_fusion.5), channel_id=1, source_target_pairs={{0,1},{1,0},{2,3},{3,2},{4,5},{5,4},{6,7},{7,6},{8,9},{9,8},{10,11... | collective-permute-start | bytes 5308424 | tf_op jit(solution)/shard_map/ppermute | solution.py:803
  696.4 87.6 %collective-permute-start.72 = (bf16[4,3,48,1536]{3,2,1,0:T(8,128)(2,1)}, bf16[4,3,48,1536]{3,2,1,0:T(8,128)(2,1)}, u32[]{:S(2)}, u32[]{:S(2)}) collective-permute-start(bf16[4,3,48,1536]{3,2,1,0:T(8,128)(2,1)} %pad_maximum_fusion.6), channel_id=1, source_target_pairs={{0,2},{1,3},{2,0},{3,1},{4,6},{5,7},{6,4},{7,5},{8,10},{9,11},{10,... | collective-permute-start | bytes 5308424 | tf_op jit(solution)/shard_map/ppermute | solution.py:803
  698.7 85.3 %collective-permute-start.73 = (bf16[4,3,48,1536]{3,2,1,0:T(8,128)(2,1)}, bf16[4,3,48,1536]{3,2,1,0:T(8,128)(2,1)}, u32[]{:S(2)}, u32[]{:S(2)}) collective-permute-start(bf16[4,3,48,1536]{3,2,1,0:T(8,128)(2,1)} %pad_maximum_fusion.7), channel_id=1, source_target_pairs={{0,3},{1,2},{2,1},{3,0},{4,7},{5,6},{6,5},{7,4},{8,11},{9,10},{10,... | collective-permute-start | bytes 5308424 | tf_op jit(solution)/shard_map/ppermute | solution.py:803
  789.5 133.9 %reduce-scatter.12.cloned.1.call-start = ((), (), s32[]{:S(2)}) async-start(), calls=%async_computation.10 | async-start | bytes 3981312 | tf_op jit(solution)/shard_map/reduce_scatter | solution.py:1127
  846.4 20.6 %collective-permute-start.83 = (bf16[256,1536]{1,0:T(8,128)(2,1)}, bf16[256,1536]{1,0:T(8,128)(2,1)S(1)}, u32[]{:S(2)}, u32[]{:S(2)}) collective-permute-start(bf16[256,1536]{1,0:T(8,128)(2,1)} %get-tuple-element.282), channel_id=1, source_target_pairs={{0,1},{1,0},{2,3},{3,2},{4,5},{5,4},{6,7},{7,6},{8,9},{9,8},{10,11... | collective-permute-start | bytes 2359304 | tf_op jit(solution)/shard_map/ppermute | solution.py:803
  848.6 20.8 %collective-permute-start.84 = (bf16[256,1536]{1,0:T(8,128)(2,1)}, bf16[256,1536]{1,0:T(8,128)(2,1)}, u32[]{:S(2)}, u32[]{:S(2)}) collective-permute-start(bf16[256,1536]{1,0:T(8,128)(2,1)} %get-tuple-element.281), channel_id=1, source_target_pairs={{0,2},{1,3},{2,0},{3,1},{4,6},{5,7},{6,4},{7,5},{8,10},{9,11},{10,... | collective-permute-start | bytes 2359304 | tf_op jit(solution)/shard_map/ppermute | solution.py:803
  849.2 34.3 %collective-permute-start.85 = (bf16[256,1536]{1,0:T(8,128)(2,1)}, bf16[256,1536]{1,0:T(8,128)(2,1)}, u32[]{:S(2)}, u32[]{:S(2)}) collective-permute-start(bf16[256,1536]{1,0:T(8,128)(2,1)} %get-tuple-element.280), channel_id=1, source_target_pairs={{0,1},{1,0},{2,3},{3,2},{4,5},{5,4},{6,7},{7,6},{8,9},{9,8},{10,11... | collective-permute-start | bytes 2359304 | tf_op jit(solution)/shard_map/ppermute | solution.py:803
  851.4 33.6 %collective-permute-start.86 = (bf16[256,1536]{1,0:T(8,128)(2,1)}, bf16[256,1536]{1,0:T(8,128)(2,1)}, u32[]{:S(2)}, u32[]{:S(2)}) collective-permute-start(bf16[256,1536]{1,0:T(8,128)(2,1)} %get-tuple-element.279), channel_id=1, source_target_pairs={{0,2},{1,3},{2,0},{3,1},{4,6},{5,7},{6,4},{7,5},{8,10},{9,11},{10,... | collective-permute-start | bytes 2359304 | tf_op jit(solution)/shard_map/ppermute | solution.py:803
  890.8 12.2 %collective-permute-start.93 = (f32[5,192]{1,0:T(8,128)S(1)}, f32[5,192]{1,0:T(8,128)S(1)}, u32[]{:S(2)}, u32[]{:S(2)}) collective-permute-start(f32[5,192]{1,0:T(8,128)S(1)} %reshape.536), channel_id=1, source_target_pairs={{0,16},{4,20},{8,24},{12,28},{16,0},{20,4},{24,8},{28,12},{1,17},{... | collective-permute-start | bytes 11528 | tf_op jit(solution)/shard_map/ppermute | solution.py:803
  901.6 20.6 %collective-permute-start.97 = (bf16[256,1536]{1,0:T(8,128)(2,1)}, bf16[256,1536]{1,0:T(8,128)(2,1)S(1)}, u32[]{:S(2)}, u32[]{:S(2)}) collective-permute-start(bf16[256,1536]{1,0:T(8,128)(2,1)} %get-tuple-element.278), channel_id=1, source_target_pairs={{0,2},{1,3},{2,0},{3,1},{4,6},{5,7},{6,4},{7,5},{8,10},{9,11},{10,... | collective-permute-start | bytes 2359304 | tf_op jit(solution)/shard_map/ppermute | solution.py:803
  903.0 20.4 %collective-permute-start.98 = (bf16[256,1536]{1,0:T(8,128)(2,1)}, bf16[256,1536]{1,0:T(8,128)(2,1)}, u32[]{:S(2)}, u32[]{:S(2)}) collective-permute-start(bf16[256,1536]{1,0:T(8,128)(2,1)} %get-tuple-element.277), channel_id=1, source_target_pairs={{0,1},{1,0},{2,3},{3,2},{4,5},{5,4},{6,7},{7,6},{8,9},{9,8},{10,11... | collective-permute-start | bytes 2359304 | tf_op jit(solution)/shard_map/ppermute | solution.py:803
  923.4 12.3 %collective-permute-start.101 = (f32[5,48]{1,0:T(8,128)S(1)}, f32[5,48]{1,0:T(8,128)S(1)}, u32[]{:S(2)}, u32[]{:S(2)}) collective-permute-start(f32[5,48]{1,0:T(8,128)S(1)} %convolution_multiply_fusion), channel_id=1, source_target_pairs={{0,3},{1,2},{2,1},{3,0},{4,7},{5,6},{6,5},{7,4},{8,11},{9,10},{10,... | collective-permute-start | bytes 2888 | tf_op jit(solution)/shard_map/ppermute | solution.py:803
  925.0 12.0 %collective-permute-start.100 = (f32[5,48]{1,0:T(8,128)S(1)}, f32[5,48]{1,0:T(8,128)S(1)}, u32[]{:S(2)}, u32[]{:S(2)}) collective-permute-start(f32[5,48]{1,0:T(8,128)S(1)} %convolution_multiply_fusion), channel_id=1, source_target_pairs={{0,2},{1,3},{2,0},{3,1},{4,6},{5,7},{6,4},{7,5},{8,10},{9,11},{10,... | collective-permute-start | bytes 2888 | tf_op jit(solution)/shard_map/ppermute | solution.py:803
  (205 other events, 2682.2 us)
Sparse Core Ops, SparseCore 0:
  23.6 56.0 all-gather.3
  82.6 111.6 all-gather.5
  253.1 90.2 all-gather.7
  562.0 98.6 reduce-scatter.7
  668.8 31.4 reduce-scatter.15
  702.5 53.1 reduce-scatter.9
  789.6 37.0 reduce-scatter.13
  829.3 48.7 reduce-scatter.11

commit v3 on v2

--- a/solution.py
+++ b/solution.py
@@ -47,13 +47,21 @@
     return center * lax.rsqrt(jnp.mean(center * center, axis=-1, keepdims=True) + 1e-05)
 
 
+def joined(blocks):
+    return blocks.reshape(blocks.shape[0] * blocks.shape[1], blocks.shape[2])
+
+
+def gathered_spec(w, part, rows, width, **kwargs):
+    return pl.BlockSpec((w.shape[0], rows, width), lambda i: (0, part, 0), **kwargs)
+
+
 def project_kernel(per_slot, *refs):
     x_refs, (scale_ref, shift_ref, w_ref, cos_ref, sin_ref, in_ref, out_ref) = refs[:-7], refs[-7:]
 
     def run(x_ref):
         modulated = (norm_block(x_ref) * scale_ref[...] + shift_ref[...]).astype(bf16)
         in_ref[...] = modulated
-        projected = dot_nn(modulated, w_ref[...])
+        projected = dot_nn(modulated, joined(w_ref[...]))
         cosine = cos_ref[...]
         sine = sin_ref[...]
         width = out_ref.shape[1]
@@ -90,7 +98,7 @@
         + [
             whole(scale),
             whole(shift),
-            pl.BlockSpec((depth, width), lambda i: (0, 0)),
+            gathered_spec(w, 0, depth // w.shape[0], width),
             row_spec(PAIR),
             row_spec(PAIR),
         ],
@@ -117,7 +125,7 @@
         sums_ref[...] = jnp.zeros_like(sums_ref)
 
     def run(x_ref):
-        part = dot_nt(grad_ref[...], w_ref[...])
+        part = dot_nt(grad_ref[...], joined(w_ref[...]))
         out_ref[...] = part.astype(bf16)
         sums_ref[0:1, :] += jnp.sum(part, axis=0, keepdims=True)
         sums_ref[1:2, :] += jnp.sum(part * norm_block(x_ref), axis=0, keepdims=True)
@@ -136,7 +144,7 @@
         in_specs=x_specs
         + [
             pl.BlockSpec((block, width), lambda i: (i, 0)),
-            pl.BlockSpec((depth, width), lambda i: (0, 0)),
+            gathered_spec(w, 0, depth // w.shape[0], width),
         ],
         out_specs=[
             pl.BlockSpec((block, depth), lambda i: (i, 0)),
@@ -361,6 +369,145 @@
     )(stack)
 
 
+def feed_kernel(per_slot, slots, chunk, chained, *refs):
+    x_refs, g_refs = refs[:slots], refs[slots : 2 * slots]
+    gate_ref, scale_ref, glu_ref, down_ref = refs[2 * slots : 2 * slots + 4]
+    outs = refs[2 * slots + 4 + (4 if chained else 0) :]
+    x_out, g_out, hidden_ref, grads_ref, back_ref, out_ref, dgate_ref, back_sum, out_sum = outs
+    blocks, block_units = down_ref.shape[:2]
+    units = blocks * block_units
+    taken = chunk // block_units
+
+    def run(x_ref, g_ref):
+        x = x_ref[...]
+        grad_out = g_ref[...].astype(f32) * scale_ref[...]
+        g = (gate_ref[...] * grad_out).astype(bf16)
+        x_out[...] = x
+        g_out[...] = g
+        for start in range(0, units, chunk):
+            gate_cols, up_cols = slice(start, start + chunk), slice(units + start, units + start + chunk)
+            gate = dot_nn(x, glu_ref[:, gate_cols])
+            up = dot_nn(x, glu_ref[:, up_cols])
+            down = joined(down_ref[start // block_units : start // block_units + taken])
+            grad_hidden = dot_nt(g, down)
+            opened = 1.0 / (1.0 + jnp.exp(-gate))
+            act = gate * opened
+            hidden = (act * up).astype(bf16)
+            grad_gate = (grad_hidden * up * (opened * (1.0 + gate * (1.0 - opened)))).astype(bf16)
+            grad_up = (grad_hidden * act).astype(bf16)
+            hidden_ref[:, gate_cols] = hidden
+            grads_ref[:, gate_cols] = grad_gate
+            grads_ref[:, up_cols] = grad_up
+            back = dot_nt(grad_gate, glu_ref[:, gate_cols]) + dot_nt(grad_up, glu_ref[:, up_cols])
+            out = dot_nn(hidden, down)
+            if start == 0:
+                back_sum[...] = back
+                out_sum[...] = out
+            else:
+                back_sum[...] += back
+                out_sum[...] += out
+        back_ref[...] = back_sum[...].astype(bf16)
+        out_ref[...] = out_sum[...].astype(bf16)
+        dgate_ref[...] += jnp.sum(grad_out * out_sum[...], axis=0, keepdims=True)
+
+    @pl.when(pl.program_id(0) == 0)
+    def _():
+        dgate_ref[...] = jnp.zeros_like(dgate_ref)
+
+    for slot in range(slots):
+        pl.when(pl.program_id(0) // per_slot == slot)(functools.partial(run, x_refs[slot], g_refs[slot]))
+
+
+def feed(x_slots, g_slots, gate, scale, glu, down, first, total, kept=None, block=256):
+    per_slot, x_specs = slot_specs(x_slots, block)
+    slots, (frames, depth) = len(x_slots), x_slots[0].shape
+    count, units = slots * frames, glu.shape[1] // 2
+    chunk = units // 2
+    own_units = units // down.shape[0]
+    offset = first * per_slot
+    own_rows = lambda cols: pl.BlockSpec((block, cols), lambda i: (i, 0))
+    all_rows = lambda cols: pl.BlockSpec((block, cols), lambda i: (i + offset, 0))
+    whole = lambda a: pl.BlockSpec(a.shape, lambda i: (0, 0), pipeline_mode=pl.Buffered(1))
+    everywhere = [depth, depth, units, 2 * units]
+    return pl.pallas_call(
+        functools.partial(feed_kernel, per_slot, slots, chunk, kept is not None),
+        grid=(count // block,),
+        in_specs=x_specs
+        + slot_specs(g_slots, block)[1]
+        + [
+            whole(gate),
+            whole(scale),
+            whole(glu),
+            gathered_spec(
+                down, down.shape[1] // own_units - 1, own_units, depth, pipeline_mode=pl.Buffered(1)
+            ),
+        ]
+        + [pl.BlockSpec(memory_space=pl.ANY)] * (4 if kept is not None else 0),
+        out_specs=[all_rows(cols) for cols in everywhere] + [own_rows(depth), own_rows(depth), pl.BlockSpec((1, depth), lambda i: (0, 0))],
+        out_shape=[jax.ShapeDtypeStruct((total * frames, cols), bf16) for cols in everywhere]
+        + [jax.ShapeDtypeStruct((count, depth), bf16)] * 2
+        + [jax.ShapeDtypeStruct((1, depth), f32)],
+        scratch_shapes=[pltpu.VMEM((block, depth), f32), pltpu.VMEM((block, depth), f32)],
+        input_output_aliases={2 * slots + 4 + k: k for k in range(4)} if kept is not None else {},
+        compiler_params=pltpu.CompilerParams(vmem_limit_bytes=VMEM),
+        cost_estimate=pl.CostEstimate(
+            flops=12 * count * depth * units,
+            bytes_accessed=2 * (3 * depth * units + count * (6 * depth + 3 * units)),
+            transcendentals=count * units,
+        ),
+        name="feed",
+    )(*x_slots, *g_slots, gate, scale, glu, down, *(kept or ()))
+
+
+def outer_kernel(left_ref, right_ref, out_ref):
+    left = left_ref[...].T
+    height = out_ref.shape[0]
+    total = left[:height, 0:1] * right_ref[0:1, :]
+    for b in range(1, right_ref.shape[0]):
+        total += left[:height, b : b + 1] * right_ref[b : b + 1, :]
+    out_ref[...] = total
+
+
+def outer(left, right):
+    buckets, height = left.shape
+    width = right.shape[1]
+    left = jnp.pad(left.astype(f32), ((0, -buckets % 8), (0, -height % 128)))
+    return pl.pallas_call(
+        outer_kernel,
+        out_shape=jax.ShapeDtypeStruct((height, width), f32),
+        compiler_params=pltpu.CompilerParams(vmem_limit_bytes=VMEM),
+        cost_estimate=pl.CostEstimate(
+            flops=2 * buckets * height * width, bytes_accessed=4 * height * width, transcendentals=0
+        ),
+        name="outer",
+    )(left, right)
+
+
+def text_product_kernel(left_ref, right_ref, out_ref):
+    left = left_ref[...].astype(f32).T.astype(bf16)
+    out_ref[...] = dot_nn(left, right_ref[...]).astype(bf16)
+
+
+def text_product(left, right, block=1024):
+    tokens, height = left.shape
+    width = right.shape[1]
+    return pl.pallas_call(
+        text_product_kernel,
+        grid=(width // block,),
+        in_specs=[
+            pl.BlockSpec((tokens, height), lambda i: (0, 0)),
+            pl.BlockSpec((tokens, block), lambda i: (0, i)),
+        ],
+        out_specs=pl.BlockSpec((height, block), lambda i: (0, i)),
+        out_shape=jax.ShapeDtypeStruct((height, width), bf16),
+        compiler_params=pltpu.CompilerParams(vmem_limit_bytes=VMEM),
+        cost_estimate=pl.CostEstimate(
+            flops=2 * tokens * height * width, bytes_accessed=2 * height * width, transcendentals=0
+        ),
+        name="text_product",
+    )(left, right)
+
+
 highest = lax.Precision.HIGHEST
 
 
@@ -795,6 +942,9 @@
     cotangent,
 ):
     my_row = lax.axis_index("row")
+    row_order = my_row ^ jnp.arange(rows, dtype=jnp.int32)
+    hits = jnp.arange(BUCKETS, dtype=jnp.int32)[:, None] == bucket_ids[row_order][None, :]
+    hits = hits.astype(jnp.float32)
     my_seq = lax.axis_index("seq")
     flat = my_row * seqs + my_seq
     sizes = {"row": rows, "seq": seqs}
@@ -846,6 +996,11 @@
     def opposite(near):
         half = near[0].shape[0] // 2
         return jnp.concatenate([swap(near[1][:half], "seq", 1), swap(near[0][half:], "seq", 2)])
+
+    def spread_row(value):
+        both = jnp.stack([value, swap(value, "row", 1)])
+        lines = [both] + [swap(both, "row", 2 * j) for j in range(1, rows // 2)]
+        return [line[c] for line in lines for c in range(2)]
 
     def columns(values, axis_name, j, width, start=0):
         me = my_row if axis_name == "row" else my_seq
@@ -893,8 +1048,9 @@
     ]
     first_slots = [first_pieces[0]] + [swap(p, "seq", j) for j, p in enumerate(first_pieces) if j]
     first_w = natural(first_slots).reshape(seqs * depth, -1)
-    first_w = lax.all_gather(first_w, "row", axis=0, tiled=True)
-    kv_w = first_w[:, 3 * local_heads :].reshape(rows * seqs, 2, depth // 2, -1)
+    first_w = jnp.concatenate([first_w, w_down])
+    first_w = lax.all_gather(first_w, "row", axis=0, tiled=True).reshape(rows, -1, D)
+    kv_w = first_w[:, : seqs * depth, 3 * local_heads :].reshape(rows * seqs, 2, depth // 2, -1)
     kv_w = jnp.concatenate([kv_w[:, h].reshape(ctx_dim, -1) for h in range(2)], axis=1)
 
     features = time_features(timesteps.astype(jnp.float32)).astype(low)
@@ -911,21 +1067,22 @@
     time_token = sum_over(dot(mine(time_hidden, depth), w_time_out), "row")
     if near is not None:
         time_token, *near = lax.optimization_barrier((time_token, *near))
+    wide_w = jnp.concatenate([w_attn_out, w_cross_q, w_cross_out], axis=1)
+    wide_w = lax.all_gather(after(wide_w, time_token), ("row", "seq"), axis=0, tiled=True)
+    attn_w, crossq_w, crossout_w = wide_w[:, :D], wide_w[:, D : 2 * D], wide_w[:, 2 * D :]
+    time_token = sum_over(time_token, "seq")
+    if near is not None:
+        time_token, *near = lax.optimization_barrier((time_token, *near))
         x_slots = [x_own, *near, opposite(near)]
-    time_token = sum_over(time_token, "seq")
     token_act = jax.nn.silu(time_token).astype(low)
     mod_part = dot(mine(token_act, depth), w_mod)
     mod_part, *x_slots = lax.optimization_barrier((mod_part, *x_slots))
+    glu_slots = exchange(split_units(after(w_glu, x_slots[-1]), seqs, part))
     row_part = lambda j: lax.dynamic_index_in_dim(mod_part, bucket_ids[my_row ^ j], 0)
     modulation = row_part(0)
     for j in range(1, rows):
         modulation = modulation + swap(row_part(j), "row", j)
     modulation = sum_over(modulation, "seq")
-    wide_w = lax.all_gather(
-        after(jnp.concatenate([w_attn_out, w_cross_q, w_cross_out], axis=1), time_token), ("row", "seq"), axis=0, tiled=True
-    )
-    attn_w, crossq_w, crossout_w = wide_w[:, :D], wide_w[:, D : 2 * D], wide_w[:, 2 * D :]
-
     shift_attn, scale_attn, gate_attn, shift_ffn, scale_ffn, gate_ffn = jnp.split(modulation, 6, axis=1)
 
     bounds = jnp.cumsum(seg_lengths[0])
@@ -948,34 +1105,23 @@
     attn_in, qkv = project(x_slots, 1.0 + scale_attn, shift_attn, first_w, 3 * local_heads, cosine, sine)
     row_scale = lax.dynamic_index_in_dim(bucket_weights, bucket_ids[my_row], 0)
     grad_out = cotangent[0].astype(jnp.float32) * row_scale
-    w_glu, w_down, grad_ffn_own, qkv = lax.optimization_barrier(
-        (w_glu, w_down, (gate_ffn * grad_out).astype(low), qkv)
-    )
-    glu_slots = exchange(split_units(w_glu, seqs, part))
-    down_lines = [w_down] + [swap(w_down, "row", 2 * j) for j in range(1, rows // 2)]
-    grad_ffn_slots, near = spread_two(grad_ffn_own)
+    kv_slots = spread(dot(context[0], kv_w).astype(low))
+    qkv, *got = lax.optimization_barrier((qkv, *kv_slots, *glu_slots))
+    kv_slots, glu_slots = got[:seqs], got[seqs:]
+    glu_w = lax.all_gather(natural(glu_slots).reshape(seqs * depth, -1), "row", axis=0, tiled=True)
     mixed_heads, lse = attend(qkv, qkv, qkv, 0, pairs, 2 * pairs, pairs, 512, masks)
-    mixed_heads, *got = lax.optimization_barrier(
-        (mixed_heads, *grad_ffn_slots, *glu_slots, *down_lines)
-    )
-    grad_ffn_slots = got[: len(grad_ffn_slots)]
-    glu_slots, down_lines = got[len(grad_ffn_slots) : -len(down_lines)], got[-len(down_lines) :]
-    glu_w = lax.all_gather(natural(glu_slots).reshape(seqs * depth, -1), "row", axis=0, tiled=True)
-    down_other = swap(jnp.stack(down_lines), "row", 1)
-    down_w = [w for j in range(rows // 2) for w in (down_lines[j], down_other[j])]
-    down_w = jnp.concatenate(natural(down_w, "row"))
     mixed_slots = slots(mixed_heads)
     mixed_got = [mixed_slots[0]] + [swap(mixed_slots[j], "seq", j) for j in range(1, seqs)]
     attn_mixed = side_by_side(mixed_got)
     attn_out = dot(attn_mixed, attn_w)
+    cot_slots, _ = spread_two(after(cotangent[0], attn_out))
     inputs = x_own.astype(jnp.float32)
     after_attn = inputs + gate_attn * attn_out
 
     normed_c, inv_c = layer_stats(after_attn)
     cross_in = (normed_c * gain_values).astype(low)
     cross_q = dot(cross_in, crossq_w).astype(low)
-    kv_mine = dot(context[0], kv_w).astype(low)
-    cross_kv = side_by_side(spread(kv_mine))
+    cross_kv = side_by_side(kv_slots)
     all_pairs = D // PAIR
     cross_mixed, cross_lse = attend(cross_q, cross_kv, cross_kv, 0, 0, all_pairs, all_pairs, frames_here)
     after_cross = after_attn + dot(cross_mixed, crossout_w)
@@ -984,22 +1130,22 @@
     ffn_in = (normed_f * (1.0 + scale_ffn) + shift_ffn).astype(low)
     units = FF // seqs
     ffn_slots, near = spread_two(ffn_in)
-    if near is not None:
-        ffn_slots.append(opposite(near))
-        grad_ffn_slots = lax.optimization_barrier((*grad_ffn_slots, ffn_in))[:-1]
-        grad_ffn_slots = [*grad_ffn_slots, opposite(grad_ffn_slots[1:])]
-    gate_up = [dot(values, glu_w) for values in ffn_slots]
-    gate_pre = [values[:, :units] for values in gate_up]
-    up_pre = [values[:, units:] for values in gate_up]
-    gate_act = [jax.nn.silu(values) for values in gate_pre]
-    hidden = [(a * u).astype(low) for a, u in zip(gate_act, up_pre)]
-
-    grad_hidden = [dot_right_t(values, down_w) for values in grad_ffn_slots]
-    grad_gate_up = [
-        jnp.concatenate([g * u * silu_slope(p), g * a], axis=-1).astype(low)
-        for g, u, p, a in zip(grad_hidden, up_pre, gate_pre, gate_act)
-    ]
-    far_first = list(range(seqs - 1, -1, -1))
+    calls = [slice(0, 1), slice(1, 3), slice(3, 4)] if seqs == 4 else [slice(0, seqs)]
+    kept, ffn_back, ffn_parts, dgate_ffn = None, [], [], 0.0
+    scale_row = jnp.broadcast_to(row_scale[None], (1, D))
+    for call in calls:
+        if call.start == 1:
+            near, kept = lax.optimization_barrier((near, kept))
+            cot_near, near = lax.optimization_barrier((cot_slots[1:], near))
+            ffn_slots = [ffn_in, *near, opposite(near)]
+            cot_slots = [*cot_slots, opposite(cot_near)]
+        *kept, back, out, dgate = feed(
+            ffn_slots[call], cot_slots[call], gate_ffn, scale_row, glu_w, first_w, call.start, seqs, kept
+        )
+        dgate_ffn = dgate_ffn + dgate
+        ffn_back += [back[i : i + frames_here] for i in range(0, back.shape[0], frames_here)]
+        ffn_parts += [out[i : i + frames_here] for i in range(0, out.shape[0], frames_here)]
+    ffn_all, grad_ffn_all, hidden_all, grad_gate_up = kept
 
     def returned_near(parts):
         if seqs != 4:
@@ -1028,12 +1174,9 @@
             return sum(term.astype(jnp.float32) for term in near + far)
         return jnp.concatenate([n + f.astype(jnp.float32) for n, f in zip(near, far)])
 
-    ffn_back = {j: dot_right_t(grad_gate_up[j], glu_w).astype(low) for j in far_first}
     ffn_back_near = returned_near(ffn_back)
-    ffn_all, hidden_all = jnp.concatenate(ffn_slots), jnp.concatenate(hidden)
-    grad_glu = dot_left_t(ffn_all, jnp.concatenate(grad_gate_up)).astype(low)
-    grad_down = dot_left_t(hidden_all, jnp.concatenate(grad_ffn_slots)).astype(low)
-    ffn_parts = [dot(values, down_w).astype(low) for values in hidden]
+    grad_glu = dot_left_t(ffn_all, grad_gate_up).astype(low)
+    grad_down = dot_left_t(hidden_all, grad_ffn_all).astype(low)
     grad_glu, *ffn_back_near = lax.optimization_barrier((grad_glu, *ffn_back_near))
     ffn_back_far = returned_far(ffn_back, ffn_back_near)
     grad_ffn_in, grad_glu, grad_down, *ffn_parts = lax.optimization_barrier(
@@ -1052,6 +1195,7 @@
         cross_q, cross_kv, cross_kv, grad_cmixed, cross_mixed, cross_lse,
         0, 0, all_pairs, all_pairs, frames_here, text_len,
     )
+    grad_cquery, *ffn_near = lax.optimization_barrier((grad_cquery, *ffn_near))
     grad_cross_in = dot_right_t(grad_cquery, crossq_w)
     grad_gain = jnp.sum(grad_cross_in * normed_c, axis=0, keepdims=True)
     grad_attn = grad_cross + norm_back(grad_cross_in * gain_values, normed_c, inv_c)
@@ -1059,14 +1203,13 @@
     grad_attn_low = (gate_attn * grad_attn).astype(low)
     dgate_attn = jnp.sum(grad_attn * attn_out, axis=0, keepdims=True)
     grad_amixed = dot_right_t(grad_attn_low, attn_w).astype(low)
-    grad_amixed, *ffn_near = lax.optimization_barrier((grad_amixed, *ffn_near))
     head_pieces = [columns(grad_amixed, "seq", j, local_heads) for j in range(seqs)]
-    grad_heads = jnp.concatenate(
-        [head_pieces[0]] + [swap(p, "seq", j) for j, p in enumerate(head_pieces) if j]
-    )
-    cross_mixed, cross_in, attn_mixed, grad_ckey, grad_amixed = lax.optimization_barrier(
-        (cross_mixed, cross_in, attn_mixed, grad_ckey, grad_amixed)
-    )
+    head_pieces = [head_pieces[0]] + [swap(p, "seq", j) for j, p in enumerate(head_pieces) if j]
+    wide_left = [cross_mixed, cross_in, attn_mixed]
+    for j in range(1, min(seqs, 4)):
+        wide_left[j - 1], head_pieces[j] = lax.optimization_barrier((wide_left[j - 1], head_pieces[j]))
+    cross_mixed, cross_in, attn_mixed = wide_left
+    grad_heads = jnp.concatenate(head_pieces)
 
     core = my_row % 2
     wide_own = [
@@ -1079,19 +1222,14 @@
     ]
     half_of = lambda g, c: lax.dynamic_index_in_dim(g, c, 1, keepdims=False)
     wide_got = [swap(half_of(g, 1 - core), "row", 1) for g in wide_own]
-    ffn_out = returned_total(*returned_far(ffn_parts, ffn_near))
-
-    grad_ckv = jnp.concatenate([grad_ckey, grad_cvalue], axis=1)
-    ckv_pieces = [columns(grad_ckv, "seq", j, kv_width) for j in range(seqs)]
-    grad_ckv = ckv_pieces[0] + sum(swap(p, "seq", j) for j, p in enumerate(ckv_pieces) if j)
-    grad_kv = dot_left_t(context[0], grad_ckv.astype(low)).astype(low)
-    result = (after_cross + gate_ffn * ffn_out).astype(low)
-    dgate_ffn = jnp.sum(grad_out * ffn_out, axis=0, keepdims=True)
-    grad_heads, grad_kv, result, dgate_ffn, grad_glu, *wide_got = lax.optimization_barrier(
-        (grad_heads, grad_kv, result, dgate_ffn, grad_glu, *wide_got)
-    )
-    glu_got = exchange(grad_glu.reshape(seqs, depth, -1))
+
+    grad_ckv = jnp.concatenate([grad_ckey, grad_cvalue], axis=1).astype(low)
+    grad_kv = text_product(context[0], grad_ckv)
+    grad_heads, grad_kv, grad_down, *wide_got = lax.optimization_barrier(
+        (grad_heads, grad_kv, grad_down, *wide_got)
+    )
     grad_kv = lax.psum_scatter(grad_kv, "row", scatter_dimension=0, tiled=True)
+    ffn_far, ffn_near = returned_far(ffn_parts, ffn_near)
     wide_both = [(half_of(own, core), got) for own, got in zip(wide_own, wide_got)]
 
     def wide_piece(j):
@@ -1110,11 +1248,27 @@
         ),
         axis=1,
     )
-    grad_projected, grad_down, grad_kv, *got = lax.optimization_barrier(
-        (grad_projected, grad_down, grad_kv, *glu_got, *wide_got)
-    )
-    glu_got, wide_got = got[:seqs], got[seqs:]
-    wide = sum(g.astype(jnp.float32) for g in wide_got).astype(low)
+    grad_projected, grad_glu, wide_got, ffn_far = lax.optimization_barrier(
+        (grad_projected, grad_glu, wide_got, ffn_far)
+    )
+    glu_got = exchange(after(grad_glu, grad_projected).reshape(seqs, depth, -1))
+    grad_qkv = dot_left_t(attn_in, grad_projected).astype(low)
+    grad_projected, grad_qkv = lax.optimization_barrier((grad_projected, grad_qkv))
+    grad_qkv = lax.psum_scatter(grad_qkv, "row", scatter_dimension=0, tiled=True)
+    attn_back, attn_sums = project_back(grad_projected, first_w, x_slots)
+    attn_sums, attn_back, grad_down, grad_kv, glu_got = lax.optimization_barrier(
+        (attn_sums, attn_back, grad_down, grad_kv, glu_got)
+    )
+    own_sums = jnp.concatenate([attn_sums, dgate_attn, dshift_ffn, dscale_ffn, dgate_ffn, grad_gain])
+    own_sums = sum_over(own_sums, "seq")
+    own_sums, attn_back = lax.optimization_barrier((own_sums, attn_back))
+    attn_back = slots(attn_back)
+    attn_near = returned_near(attn_back)
+
+    sums_list, attn_near, grad_qkv = lax.optimization_barrier(
+        (spread_row(own_sums), attn_near, grad_qkv)
+    )
+    wide = sum(g.astype(jnp.float32) for g in after(tuple(wide_got), grad_qkv)).astype(low)
     grad_wide = lax.psum_scatter(
         wide,
         "row",
@@ -1122,28 +1276,12 @@
         axis_index_groups=[list(range(c, rows, 2)) for c in range(2)],
         tiled=True,
     )[0].astype(jnp.float32)
-    grad_qkv = dot_left_t(attn_in, grad_projected).astype(low)
-    grad_projected, grad_qkv = lax.optimization_barrier((grad_projected, grad_qkv))
-    grad_qkv = lax.psum_scatter(grad_qkv, "row", scatter_dimension=0, tiled=True)
-    attn_back, attn_sums = project_back(grad_projected, first_w, x_slots)
-    own_sums = jnp.concatenate([attn_sums, dgate_attn, dshift_ffn, dscale_ffn, dgate_ffn, grad_gain])
-    own_sums = sum_over(own_sums, "seq")
-    attn_back = slots(after(attn_back, own_sums))
-    attn_near = returned_near(attn_back)
-
-    bucket_list = jnp.arange(BUCKETS, dtype=jnp.int32)
-    grad_mods = jnp.zeros((BUCKETS, 6 * D), jnp.float32)
-    gain_total = jnp.zeros((D,), jnp.float32)
-    for j, sums in enumerate(spread(own_sums, "row")):
-        hit = (bucket_list == bucket_ids[my_row ^ j]).astype(jnp.float32)
-        grad_mods = grad_mods + hit[:, None] * sums[:6].reshape(1, 6 * D)
-        gain_total = gain_total + sums[6]
-
-    def outer(left, right):
-        return sum(left[b][:, None] * right[b][None, :] for b in range(BUCKETS))
-
-    def gather_row(own):
-        return natural(spread(own, "row"), "row").transpose(1, 0, 2).reshape(BUCKETS, -1)
+    total = sum(hits[:, j, None, None] * sums for j, sums in enumerate(sums_list))
+    grad_mods = total[:, :6].reshape(BUCKETS, 6 * D)
+    gain_total = jnp.sum(total[:, 6], axis=0)
+
+    def gather_row(slots):
+        return natural(slots, "row").transpose(1, 0, 2).reshape(BUCKETS, -1)
 
     def gather_seq(own):
         return natural(spread(own)).transpose(1, 0, 2).reshape(BUCKETS, -1)
@@ -1151,23 +1289,28 @@
     grad_modul = outer(mine(token_act, depth).astype(jnp.float32), grad_mods)
     token_own = jnp.dot(grad_mods, w_mod.astype(jnp.float32).T, precision=highest)
     token_own = token_own * silu_slope(mine(time_token, depth))
-    token_own, *attn_near = lax.optimization_barrier((token_own, *attn_near))
     token_seq = gather_seq(token_own)
     token_seq, *attn_near = lax.optimization_barrier((token_seq, *attn_near))
     attn_far, attn_own = returned_far(attn_back, attn_near)
-    grad_token = gather_row(token_seq)
+    token_slots, attn_far = lax.optimization_barrier((spread_row(token_seq), attn_far))
+    result = (after_cross + gate_ffn * returned_total(ffn_far, ffn_near)).astype(low)
+    grad_token = gather_row(token_slots)
     grad_timeout = outer(mine(time_hidden, depth).astype(jnp.float32), grad_token)
     hidden_own = jnp.dot(grad_token, w_time_out.astype(jnp.float32).T, precision=highest)
     hidden_own = hidden_own * silu_slope(mine(pre_hidden, depth))
-    hidden_own, grad_qkv, *attn_far = lax.optimization_barrier((hidden_own, grad_qkv, *attn_far))
-    qkv_got = exchange(grad_qkv.reshape(seqs, depth, -1))
     grad_attn_in = returned_total(attn_far, attn_own)
+    kv_stack = grad_kv.reshape(seqs, depth // 2, 2 * D)
+    kv_stack = jnp.concatenate([kv_stack[..., :D], kv_stack[..., D:]], axis=1)
+    qkv_stack = jnp.concatenate([grad_qkv.reshape(seqs, depth, -1), kv_stack], axis=2)
+    qkv_stack, hidden_own = lax.optimization_barrier((qkv_stack, hidden_own))
+    qkv_got = exchange(qkv_stack)
     hidden_seq, *qkv_got = lax.optimization_barrier((gather_seq(hidden_own), *qkv_got))
-    grad_pre = gather_row(hidden_seq)
+    grad_pre = gather_row(spread_row(hidden_seq))
     grad_timein = outer(mine(features, w_time_in.shape[0]).astype(jnp.float32), grad_pre)
     normed_a, inv_a = layer_stats(inputs)
     grad_frames = grad_attn + norm_back(grad_attn_in * (1.0 + scale_attn), normed_a, inv_a)
 
+    qkv_list = qkv_got
     qkv_got = jnp.stack(qkv_got)
     grad_qkv = jnp.concatenate(
         [
@@ -1178,7 +1321,8 @@
         axis=1,
     )
     grad_glu = join_units(natural(glu_got), part)
-    grad_crosskv = side_by_side(exchange(grad_kv.reshape(seqs, ctx_dim // (rows * seqs), -1)))
+    grad_crosskv = sum(piece[:, 3 * local_heads :].astype(jnp.float32) for piece in qkv_list)
+    grad_crosskv = jnp.concatenate([grad_crosskv[: depth // 2], grad_crosskv[depth // 2 :]], axis=1)
 
     return (
         result[None],
@@ -1190,7 +1334,7 @@
         grad_wide[0],
         mine(gain_total, depth),
         grad_wide[1],
-        grad_crosskv.astype(jnp.float32),
+        grad_crosskv,
         grad_wide[2],
         grad_glu,
         grad_down.astype(jnp.float32),

time: 971 us -> 877 us (0.903)
  matrix products: 216 us -> 108 us
  Pallas kernels: 180 us -> 276 us
  waiting for transfers between devices: 198 us -> 166 us
  local copies, waits for them, and re-layouts: 103 us -> 79.7 us
  starting transfers between devices: 127 us -> 110 us
    pallas_call x0 -> x7, Pallas kernels: none -> 96.7 us  [the longest x3 88.3 us: feed(): pl.pallas_call(functools.partial(feed_kernel, per_slot, slots, chunk, kep...]
    ppermute x115 -> x96, waiting for transfers between devices: 198 us -> 121 us  [swap(): return lax.ppermute(value, axis, [(i, i ^ j) for i in range(sizes[axis])])]
    dot_general x11 -> x3, matrix products: 73.7 us -> 19.4 us  [dot_right_t(): jnp.einsum('fj,ij->fi', left, right, preferred_element_type=jnp.float32)]
    dot_general x15 -> x7, matrix products: 71.5 us -> 20.6 us  [dot(): return jnp.dot(left, right, preferred_element_type=jnp.float32)]
    all_gather x1, waiting for transfers between devices: 0.01 us -> 44.3 us  [on_device_split(): lax.all_gather(natural(glu_slots).reshape(seqs * depth, -1), 'row', axis=...]
    unnamed x353 -> x299, local copies, waits for them, and re-layouts: 40.5 us -> 19.5 us
    ppermute x115 -> x96, starting transfers between devices: 126 us -> 109 us  [swap(): return lax.ppermute(value, axis, [(i, i ^ j) for i in range(sizes[axis])])]
    convert_element_type x10 -> x5, other arithmetic: 18.5 us -> 6.81 us  [the longest x1 4.85 us: on_device_split(): sum((g.astype(jnp.float32) for g in after(tuple(wide_got), grad_qkv)))]
  transfers between devices with their start and end apart: 123 -> 104, of which waited for: 46 -> 39; matrix products, arithmetic and copies ran while one was open for 41% -> 29% of each run, Pallas kernels for 19% -> 32%
where the time goes in v3:
time: 877 us; the launch traced here: 872 us
  Pallas kernels  276 us (31%)
  waiting for transfers between devices  166 us (19%)
  starting transfers between devices  110 us (13%)
  matrix products  108 us (12%)
  other arithmetic  100 us (11%)
  local copies, waits for them, and re-layouts  79.7 us (9%)
  between operations  32.4 us (4%)
    ppermute x96, waiting for transfers between devices, swap(): return lax.ppermute(value, axis, [(i, i ^ j) for i in range(sizes[axis])])  121 us
    ppermute x96, starting transfers between devices, swap(): return lax.ppermute(value, axis, [(i, i ^ j) for i in range(sizes[axis])])  109 us
    pallas_call x3, Pallas kernels, feed(): pl.pallas_call(functools.partial(feed_kernel, per_slot, slots, chunk, kep...  88.3 us
    pallas_call x2, Pallas kernels, attend_back(): pl.pallas_call(functools.partial(attend_back_kernel, masked, chunk), grid...  87.9 us
    dot_general x6, matrix products, dot_left_t(): jnp.einsum('fi,fj->ij', left, right, preferred_element_type=jnp.float32)  65.4 us
    pallas_call x2, Pallas kernels, attend(): pl.pallas_call(functools.partial(attend_kernel, masked), grid=(pairs, cou...  56.4 us
    all_gather x1, waiting for transfers between devices, on_device_split(): lax.all_gather(natural(glu_slots).reshape(seqs * depth, -1), 'row', axis=...  44.3 us
    dot_general x7, matrix products, dot(): return jnp.dot(left, right, preferred_element_type=jnp.float32)  20.6 us
  transfers between devices with their start and end apart: 104, of which 39 were waited for; matrix products, arithmetic and copies ran while one was open for 29% of the time, Pallas kernels for 32%

profile of v3, /device:TPU:0, one launch (start us, length us, event | category | flops | bytes accessed | tf_op | source)
XLA Modules:
  0.0 872.3 jit_solution(17452576687936832519)
XLA Ops:
  9.4 4.0 collective-permute-start.2
  14.1 3.5 collective-permute-done.2
  17.6 2.8 collective-permute-done.1
  28.5 2.5 collective-permute-done.4
  36.4 7.8 collective-permute-done.6
  44.3 6.6 collective-permute-done.7
  54.4 5.5 collective-permute-done.9
  59.9 4.4 collective-permute-start.10
  65.1 5.6 collective-permute-done.10
  72.6 2.5 collective-permute-done.13
  76.8 2.5 collective-permute-done.14
  102.4 2.6 pad_maximum_fusion.6.refs_3_
  109.9 3.5 collective-permute-start.22
  142.6 3.3 collective-permute-done.29
  147.5 17.3 %project.1 = (bf16[2048,1536]{1,0:T(8,128)(2,1)}, bf16[2048,1152]{1,0:T(8,128)(2,1)}) custom-call(bf16[512,1536]{1,0:T(8,128)(2,1)S(1)} %bitcast.300, bf16[512,1536]{1,0:T(8,128)(2,1)} %collective-permute-done.11.refs_1_, bf16[512,1536]{1,0:T(8,128)(2,1)} %collective-permute-done.12.refs_2_, bf16[512,1536]{1,0:T(8,128)(2,1)} %pad_maximum_fusion.6.refs_3_, ...), custom_call_target="tpu_custom_call" | custom-call | flops 7247757312 | bytes 20840448 | tf_op jit(solution)/shard_map/project/pallas_call | solution.py:94
  170.2 46.8 %attend.2 = (bf16[2048,384]{1,0:T(8,128)(2,1)S(1)}, f32[3,2,2048]{2,1,0:T(2,128)S(1)}) custom-call(bf16[2048,1152]{1,0:T(8,128)(2,1)} %get-tuple-element.187.refs_0_.refs_1_.refs_2_, bf16[2048,1152]{1,0:T(8,128)(2,1)} %get-tuple-element.187.refs_0_.refs_1_.refs_2_, bf16[2048,1152]{1,0:T(8,128)(2,1)} %get-tuple-element.187.refs_0_.refs_1_.refs_2_, ...), custom_call_target="tpu_custom_call" | custom-call | flops 25769803776 | bytes 6291456 | tf_op jit(solution)/shard_map/attend/pallas_call | solution.py:209
  231.9 6.5 collective-permute-done.33
  241.2 8.9 %fusion.75 = (f32[512]{0:T(512)S(1)}, f32[512,1536]{1,0:T(8,128)S(1)}, f32[512]{0:T(512)}, f32[512,1536]{1,0:T(8,128)}) fusion(f32[1536]{0:T(1024)S(1)} %copy-done.119, bf16[1,512,1536]{2,1,0:T(8,128)(2,1)S(1)} %copy-done.1, f32[512]{0:T(512)S(1)} %broadcast_multiply_fusion.2, bf16[1536,4608]{1,0:T(8,128)(2,1)} %all-gather.6.cloned.1.call-done, ...), kind=kOutput, calls=%fused_computation.367 | convolution fusion | flops 2427714560 | bytes 14168064 | tf_op jit(solution)/shard_map/dot_general | solution.py:1017
  252.7 5.1 fusion.30.refs_0_
  257.8 9.7 %attend.3 = (bf16[512,1536]{1,0:T(8,128)(2,1)S(1)}, f32[12,2,512]{2,1,0:T(2,128)S(1)}) custom-call(bf16[512,1536]{1,0:T(8,128)(2,1)S(1)} %fusion.30.refs_0_, bf16[128,3072]{1,0:T(8,128)(2,1)S(1)} %copy-done.10, bf16[128,3072]{1,0:T(8,128)(2,1)S(1)} %copy-done.10), custom_call_target="tpu_custom_call" | custom-call | flops 1610612736 | bytes 3932160 | tf_op jit(solution)/shard_map/attend/pallas_call | solution.py:209
  267.5 5.6 fusion.86
  280.1 44.3 %all-gather.8.cloned.1.call-done.refs_4_.refs_6_ = bf16[1536,3072]{1,0:T(8,128)(2,1)} async-done(((bf16[192,3072]{1,0:T(8,128)(2,1)}), bf16[1536,3072]{1,0:T(8,128)(2,1)}) %all-gather.8.cloned.1.call-update) | async-done | bytes 9437200 | tf_op jit(solution)/shard_map/all_gather | solution.py:1111
  325.1 23.5 %feed.3 = (bf16[2048,1536]{1,0:T(8,128)(2,1)}, bf16[2048,1536]{1,0:T(8,128)(2,1)}, bf16[2048,1536]{1,0:T(8,128)(2,1)}, bf16[2048,3072]{1,0:T(8,128)(2,1)}, bf16[...) custom-call(bf16[512,1536]{1,0:T(8,128)(2,1)} %add_convert_fusion.1.refs_0_, ...), custom_call_target="tpu_custom_call" | custom-call | flops 14495514624 | bytes 28311552 | tf_op jit(solution)/shard_map/feed/pallas_call | solution.py:432
  358.3 41.2 %feed.4 = (bf16[2048,1536]{1,0:T(8,128)(2,1)}, bf16[2048,1536]{1,0:T(8,128)(2,1)}, bf16[2048,1536]{1,0:T(8,128)(2,1)}, bf16[2048,3072]{1,0:T(8,128)(2,1)}, bf16[...) custom-call(bf16[512,1536]{1,0:T(8,128)(2,1)} %collective-permute-do, ...), custom_call_target="tpu_custom_call", output_to_operand_aliasing={{0}: (8, {}), {1}: (9, {}), {2}: (10, {}), {3}: (11, {})} | custom-call | flops 28991029248 | bytes 42467328 | tf_op jit(solution)/shard_map/feed/pallas_call | solution.py:432
  399.5 2.8 fusion.78
  411.9 23.6 %feed.5 = (bf16[2048,1536]{1,0:T(8,128)(2,1)}, bf16[2048,1536]{1,0:T(8,128)(2,1)}, bf16[2048,1536]{1,0:T(8,128)(2,1)}, bf16[2048,3072]{1,0:T(8,128)(2,1)}, bf16[...) custom-call(bf16[512,1536]{1,0:T(8,128)(2,1)} %pad_maximum_fusion.9., ...), custom_call_target="tpu_custom_call", output_to_operand_aliasing={{0}: (6, {}), {1}: (7, {}), {2}: (8, {}), {3}: (9, {})} | custom-call | flops 14495514624 | bytes 28311552 | tf_op jit(solution)/shard_map/feed/pallas_call | solution.py:432
  438.9 26.2 %convolution_convert_fusion = bf16[1536,3072]{1,0:T(8,128)(2,1)} fusion(bf16[2048,1536]{1,0:T(8,128)(2,1)} %get-tuple-element.219, bf16[2048,3072]{1,0:T(8,128)(2,1)} %get-tuple-element.220), kind=kOutput, calls=%fused_computation.1 | convolution fusion | flops 19332071424 | bytes 28311552 | tf_op jit(solution)/shard_map/fi,fj->ij/dot_general | solution.py:1023
  465.2 3.4 add_convert_fusion.7
  471.5 15.5 %convolution_convert_fusion.5 = bf16[1536,1536]{1,0:T(8,128)(2,1)} fusion(bf16[2048,1536]{1,0:T(8,128)(2,1)} %get-tuple-element.228, bf16[2048,1536]{1,0:T(8,128)(2,1)} %get-tuple-element.229), kind=kOutput, calls=%fused_computation.6 | convolution fusion | flops 9666035712 | bytes 17301504 | tf_op jit(solution)/shard_map/fi,fj->ij/dot_general | solution.py:1023
  487.5 2.9 convert_add_fusion.6
  504.3 3.4 multiply_add_fusion.1
  507.7 7.3 fusion.33.refs_3_
  515.1 12.2 %attend_back.2 = (bf16[512,1536]{1,0:T(8,128)(2,1)S(1)}, f32[128,1536]{1,0:T(8,128)S(1)}, f32[128,1536]{1,0:T(8,128)S(1)}) custom-call(bf16[512,1536]{1,0:T(8,128)(2,1)} %copy-done.22, bf16[128,3072]{1,0:T(8,128)(2,1)S(1)} %copy-done.11, bf16[128,3072]{1,0:T(8,128)(2,1)S(1)} %copy-done.11, bf16[512,1536]{1,0:T(8,128)(2,1)} %fusion.33.refs_3_, ...), custom_call_target="tpu_custom_call" | custom-call | flops 4026531840 | bytes 7864320 | tf_op jit(solution)/shard_map/attend_back/pallas_call | solution.py:306
  530.2 5.9 multiply_reduce_fusion
  537.7 6.2 fusion.27
  550.3 5.9 collective-permute-done.53
  556.2 4.8 convolution_convert_fusion.2
  565.2 2.9 convolution_convert_fusion.3
  572.3 2.9 convolution_convert_fusion.4
  580.6 4.1 text_product.1
  584.8 2.6 add_convert_fusion.4
  593.5 4.1 fusion.44
  597.6 4.0 fusion.43
  601.6 4.0 fusion.42
  612.8 75.7 %attend_back.3 = (bf16[2048,384]{1,0:T(8,128)(2,1)}, bf16[2048,384]{1,0:T(8,128)(2,1)}, bf16[2048,384]{1,0:T(8,128)(2,1)}) custom-call(bf16[2048,1152]{1,0:T(8,128)(2,1)} %get-tuple-element.187.refs_0_.refs_1_.refs_2_, bf16[2048,1152]{1,0:T(8,128)(2,1)} %get-tuple-element.187.refs_0_.refs_1_.refs_2_, ...), custom_call_target="tpu_custom_call" | custom-call | flops 64424509440 | bytes 12582912 | tf_op jit(solution)/shard_map/attend_back/pallas_call | solution.py:306
  691.0 3.6 pad_maximum_fusion.refs_4_
  695.8 13.2 %convolution_convert_fusion.1 = bf16[1536,1152]{1,0:T(8,128)(2,1)} fusion(bf16[2048,1536]{1,0:T(8,128)(2,1)} %get-tuple-element.266, bf16[2048,1152]{1,0:T(8,128)(2,1)} %pad_maximum_fusion.refs_4_), kind=kOutput, calls=%fused_computation.2 | convolution fusion | flops 7249526784 | bytes 14548992 | tf_op jit(solution)/shard_map/fi,fj->ij/dot_general | solution.py:1023
  716.4 4.1 convert_add_fusion.4
  720.4 15.9 %project_back.1 = (bf16[2048,1536]{1,0:T(8,128)(2,1)}, f32[2,1536]{1,0:T(2,128)S(1)}) custom-call(bf16[512,1536]{1,0:T(8,128)(2,1)S(1)} %bitcast.301, bf16[512,1536]{1,0:T(8,128)(2,1)} %collective-permute-done.11.refs_1_, bf16[512,1536]{1,0:T(8,128)(2,1)} %collective-permute-done.12.refs_2_, bf16[512,1536]{1,0:T(8,128)(2,1)} %pad_maximum_fusion.6.refs_3_, ...), custom_call_target="tpu_custom_call" | custom-call | flops 7247757312 | bytes 20840448 | tf_op jit(solution)/shard_map/project_back/pallas_call | solution.py:141
  742.7 2.6 collective-permute-done.68
  756.4 5.1 collective-permute-done.71
  761.5 4.6 collective-permute-done.70
  766.1 3.8 collective-permute-done.73
  771.1 14.8 %collective-permute-done.75 = bf16[256,1536]{1,0:T(8,128)(2,1)S(1)} collective-permute-done((bf16[256,1536]{1,0:T(8,128)(2,1)S(1)}, bf16[256,1536]{1,0:T(8,128)(2,1)S(1)}, u32[]{:S(2)}, u32[]{:S(2)}) %collective-permute-start.75) | collective-permute-done | bytes 786464 | tf_op jit(solution)/shard_map/ppermute | solution.py:953
  792.8 4.8 add_convert_fusion
  804.5 3.3 collective-permute-start.83
  809.4 2.6 outer.5
  813.1 4.3 collective-permute-done.82
  817.6 4.6 collective-permute-done.84
  832.7 2.6 convert_add_fusion.2
  837.8 4.1 fusion.23
  844.8 5.5 collective-permute-done.91
  852.7 3.0 collective-permute-start.94
  857.5 3.8 collective-permute-done.95
  (683 shorter events, 247.3 us)
Async XLA Ops:
  7.2 131.7 %all-gather.4.cloned.1.call-start = ((), (), s32[]{:S(2)}) async-start(), calls=%async_computation.5 | async-start | bytes 10616832 | tf_op jit(solution)/shard_map/all_gather | solution.py:1052
  22.1 219.2 %all-gather.6.cloned.1.call-start = ((), (), s32[]{:S(2)}) async-start(), calls=%async_computation.6 | async-start | bytes 14598144 | tf_op jit(solution)/shard_map/all_gather | solution.py:1071
  31.0 39.7 %collective-permute-start.11 = (bf16[512,1536]{1,0:T(8,128)(2,1)S(1)}, bf16[512,1536]{1,0:T(8,128)(2,1)}, u32[]{:S(2)}, u32[]{:S(2)}) collective-permute-start(bf16[512,1536]{1,0:T(8,128)(2,1)S(1)} %bitcast.298), channel_id=1, source_target_pairs={{0,1},{1,0},{2,3},{3,2},{4,5},{5,4},{6,7},{7,6},{8,9},{9,8},{10,11... | collective-permute-start | bytes 4718600 | tf_op jit(solution)/shard_map/ppermute | solution.py:953
  32.7 38.0 %collective-permute-start.12 = (bf16[512,1536]{1,0:T(8,128)(2,1)S(1)}, bf16[512,1536]{1,0:T(8,128)(2,1)}, u32[]{:S(2)}, u32[]{:S(2)}) collective-permute-start(bf16[512,1536]{1,0:T(8,128)(2,1)S(1)} %bitcast.299), channel_id=1, source_target_pairs={{0,2},{1,3},{2,0},{3,1},{4,6},{5,7},{6,4},{7,5},{8,10},{9,11},{10,... | collective-permute-start | bytes 4718600 | tf_op jit(solution)/shard_map/ppermute | solution.py:953
  70.8 253.7 %all-gather.8.cloned.1.call-start = ((), (), s32[]{:S(2)}) async-start(), calls=%async_computation.7 | async-start | bytes 10616832 | tf_op jit(solution)/shard_map/all_gather | solution.py:1111
  80.6 19.7 %collective-permute-start.15 = (bf16[256,1536]{1,0:T(8,128)(2,1)S(1)}, bf16[256,1536]{1,0:T(8,128)(2,1)}, u32[]{:S(2)}, u32[]{:S(2)}) collective-permute-start(bf16[256,1536]{1,0:T(8,128)(2,1)S(1)} %slice.348), channel_id=1, source_target_pairs={{0,1},{1,0},{2,3},{3,2},{4,5},{5,4},{6,7},{7,6},{8,9},{9,8},{10,11... | collective-permute-start | bytes 2359304 | tf_op jit(solution)/shard_map/ppermute | solution.py:953
  84.2 18.2 %collective-permute-start.16 = (bf16[256,1536]{1,0:T(8,128)(2,1)}, bf16[256,1536]{1,0:T(8,128)(2,1)}, u32[]{:S(2)}, u32[]{:S(2)}) collective-permute-start(bf16[256,1536]{1,0:T(8,128)(2,1)} %slice.349), channel_id=1, source_target_pairs={{0,2},{1,3},{2,0},{3,1},{4,6},{5,7},{6,4},{7,5},{8,10},{9,11},{10,... | collective-permute-start | bytes 2359304 | tf_op jit(solution)/shard_map/ppermute | solution.py:953
  105.5 13.0 %collective-permute-start.19 = (f32[1,9216]{1,0:T(1,128)S(1)}, f32[1,9216]{1,0:T(1,128)}, u32[]{:S(2)}, u32[]{:S(2)}) collective-permute-start(f32[1,9216]{1,0:T(1,128)S(1)} %get-tuple-element.454), channel_id=1, source_target_pairs={{0,12},{4,8},{8,4},{12,0},{16,28},{20,24},{24,20},{28,16},{1,13},{... | collective-permute-start | bytes 110600 | tf_op jit(solution)/shard_map/ppermute | solution.py:953
  135.9 29.0 %collective-permute-start.30 = (bf16[48,3072]{1,0:T(8,128)(2,1)}, bf16[48,3072]{1,0:T(8,128)(2,1)}, u32[]{:S(2)}, u32[]{:S(2)}) collective-permute-start(bf16[48,3072]{1,0:T(8,128)(2,1)} %get-tuple-element.409), channel_id=1, source_target_pairs={{0,2},{1,3},{2,0},{3,1},{4,6},{5,7},{6,4},{7,5},{8,10},{9,11},{10,... | collective-permute-start | bytes 884744 | tf_op jit(solution)/shard_map/ppermute | solution.py:953
  136.1 28.8 %collective-permute-start.31 = (bf16[48,3072]{1,0:T(8,128)(2,1)}, bf16[48,3072]{1,0:T(8,128)(2,1)}, u32[]{:S(2)}, u32[]{:S(2)}) collective-permute-start(bf16[48,3072]{1,0:T(8,128)(2,1)} %get-tuple-element.408), channel_id=1, source_target_pairs={{0,3},{1,2},{2,1},{3,0},{4,7},{5,6},{6,5},{7,4},{8,11},{9,10},{10,... | collective-permute-start | bytes 884744 | tf_op jit(solution)/shard_map/ppermute | solution.py:953
  141.1 23.8 %collective-permute-start.26 = (bf16[128,768]{0,1:T(8,128)(2,1)S(1)}, bf16[128,768]{0,1:T(8,128)(2,1)S(1)}, u32[]{:S(2)}, u32[]{:S(2)}) collective-permute-start(bf16[128,768]{0,1:T(8,128)(2,1)S(1)} %fusion.57), channel_id=1, source_target_pairs={{0,1},{1,0},{2,3},{3,2},{4,5},{5,4},{6,7},{7,6},{8,9},{9,8},{10,11... | collective-permute-start | bytes 589832 | tf_op jit(solution)/shard_map/ppermute | solution.py:953
  142.3 22.6 %collective-permute-start.27 = (bf16[128,768]{0,1:T(8,128)(2,1)S(1)}, bf16[128,768]{0,1:T(8,128)(2,1)S(1)}, u32[]{:S(2)}, u32[]{:S(2)}) collective-permute-start(bf16[128,768]{0,1:T(8,128)(2,1)S(1)} %fusion.57), channel_id=1, source_target_pairs={{0,2},{1,3},{2,0},{3,1},{4,6},{5,7},{6,4},{7,5},{8,10},{9,11},{10,... | collective-permute-start | bytes 589832 | tf_op jit(solution)/shard_map/ppermute | solution.py:953
  145.8 19.1 %collective-permute-start.28 = (bf16[128,768]{0,1:T(8,128)(2,1)S(1)}, bf16[128,768]{0,1:T(8,128)(2,1)S(1)}, u32[]{:S(2)}, u32[]{:S(2)}) collective-permute-start(bf16[128,768]{0,1:T(8,128)(2,1)S(1)} %fusion.57), channel_id=1, source_target_pairs={{0,3},{1,2},{2,1},{3,0},{4,7},{5,6},{6,5},{7,4},{8,11},{9,10},{10,... | collective-permute-start | bytes 589832 | tf_op jit(solution)/shard_map/ppermute | solution.py:953
  167.7 425.8 %reduce-scatter.6.cloned.1.call-start = ((), (), s32[]{:S(2)}) async-start(), calls=%async_computation.8 | async-start | bytes 5308416 | tf_op jit(solution)/shard_map/reduce_scatter | solution.py:1186
  218.2 13.7 %collective-permute-start.32 = (bf16[512,384]{1,0:T(8,128)(2,1)}, bf16[512,384]{1,0:T(8,128)(2,1)}, u32[]{:S(2)}, u32[]{:S(2)}) collective-permute-start(bf16[512,384]{1,0:T(8,128)(2,1)} %get-tuple-element.395), channel_id=1, source_target_pairs={{0,1},{1,0},{2,3},{3,2},{4,5},{5,4},{6,7},{7,6},{8,9},{9,8},{10,11... | collective-permute-start | bytes 1179656 | tf_op jit(solution)/shard_map/ppermute | solution.py:953
  219.5 18.9 %collective-permute-start.33 = (bf16[512,384]{1,0:T(8,128)(2,1)}, bf16[512,384]{1,0:T(8,128)(2,1)}, u32[]{:S(2)}, u32[]{:S(2)}) collective-permute-start(bf16[512,384]{1,0:T(8,128)(2,1)} %get-tuple-element.394), channel_id=1, source_target_pairs={{0,2},{1,3},{2,0},{3,1},{4,6},{5,7},{6,4},{7,5},{8,10},{9,11},{10,... | collective-permute-start | bytes 1179656 | tf_op jit(solution)/shard_map/ppermute | solution.py:953
  220.0 18.4 %collective-permute-start.34 = (bf16[512,384]{1,0:T(8,128)(2,1)}, bf16[512,384]{1,0:T(8,128)(2,1)}, u32[]{:S(2)}, u32[]{:S(2)}) collective-permute-start(bf16[512,384]{1,0:T(8,128)(2,1)} %get-tuple-element.393), channel_id=1, source_target_pairs={{0,3},{1,2},{2,1},{3,0},{4,7},{5,6},{6,5},{7,4},{8,11},{9,10},{10,... | collective-permute-start | bytes 1179656 | tf_op jit(solution)/shard_map/ppermute | solution.py:953
  275.4 73.2 %collective-permute-start.37 = (bf16[512,1536]{1,0:T(8,128)(2,1)}, bf16[512,1536]{1,0:T(8,128)(2,1)}, u32[]{:S(2)}, u32[]{:S(2)}) collective-permute-start(bf16[512,1536]{1,0:T(8,128)(2,1)} %add_convert_fusion.1.refs_0_), channel_id=1, source_target_pairs={{0,1},{1,0},{2,3},{3,2},{4,5},{5,4},{6,7},{7,6},{8,9},{9,8},{10,11... | collective-permute-start | bytes 4718600 | tf_op jit(solution)/shard_map/ppermute | solution.py:953
  275.5 73.2 %collective-permute-start.38 = (bf16[512,1536]{1,0:T(8,128)(2,1)}, bf16[512,1536]{1,0:T(8,128)(2,1)}, u32[]{:S(2)}, u32[]{:S(2)}) collective-permute-start(bf16[512,1536]{1,0:T(8,128)(2,1)} %add_convert_fusion.1.refs_0_), channel_id=1, source_target_pairs={{0,2},{1,3},{2,0},{3,1},{4,6},{5,7},{6,4},{7,5},{8,10},{9,11},{10,... | collective-permute-start | bytes 4718600 | tf_op jit(solution)/shard_map/ppermute | solution.py:953
  276.8 71.9 %collective-permute-start.35 = (bf16[512,1536]{1,0:T(8,128)(2,1)}, bf16[512,1536]{1,0:T(8,128)(2,1)}, u32[]{:S(2)}, u32[]{:S(2)}) collective-permute-start(bf16[512,1536]{1,0:T(8,128)(2,1)} %bitcast.45.refs_1_), channel_id=1, source_target_pairs={{0,1},{1,0},{2,3},{3,2},{4,5},{5,4},{6,7},{7,6},{8,9},{9,8},{10,11... | collective-permute-start | bytes 4718600 | tf_op jit(solution)/shard_map/ppermute | solution.py:953
  277.7 71.0 %collective-permute-start.36 = (bf16[512,1536]{1,0:T(8,128)(2,1)}, bf16[512,1536]{1,0:T(8,128)(2,1)}, u32[]{:S(2)}, u32[]{:S(2)}) collective-permute-start(bf16[512,1536]{1,0:T(8,128)(2,1)} %bitcast.45.refs_1_), channel_id=1, source_target_pairs={{0,2},{1,3},{2,0},{3,1},{4,6},{5,7},{6,4},{7,5},{8,10},{9,11},{10,... | collective-permute-start | bytes 4718600 | tf_op jit(solution)/shard_map/ppermute | solution.py:953
  350.4 55.2 %collective-permute-start.41 = (bf16[256,1536]{1,0:T(8,128)(2,1)S(1)}, bf16[256,1536]{1,0:T(8,128)(2,1)S(1)}, u32[]{:S(2)}, u32[]{:S(2)}) collective-permute-start(bf16[256,1536]{1,0:T(8,128)(2,1)S(1)} %slice.365), channel_id=1, source_target_pairs={{0,1},{1,0},{2,3},{3,2},{4,5},{5,4},{6,7},{7,6},{8,9},{9,8},{10,11... | collective-permute-start | bytes 2359304 | tf_op jit(solution)/shard_map/ppermute | solution.py:953
  353.2 53.9 %collective-permute-start.42 = (bf16[256,1536]{1,0:T(8,128)(2,1)S(1)}, bf16[256,1536]{1,0:T(8,128)(2,1)}, u32[]{:S(2)}, u32[]{:S(2)}) collective-permute-start(bf16[256,1536]{1,0:T(8,128)(2,1)S(1)} %slice.366), channel_id=1, source_target_pairs={{0,2},{1,3},{2,0},{3,1},{4,6},{5,7},{6,4},{7,5},{8,10},{9,11},{10,... | collective-permute-start | bytes 2359304 | tf_op jit(solution)/shard_map/ppermute | solution.py:953
  356.0 53.5 %collective-permute-start.39 = (bf16[256,1536]{1,0:T(8,128)(2,1)S(1)}, bf16[256,1536]{1,0:T(8,128)(2,1)S(1)}, u32[]{:S(2)}, u32[]{:S(2)}) collective-permute-start(bf16[256,1536]{1,0:T(8,128)(2,1)S(1)} %slice.363), channel_id=1, source_target_pairs={{0,1},{1,0},{2,3},{3,2},{4,5},{5,4},{6,7},{7,6},{8,9},{9,8},{10,11... | collective-permute-start | bytes 2359304 | tf_op jit(solution)/shard_map/ppermute | solution.py:953
  357.8 51.7 %collective-permute-start.40 = (bf16[256,1536]{1,0:T(8,128)(2,1)S(1)}, bf16[256,1536]{1,0:T(8,128)(2,1)}, u32[]{:S(2)}, u32[]{:S(2)}) collective-permute-start(bf16[256,1536]{1,0:T(8,128)(2,1)S(1)} %slice.364), channel_id=1, source_target_pairs={{0,2},{1,3},{2,0},{3,1},{4,6},{5,7},{6,4},{7,5},{8,10},{9,11},{10,... | collective-permute-start | bytes 2359304 | tf_op jit(solution)/shard_map/ppermute | solution.py:953
  402.3 62.9 %collective-permute-start.45 = (bf16[256,1536]{1,0:T(8,128)(2,1)}, bf16[256,1536]{1,0:T(8,128)(2,1)}, u32[]{:S(2)}, u32[]{:S(2)}) collective-permute-start(bf16[256,1536]{1,0:T(8,128)(2,1)} %get-tuple-element.374), channel_id=1, source_target_pairs={{0,1},{1,0},{2,3},{3,2},{4,5},{5,4},{6,7},{7,6},{8,9},{9,8},{10,11... | collective-permute-start | bytes 2359304 | tf_op jit(solution)/shard_map/ppermute | solution.py:953
  405.6 59.5 %collective-permute-start.46 = (bf16[256,1536]{1,0:T(8,128)(2,1)}, bf16[256,1536]{1,0:T(8,128)(2,1)}, u32[]{:S(2)}, u32[]{:S(2)}) collective-permute-start(bf16[256,1536]{1,0:T(8,128)(2,1)} %get-tuple-element.373), channel_id=1, source_target_pairs={{0,2},{1,3},{2,0},{3,1},{4,6},{5,7},{6,4},{7,5},{8,10},{9,11},{10,... | collective-permute-start | bytes 2359304 | tf_op jit(solution)/shard_map/ppermute | solution.py:953
  437.8 27.3 %collective-permute-start.43 = (bf16[256,1536]{1,0:T(8,128)(2,1)}, bf16[256,1536]{1,0:T(8,128)(2,1)}, u32[]{:S(2)}, u32[]{:S(2)}) collective-permute-start(bf16[256,1536]{1,0:T(8,128)(2,1)} %get-tuple-element.387), channel_id=1, source_target_pairs={{0,1},{1,0},{2,3},{3,2},{4,5},{5,4},{6,7},{7,6},{8,9},{9,8},{10,11... | collective-permute-start | bytes 2359304 | tf_op jit(solution)/shard_map/ppermute | solution.py:953
  438.4 26.8 %collective-permute-start.44 = (bf16[256,1536]{1,0:T(8,128)(2,1)}, bf16[256,1536]{1,0:T(8,128)(2,1)}, u32[]{:S(2)}, u32[]{:S(2)}) collective-permute-start(bf16[256,1536]{1,0:T(8,128)(2,1)} %get-tuple-element.386), channel_id=1, source_target_pairs={{0,2},{1,3},{2,0},{3,1},{4,6},{5,7},{6,4},{7,5},{8,10},{9,11},{10,... | collective-permute-start | bytes 2359304 | tf_op jit(solution)/shard_map/ppermute | solution.py:953
  468.5 18.5 %collective-permute-start.47 = (bf16[256,1536]{1,0:T(8,128)(2,1)}, bf16[256,1536]{1,0:T(8,128)(2,1)}, u32[]{:S(2)}, u32[]{:S(2)}) collective-permute-start(bf16[256,1536]{1,0:T(8,128)(2,1)} %get-tuple-element.371), channel_id=1, source_target_pairs={{0,2},{1,3},{2,0},{3,1},{4,6},{5,7},{6,4},{7,5},{8,10},{9,11},{10,... | collective-permute-start | bytes 2359304 | tf_op jit(solution)/shard_map/ppermute | solution.py:953
  470.1 17.5 %collective-permute-start.48 = (bf16[256,1536]{1,0:T(8,128)(2,1)}, bf16[256,1536]{1,0:T(8,128)(2,1)}, u32[]{:S(2)}, u32[]{:S(2)}) collective-permute-start(bf16[256,1536]{1,0:T(8,128)(2,1)} %get-tuple-element.372), channel_id=1, source_target_pairs={{0,1},{1,0},{2,3},{3,2},{4,5},{5,4},{6,7},{7,6},{8,9},{9,8},{10,11... | collective-permute-start | bytes 2359304 | tf_op jit(solution)/shard_map/ppermute | solution.py:953
  492.4 203.4 %reduce-scatter.8.cloned.1.call-start = ((), (), s32[]{:S(2)}) async-start(), calls=%async_computation.9 | async-start | bytes 10616832 | tf_op jit(solution)/shard_map/reduce_scatter | solution.py:1185
  493.0 243.4 %reduce-scatter.10.cloned.1.call-start = ((), (), s32[]{:S(2)}) async-start(), calls=%async_computation.10 | async-start | bytes 5308416 | tf_op jit(solution)/shard_map/reduce_scatter | solution.py:1231
  495.8 31.6 %collective-permute-start.49 = (bf16[256,1536]{1,0:T(8,128)(2,1)}, bf16[256,1536]{1,0:T(8,128)(2,1)S(1)}, u32[]{:S(2)}, u32[]{:S(2)}) collective-permute-start(bf16[256,1536]{1,0:T(8,128)(2,1)} %get-tuple-element.383), channel_id=1, source_target_pairs={{0,1},{1,0},{2,3},{3,2},{4,5},{5,4},{6,7},{7,6},{8,9},{9,8},{10,11... | collective-permute-start | bytes 2359304 | tf_op jit(solution)/shard_map/ppermute | solution.py:953
  497.2 30.1 %collective-permute-start.50 = (bf16[256,1536]{1,0:T(8,128)(2,1)S(1)}, bf16[256,1536]{1,0:T(8,128)(2,1)S(1)}, u32[]{:S(2)}, u32[]{:S(2)}) collective-permute-start(bf16[256,1536]{1,0:T(8,128)(2,1)S(1)} %get-tuple-element.382), channel_id=1, source_target_pairs={{0,2},{1,3},{2,0},{3,1},{4,6},{5,7},{6,4},{7,5},{8,10},{9,11},{10,... | collective-permute-start | bytes 2359304 | tf_op jit(solution)/shard_map/ppermute | solution.py:953
  499.0 30.3 %collective-permute-start.51 = (bf16[256,1536]{1,0:T(8,128)(2,1)S(1)}, bf16[256,1536]{1,0:T(8,128)(2,1)}, u32[]{:S(2)}, u32[]{:S(2)}) collective-permute-start(bf16[256,1536]{1,0:T(8,128)(2,1)S(1)} %slice.379), channel_id=1, source_target_pairs={{0,1},{1,0},{2,3},{3,2},{4,5},{5,4},{6,7},{7,6},{8,9},{9,8},{10,11... | collective-permute-start | bytes 2359304 | tf_op jit(solution)/shard_map/ppermute | solution.py:953
  500.9 29.3 %collective-permute-start.52 = (bf16[256,1536]{1,0:T(8,128)(2,1)S(1)}, bf16[256,1536]{1,0:T(8,128)(2,1)}, u32[]{:S(2)}, u32[]{:S(2)}) collective-permute-start(bf16[256,1536]{1,0:T(8,128)(2,1)S(1)} %slice.380), channel_id=1, source_target_pairs={{0,2},{1,3},{2,0},{3,1},{4,6},{5,7},{6,4},{7,5},{8,10},{9,11},{10,... | collective-permute-start | bytes 2359304 | tf_op jit(solution)/shard_map/ppermute | solution.py:953
  545.1 11.1 %collective-permute-start.53 = (bf16[512,384]{1,0:T(8,128)(2,1)}, bf16[512,384]{1,0:T(8,128)(2,1)}, u32[]{:S(2)}, u32[]{:S(2)}) collective-permute-start(bf16[512,384]{1,0:T(8,128)(2,1)} %get-tuple-element.381), channel_id=1, source_target_pairs={{0,1},{1,0},{2,3},{3,2},{4,5},{5,4},{6,7},{7,6},{8,9},{9,8},{10,11... | collective-permute-start | bytes 1179656 | tf_op jit(solution)/shard_map/ppermute | solution.py:953
  547.3 17.1 %collective-permute-start.54 = (bf16[512,384]{1,0:T(8,128)(2,1)S(1)}, bf16[512,384]{1,0:T(8,128)(2,1)}, u32[]{:S(2)}, u32[]{:S(2)}) collective-permute-start(bf16[512,384]{1,0:T(8,128)(2,1)S(1)} %copy-done.80), channel_id=1, source_target_pairs={{0,2},{1,3},{2,0},{3,1},{4,6},{5,7},{6,4},{7,5},{8,10},{9,11},{10,... | collective-permute-start | bytes 1179656 | tf_op jit(solution)/shard_map/ppermute | solution.py:953
  548.0 23.6 %collective-permute-start.55 = (bf16[512,384]{1,0:T(8,128)(2,1)S(1)}, bf16[512,384]{1,0:T(8,128)(2,1)S(1)}, u32[]{:S(2)}, u32[]{:S(2)}) collective-permute-start(bf16[512,384]{1,0:T(8,128)(2,1)S(1)} %copy-done.79), channel_id=1, source_target_pairs={{0,3},{1,2},{2,1},{3,0},{4,7},{5,6},{6,5},{7,4},{8,11},{9,10},{10,... | collective-permute-start | bytes 1179656 | tf_op jit(solution)/shard_map/ppermute | solution.py:953
  564.5 29.0 %collective-permute-start.58 = (bf16[4,4,48,1536]{3,2,1,0:T(8,128)(2,1)}, bf16[4,4,48,1536]{3,2,1,0:T(8,128)(2,1)}, u32[]{:S(2)}, u32[]{:S(2)}) collective-permute-start(bf16[4,4,48,1536]{3,2,1,0:T(8,128)(2,1)} %dynamic-slice_bitcast_fusion), channel_id=1, source_target_pairs={{0,4},{4,0},{8,12},{12,8},{16,20},{20,16},{24,28},{28,24},{1,5},{5... | collective-permute-start | bytes 7077896 | tf_op jit(solution)/shard_map/ppermute | solution.py:953
  571.6 21.9 %collective-permute-start.57 = (bf16[4,4,48,1536]{3,2,1,0:T(8,128)(2,1)}, bf16[4,4,48,1536]{3,2,1,0:T(8,128)(2,1)}, u32[]{:S(2)}, u32[]{:S(2)}) collective-permute-start(bf16[4,4,48,1536]{3,2,1,0:T(8,128)(2,1)} %dynamic-slice_bitcast_fusion.1), channel_id=1, source_target_pairs={{0,4},{4,0},{8,12},{12,8},{16,20},{20,16},{24,28},{28,24},{1,5},{5... | collective-permute-start | bytes 7077896 | tf_op jit(solution)/shard_map/ppermute | solution.py:953
  578.1 15.4 %collective-permute-start.56 = (bf16[4,4,48,1536]{3,2,1,0:T(8,128)(2,1)}, bf16[4,4,48,1536]{3,2,1,0:T(8,128)(2,1)}, u32[]{:S(2)}, u32[]{:S(2)}) collective-permute-start(bf16[4,4,48,1536]{3,2,1,0:T(8,128)(2,1)} %dynamic-slice_bitcast_fusion.2), channel_id=1, source_target_pairs={{0,4},{4,0},{8,12},{12,8},{16,20},{20,16},{24,28},{28,24},{1,5},{5... | collective-permute-start | bytes 7077896 | tf_op jit(solution)/shard_map/ppermute | solution.py:953
  587.4 107.2 %collective-permute-start.63 = (bf16[256,1536]{1,0:T(8,128)(2,1)}, bf16[256,1536]{1,0:T(8,128)(2,1)}, u32[]{:S(2)}, u32[]{:S(2)}) collective-permute-start(bf16[256,1536]{1,0:T(8,128)(2,1)} %add_convert_fusion.4), channel_id=1, source_target_pairs={{0,1},{1,0},{2,3},{3,2},{4,5},{5,4},{6,7},{7,6},{8,9},{9,8},{10,11... | collective-permute-start | bytes 2359304 | tf_op jit(solution)/shard_map/ppermute | solution.py:953
  590.4 104.1 %collective-permute-start.62 = (bf16[256,1536]{1,0:T(8,128)(2,1)}, bf16[256,1536]{1,0:T(8,128)(2,1)}, u32[]{:S(2)}, u32[]{:S(2)}) collective-permute-start(bf16[256,1536]{1,0:T(8,128)(2,1)} %add_convert_fusion.5), channel_id=1, source_target_pairs={{0,2},{1,3},{2,0},{3,1},{4,6},{5,7},{6,4},{7,5},{8,10},{9,11},{10,... | collective-permute-start | bytes 2359304 | tf_op jit(solution)/shard_map/ppermute | solution.py:953
  607.0 87.6 %collective-permute-start.61 = (bf16[4,3,48,1536]{3,2,1,0:T(8,128)(2,1)}, bf16[4,3,48,1536]{3,2,1,0:T(8,128)(2,1)}, u32[]{:S(2)}, u32[]{:S(2)}) collective-permute-start(bf16[4,3,48,1536]{3,2,1,0:T(8,128)(2,1)} %pad_maximum_fusion.5), channel_id=1, source_target_pairs={{0,3},{1,2},{2,1},{3,0},{4,7},{5,6},{6,5},{7,4},{8,11},{9,10},{10,... | collective-permute-start | bytes 5308424 | tf_op jit(solution)/shard_map/ppermute | solution.py:953
  609.1 177.8 %reduce-scatter.12.cloned.1.call-start = ((), (), s32[]{:S(2)}) async-start(), calls=%async_computation.11 | async-start | bytes 3981312 | tf_op jit(solution)/shard_map/reduce_scatter | solution.py:1257
  611.0 83.6 %collective-permute-start.60 = (bf16[4,3,48,1536]{3,2,1,0:T(8,128)(2,1)S(1)}, bf16[4,3,48,1536]{3,2,1,0:T(8,128)(2,1)S(1)}, u32[]{:S(2)}, u32[]{:S(2)}) collective-permute-start(bf16[4,3,48,1536]{3,2,1,0:T(8,128)(2,1)S(1)} %pad_maximum_fusion.4), channel_id=1, source_target_pairs={{0,2},{1,3},{2,0},{3,1},{4,6},{5,7},{6,4},{7,5},{8,10},{9,11},{10,... | collective-permute-start | bytes 5308424 | tf_op jit(solution)/shard_map/ppermute | solution.py:953
  611.9 83.9 %collective-permute-start.59 = (bf16[4,3,48,1536]{3,2,1,0:T(8,128)(2,1)S(1)}, bf16[4,3,48,1536]{3,2,1,0:T(8,128)(2,1)}, u32[]{:S(2)}, u32[]{:S(2)}) collective-permute-start(bf16[4,3,48,1536]{3,2,1,0:T(8,128)(2,1)S(1)} %pad_maximum_fusion.3), channel_id=1, source_target_pairs={{0,1},{1,0},{2,3},{3,2},{4,5},{5,4},{6,7},{7,6},{8,9},{9,8},{10,11... | collective-permute-start | bytes 5308424 | tf_op jit(solution)/shard_map/ppermute | solution.py:953
  709.1 154.2 %reduce-scatter.14.cloned.1.call-start = ((), (), s32[]{:S(2)}) async-start(), calls=%async_computation.12 | async-start | bytes 2211840 | tf_op jit(solution)/shard_map/reduce_scatter | solution.py:1272
  712.9 23.5 %collective-permute-start.64 = (bf16[48,3072]{1,0:T(8,128)(2,1)}, bf16[48,3072]{1,0:T(8,128)(2,1)S(1)}, u32[]{:S(2)}, u32[]{:S(2)}) collective-permute-start(bf16[48,3072]{1,0:T(8,128)(2,1)} %get-tuple-element.402), channel_id=1, source_target_pairs={{0,1},{1,0},{2,3},{3,2},{4,5},{5,4},{6,7},{7,6},{8,9},{9,8},{10,11... | collective-permute-start | bytes 884744 | tf_op jit(solution)/shard_map/ppermute | solution.py:953
  714.2 22.2 %collective-permute-start.65 = (bf16[48,3072]{1,0:T(8,128)(2,1)}, bf16[48,3072]{1,0:T(8,128)(2,1)}, u32[]{:S(2)}, u32[]{:S(2)}) collective-permute-start(bf16[48,3072]{1,0:T(8,128)(2,1)} %get-tuple-element.401), channel_id=1, source_target_pairs={{0,2},{1,3},{2,0},{3,1},{4,6},{5,7},{6,4},{7,5},{8,10},{9,11},{10,... | collective-permute-start | bytes 884744 | tf_op jit(solution)/shard_map/ppermute | solution.py:953
  715.6 20.8 %collective-permute-start.66 = (bf16[48,3072]{1,0:T(8,128)(2,1)}, bf16[48,3072]{1,0:T(8,128)(2,1)}, u32[]{:S(2)}, u32[]{:S(2)}) collective-permute-start(bf16[48,3072]{1,0:T(8,128)(2,1)} %get-tuple-element.400), channel_id=1, source_target_pairs={{0,3},{1,2},{2,1},{3,0},{4,7},{5,6},{6,5},{7,4},{8,11},{9,10},{10,... | collective-permute-start | bytes 884744 | tf_op jit(solution)/shard_map/ppermute | solution.py:953
  749.3 20.6 %collective-permute-start.73 = (bf16[256,1536]{1,0:T(8,128)(2,1)S(1)}, bf16[256,1536]{1,0:T(8,128)(2,1)}, u32[]{:S(2)}, u32[]{:S(2)}) collective-permute-start(bf16[256,1536]{1,0:T(8,128)(2,1)S(1)} %get-tuple-element.368), channel_id=1, source_target_pairs={{0,1},{1,0},{2,3},{3,2},{4,5},{5,4},{6,7},{7,6},{8,9},{9,8},{10,11... | collective-permute-start | bytes 2359304 | tf_op jit(solution)/shard_map/ppermute | solution.py:953
  750.5 20.5 %collective-permute-start.74 = (bf16[256,1536]{1,0:T(8,128)(2,1)S(1)}, bf16[256,1536]{1,0:T(8,128)(2,1)}, u32[]{:S(2)}, u32[]{:S(2)}) collective-permute-start(bf16[256,1536]{1,0:T(8,128)(2,1)S(1)} %get-tuple-element.367), channel_id=1, source_target_pairs={{0,2},{1,3},{2,0},{3,1},{4,6},{5,7},{6,4},{7,5},{8,10},{9,11},{10,... | collective-permute-start | bytes 2359304 | tf_op jit(solution)/shard_map/ppermute | solution.py:953
  751.7 34.2 %collective-permute-start.75 = (bf16[256,1536]{1,0:T(8,128)(2,1)S(1)}, bf16[256,1536]{1,0:T(8,128)(2,1)S(1)}, u32[]{:S(2)}, u32[]{:S(2)}) collective-permute-start(bf16[256,1536]{1,0:T(8,128)(2,1)S(1)} %get-tuple-element.366), channel_id=1, source_target_pairs={{0,1},{1,0},{2,3},{3,2},{4,5},{5,4},{6,7},{7,6},{8,9},{9,8},{10,11... | collective-permute-start | bytes 2359304 | tf_op jit(solution)/shard_map/ppermute | solution.py:953
  752.8 34.0 %collective-permute-start.76 = (bf16[256,1536]{1,0:T(8,128)(2,1)S(1)}, bf16[256,1536]{1,0:T(8,128)(2,1)}, u32[]{:S(2)}, u32[]{:S(2)}) collective-permute-start(bf16[256,1536]{1,0:T(8,128)(2,1)S(1)} %get-tuple-element.365), channel_id=1, source_target_pairs={{0,2},{1,3},{2,0},{3,1},{4,6},{5,7},{6,4},{7,5},{8,10},{9,11},{10,... | collective-permute-start | bytes 2359304 | tf_op jit(solution)/shard_map/ppermute | solution.py:953
  802.1 20.0 %collective-permute-start.84 = (bf16[256,1536]{1,0:T(8,128)(2,1)S(1)}, bf16[256,1536]{1,0:T(8,128)(2,1)S(1)}, u32[]{:S(2)}, u32[]{:S(2)}) collective-permute-start(bf16[256,1536]{1,0:T(8,128)(2,1)S(1)} %get-tuple-element.364), channel_id=1, source_target_pairs={{0,2},{1,3},{2,0},{3,1},{4,6},{5,7},{6,4},{7,5},{8,10},{9,11},{10,... | collective-permute-start | bytes 2359304 | tf_op jit(solution)/shard_map/ppermute | solution.py:953
  803.5 19.7 %collective-permute-start.85 = (bf16[256,1536]{1,0:T(8,128)(2,1)S(1)}, bf16[256,1536]{1,0:T(8,128)(2,1)S(1)}, u32[]{:S(2)}, u32[]{:S(2)}) collective-permute-start(bf16[256,1536]{1,0:T(8,128)(2,1)S(1)} %get-tuple-element.363), channel_id=1, source_target_pairs={{0,1},{1,0},{2,3},{3,2},{4,5},{5,4},{6,7},{7,6},{8,9},{9,8},{10,11... | collective-permute-start | bytes 2359304 | tf_op jit(solution)/shard_map/ppermute | solution.py:953
  825.2 17.7 %collective-permute-start.86 = (f32[5,48]{1,0:T(8,128)S(1)}, f32[5,48]{1,0:T(8,128)S(1)}, u32[]{:S(2)}, u32[]{:S(2)}) collective-permute-start(f32[5,48]{1,0:T(8,128)S(1)} %convolution_multiply_fusion), channel_id=1, source_target_pairs={{0,1},{1,0},{2,3},{3,2},{4,5},{5,4},{6,7},{7,6},{8,9},{9,8},{10,11... | collective-permute-start | bytes 2888 | tf_op jit(solution)/shard_map/ppermute | solution.py:953
  826.2 18.5 %collective-permute-start.87 = (f32[5,48]{1,0:T(8,128)S(1)}, f32[5,48]{1,0:T(8,128)S(1)}, u32[]{:S(2)}, u32[]{:S(2)}) collective-permute-start(f32[5,48]{1,0:T(8,128)S(1)} %convolution_multiply_fusion), channel_id=1, source_target_pairs={{0,2},{1,3},{2,0},{3,1},{4,6},{5,7},{6,4},{7,5},{8,10},{9,11},{10,... | collective-permute-start | bytes 2888 | tf_op jit(solution)/shard_map/ppermute | solution.py:953
  827.0 17.7 %collective-permute-start.88 = (f32[5,48]{1,0:T(8,128)S(1)}, f32[5,48]{1,0:T(8,128)S(1)}, u32[]{:S(2)}, u32[]{:S(2)}) collective-permute-start(f32[5,48]{1,0:T(8,128)S(1)} %convolution_multiply_fusion), channel_id=1, source_target_pairs={{0,3},{1,2},{2,1},{3,0},{4,7},{5,6},{6,5},{7,4},{8,11},{9,10},{10,... | collective-permute-start | bytes 2888 | tf_op jit(solution)/shard_map/ppermute | solution.py:953
  830.9 13.9 %collective-permute-start.89 = (bf16[48,2688]{1,0:T(8,128)(2,1)}, bf16[48,2688]{1,0:T(8,128)(2,1)S(1)}, u32[]{:S(2)}, u32[]{:S(2)}) collective-permute-start(bf16[48,2688]{1,0:T(8,128)(2,1)} %get-tuple-element.420), channel_id=1, source_target_pairs={{0,1},{1,0},{2,3},{3,2},{4,5},{5,4},{6,7},{7,6},{8,9},{9,8},{10,11... | collective-permute-start | bytes 774152 | tf_op jit(solution)/shard_map/ppermute | solution.py:953
  831.9 12.9 %collective-permute-start.90 = (bf16[48,2688]{1,0:T(8,128)(2,1)}, bf16[48,2688]{1,0:T(8,128)(2,1)S(1)}, u32[]{:S(2)}, u32[]{:S(2)}) collective-permute-start(bf16[48,2688]{1,0:T(8,128)(2,1)} %get-tuple-element.419), channel_id=1, source_target_pairs={{0,2},{1,3},{2,0},{3,1},{4,6},{5,7},{6,4},{7,5},{8,10},{9,11},{10,... | collective-permute-start | bytes 774152 | tf_op jit(solution)/shard_map/ppermute | solution.py:953
  (170 other events, 1533.0 us)
Sparse Core Ops, SparseCore 0:
  22.2 100.9 all-gather.3
  126.6 106.6 all-gather.5
  235.6 88.8 all-gather.7
  492.5 52.4 reduce-scatter.5
  547.2 97.8 reduce-scatter.7
  647.2 53.3 reduce-scatter.9
  709.2 41.9 reduce-scatter.11
  797.8 39.5 reduce-scatter.13

commit v4 on v3

--- a/solution.py
+++ b/solution.py
@@ -993,9 +993,12 @@
         near = [swap(value, "seq", 1), swap(value, "seq", 2)]
         return [value] + near, near
 
+    def opposite_halves(near):
+        half = near[0].shape[0] // 2
+        return [swap(near[1][:half], "seq", 1), swap(near[0][half:], "seq", 2)]
+
     def opposite(near):
-        half = near[0].shape[0] // 2
-        return jnp.concatenate([swap(near[1][:half], "seq", 1), swap(near[0][half:], "seq", 2)])
+        return jnp.concatenate(opposite_halves(near))
 
     def spread_row(value):
         both = jnp.stack([value, swap(value, "row", 1)])
@@ -1109,7 +1112,7 @@
     qkv, *got = lax.optimization_barrier((qkv, *kv_slots, *glu_slots))
     kv_slots, glu_slots = got[:seqs], got[seqs:]
     glu_w = lax.all_gather(natural(glu_slots).reshape(seqs * depth, -1), "row", axis=0, tiled=True)
-    mixed_heads, lse = attend(qkv, qkv, qkv, 0, pairs, 2 * pairs, pairs, 512, masks)
+    mixed_heads, lse = attend(qkv, qkv, qkv, 0, pairs, 2 * pairs, pairs, LENGTH, masks)
     mixed_slots = slots(mixed_heads)
     mixed_got = [mixed_slots[0]] + [swap(mixed_slots[j], "seq", j) for j in range(1, seqs)]
     attn_mixed = side_by_side(mixed_got)
@@ -1124,21 +1127,25 @@
     cross_kv = side_by_side(kv_slots)
     all_pairs = D // PAIR
     cross_mixed, cross_lse = attend(cross_q, cross_kv, cross_kv, 0, 0, all_pairs, all_pairs, frames_here)
+    cross_mixed, cot_slots = lax.optimization_barrier((cross_mixed, cot_slots))
     after_cross = after_attn + dot(cross_mixed, crossout_w)
 
     normed_f, inv_f = layer_stats(after_cross)
     ffn_in = (normed_f * (1.0 + scale_ffn) + shift_ffn).astype(low)
     units = FF // seqs
     ffn_slots, near = spread_two(ffn_in)
-    calls = [slice(0, 1), slice(1, 3), slice(3, 4)] if seqs == 4 else [slice(0, seqs)]
+    if near is not None:
+        far_halves = (opposite_halves(near), opposite_halves(cot_slots[1:]))
+    calls = [slice(0, 3), slice(3, 4)] if seqs == 4 else [slice(0, seqs)]
     kept, ffn_back, ffn_parts, dgate_ffn = None, [], [], 0.0
     scale_row = jnp.broadcast_to(row_scale[None], (1, D))
     for call in calls:
-        if call.start == 1:
-            near, kept = lax.optimization_barrier((near, kept))
-            cot_near, near = lax.optimization_barrier((cot_slots[1:], near))
-            ffn_slots = [ffn_in, *near, opposite(near)]
-            cot_slots = [*cot_slots, opposite(cot_near)]
+        if call.start == 3:
+            far_halves, kept = lax.optimization_barrier((far_halves, kept))
+            ffn_slots, cot_slots = [
+                [*slots_here, jnp.concatenate(halves)]
+                for slots_here, halves in zip((ffn_slots, cot_slots), far_halves)
+            ]
         *kept, back, out, dgate = feed(
             ffn_slots[call], cot_slots[call], gate_ffn, scale_row, glu_w, first_w, call.start, seqs, kept
         )
@@ -1178,9 +1185,10 @@
     grad_glu = dot_left_t(ffn_all, grad_gate_up).astype(low)
     grad_down = dot_left_t(hidden_all, grad_ffn_all).astype(low)
     grad_glu, *ffn_back_near = lax.optimization_barrier((grad_glu, *ffn_back_near))
-    ffn_back_far = returned_far(ffn_back, ffn_back_near)
+    ffn_back_far, ffn_back_own = returned_far(ffn_back, ffn_back_near)
+    ffn_back_far, grad_down = lax.optimization_barrier((ffn_back_far, grad_down))
     grad_ffn_in, grad_glu, grad_down, *ffn_parts = lax.optimization_barrier(
-        (returned_total(*ffn_back_far), grad_glu, grad_down, *ffn_parts)
+        (returned_total(ffn_back_far, ffn_back_own), grad_glu, grad_down, *ffn_parts)
     )
     grad_glu = lax.psum_scatter(grad_glu, "row", scatter_dimension=0, tiled=True)
     grad_down = lax.psum_scatter(grad_down, "row", scatter_dimension=0, tiled=True)
@@ -1244,7 +1252,7 @@
     grad_projected = jnp.concatenate(
         attend_back(
             qkv, qkv, qkv, grad_heads, mixed_heads, lse,
-            0, pairs, 2 * pairs, pairs, 512, 512, masks, tables,
+            0, pairs, 2 * pairs, pairs, LENGTH // 2, 512, masks, tables,
         ),
         axis=1,
     )
@@ -1265,9 +1273,9 @@
     attn_back = slots(attn_back)
     attn_near = returned_near(attn_back)
 
-    sums_list, attn_near, grad_qkv = lax.optimization_barrier(
-        (spread_row(own_sums), attn_near, grad_qkv)
-    )
+    sums_list = spread_row(own_sums)
+    ffn_far, sums_list[1] = lax.optimization_barrier((ffn_far, sums_list[1]))
+    sums_list, attn_near, grad_qkv = lax.optimization_barrier((sums_list, attn_near, grad_qkv))
     wide = sum(g.astype(jnp.float32) for g in after(tuple(wide_got), grad_qkv)).astype(low)
     grad_wide = lax.psum_scatter(
         wide,

time: 877 us -> 864 us (0.985)
  Pallas kernels: 276 us -> 255 us
    ppermute x96, waiting for transfers between devices: 121 us -> 169 us  [swap(): return lax.ppermute(value, axis, [(i, i ^ j) for i in range(sizes[axis])])]
    all_gather x1, waiting for transfers between devices: 44.3 us -> 0.01 us  [on_device_split(): lax.all_gather(natural(glu_slots).reshape(seqs * depth, -1), 'row', axis=...]
    pallas_call x2, Pallas kernels: 56.4 us -> 45 us  [attend(): pl.pallas_call(functools.partial(attend_kernel, masked), grid=(pairs, cou...]
    pallas_call x3 -> x2, Pallas kernels: 88.3 us -> 81.3 us  [feed(): pl.pallas_call(functools.partial(feed_kernel, per_slot, slots, chunk, kep...]
    unnamed x299 -> x295, local copies, waits for them, and re-layouts: 19.5 us -> 23.1 us
  transfers between devices with their start and end apart: 104 -> 104, of which waited for: 39 -> 42; matrix products, arithmetic and copies ran while one was open for 29% -> 29% of each run, Pallas kernels for 32% -> 27%
where the time goes in v4:
time: 864 us; the launch traced here: 859 us
  Pallas kernels  255 us (30%)
  waiting for transfers between devices  173 us (20%)
  starting transfers between devices  109 us (13%)
  matrix products  104 us (12%)
  other arithmetic  99.1 us (11%)
  local copies, waits for them, and re-layouts  87.6 us (10%)
  between operations  32.3 us (4%)
    ppermute x96, waiting for transfers between devices, swap(): return lax.ppermute(value, axis, [(i, i ^ j) for i in range(sizes[axis])])  169 us
    ppermute x96, starting transfers between devices, swap(): return lax.ppermute(value, axis, [(i, i ^ j) for i in range(sizes[axis])])  108 us
    pallas_call x2, Pallas kernels, attend_back(): pl.pallas_call(functools.partial(attend_back_kernel, masked, chunk), grid...  85 us
    pallas_call x2, Pallas kernels, feed(): pl.pallas_call(functools.partial(feed_kernel, per_slot, slots, chunk, kep...  81.3 us
    dot_general x6, matrix products, dot_left_t(): jnp.einsum('fi,fj->ij', left, right, preferred_element_type=jnp.float32)  63.8 us
    pallas_call x2, Pallas kernels, attend(): pl.pallas_call(functools.partial(attend_kernel, masked), grid=(pairs, cou...  45 us
    unnamed x295, local copies, waits for them, and re-layouts  23.1 us
    dot_general x3, matrix products, dot_right_t(): jnp.einsum('fj,ij->fi', left, right, preferred_element_type=jnp.float32)  19.5 us
  transfers between devices with their start and end apart: 104, of which 42 were waited for; matrix products, arithmetic and copies ran while one was open for 29% of the time, Pallas kernels for 27%

profile of v4, /device:TPU:0, one launch (start us, length us, event | category | flops | bytes accessed | tf_op | source)
XLA Modules:
  0.0 859.4 jit_solution(8857298473235367400)
XLA Ops:
  9.4 4.0 collective-permute-start.2
  14.1 3.5 collective-permute-done.2
  17.6 2.8 collective-permute-done.1
  36.4 7.8 collective-permute-done.6
  44.3 6.6 collective-permute-done.7
  54.4 5.5 collective-permute-done.9
  59.9 4.4 collective-permute-start.10
  65.1 5.6 collective-permute-done.10
  102.7 2.6 pad_maximum_fusion.6.refs_3_
  110.1 3.6 collective-permute-start.22
  142.9 2.7 collective-permute-done.29
  147.4 17.3 %project.1 = (bf16[2048,1536]{1,0:T(8,128)(2,1)}, bf16[2048,1152]{1,0:T(8,128)(2,1)}) custom-call(bf16[512,1536]{1,0:T(8,128)(2,1)S(1)} %bitcast.300, bf16[512,1536]{1,0:T(8,128)(2,1)} %collective-permute-done.11.refs_1_, bf16[512,1536]{1,0:T(8,128)(2,1)} %collective-permute-done.12.refs_2_, bf16[512,1536]{1,0:T(8,128)(2,1)} %pad_maximum_fusion.6.refs_3_, ...), custom_call_target="tpu_custom_call" | custom-call | flops 7247757312 | bytes 20840448 | tf_op jit(solution)/shard_map/project/pallas_call | solution.py:94
  170.0 35.3 %attend.2 = (bf16[2048,384]{1,0:T(8,128)(2,1)S(1)}, f32[3,2,2048]{2,1,0:T(2,128)S(1)}) custom-call(bf16[2048,1152]{1,0:T(8,128)(2,1)} %get-tuple-element.188.refs_0_.refs_1_.refs_2_, bf16[2048,1152]{1,0:T(8,128)(2,1)} %get-tuple-element.188.refs_0_.refs_1_.refs_2_, bf16[2048,1152]{1,0:T(8,128)(2,1)} %get-tuple-element.188.refs_0_.refs_1_.refs_2_, ...), custom_call_target="tpu_custom_call" | custom-call | flops 25769803776 | bytes 6291456 | tf_op jit(solution)/shard_map/attend/pallas_call | solution.py:209
  220.3 3.2 collective-permute-done.32
  223.5 8.7 %collective-permute-done.34 = bf16[512,384]{1,0:T(8,128)(2,1)} collective-permute-done((bf16[512,384]{1,0:T(8,128)(2,1)}, bf16[512,384]{1,0:T(8,128)(2,1)}, u32[]{:S(2)}, u32[]{:S(2)}) %collective-permute-start.34) | collective-permute-done | bytes 393248 | tf_op jit(solution)/shard_map/ppermute | solution.py:953
  235.2 2.8 all-gather.6.cloned.1.call-done
  238.0 8.0 fusion.75
  250.6 5.0 fusion.30.refs_0_
  255.6 9.7 %attend.3 = (bf16[512,1536]{1,0:T(8,128)(2,1)S(1)}, f32[12,2,512]{2,1,0:T(2,128)S(1)}) custom-call(bf16[512,1536]{1,0:T(8,128)(2,1)S(1)} %fusion.30.refs_0_, bf16[128,3072]{1,0:T(8,128)(2,1)S(1)} %copy-done.9, bf16[128,3072]{1,0:T(8,128)(2,1)S(1)} %copy-done.9), custom_call_target="tpu_custom_call" | custom-call | flops 1610612736 | bytes 3932160 | tf_op jit(solution)/shard_map/attend/pallas_call | solution.py:209
  265.3 17.3 %collective-permute-done.35.refs_4_ = bf16[512,1536]{1,0:T(8,128)(2,1)S(1)} collective-permute-done((bf16[512,1536]{1,0:T(8,128)(2,1)S(1)}, bf16[512,1536]{1,0:T(8,128)(2,1)S(1)}, u32[]{:S(2)}, u32[]{:S(2)}) %collective-permute-start.35) | collective-permute-done | bytes 1572896 | tf_op jit(solution)/shard_map/ppermute | solution.py:953
  283.5 4.6 fusion.86
  297.6 29.5 %collective-permute-done.38.refs_2_ = bf16[512,1536]{1,0:T(8,128)(2,1)S(1)} collective-permute-done((bf16[512,1536]{1,0:T(8,128)(2,1)S(1)}, bf16[512,1536]{1,0:T(8,128)(2,1)S(1)}, u32[]{:S(2)}, u32[]{:S(2)}) %collective-permute-start.38) | collective-permute-done | bytes 1572896 | tf_op jit(solution)/shard_map/ppermute | solution.py:953
  337.0 57.8 %feed.2 = (bf16[2048,1536]{1,0:T(8,128)(2,1)}, bf16[2048,1536]{1,0:T(8,128)(2,1)}, bf16[2048,1536]{1,0:T(8,128)(2,1)}, bf16[2048,3072]{1,0:T(8,128)(2,1)}, bf16[...) custom-call(bf16[512,1536]{1,0:T(8,128)(2,1)S(1)} %copy-done.5, ...), custom_call_target="tpu_custom_call" | custom-call | flops 43486543872 | bytes 56623104 | tf_op jit(solution)/shard_map/feed/pallas_call | solution.py:432
  394.8 2.6 pad_maximum_fusion.10.refs_1_
  397.5 2.6 pad_maximum_fusion.9.refs_0_
  400.1 23.6 %feed.3 = (bf16[2048,1536]{1,0:T(8,128)(2,1)}, bf16[2048,1536]{1,0:T(8,128)(2,1)}, bf16[2048,1536]{1,0:T(8,128)(2,1)}, bf16[2048,3072]{1,0:T(8,128)(2,1)}, bf16[...) custom-call(bf16[512,1536]{1,0:T(8,128)(2,1)} %pad_maximum_fusion.9., ...), custom_call_target="tpu_custom_call", output_to_operand_aliasing={{0}: (6, {}), {1}: (7, {}), {2}: (8, {}), {3}: (9, {})} | custom-call | flops 14495514624 | bytes 28311552 | tf_op jit(solution)/shard_map/feed/pallas_call | solution.py:432
  425.9 3.4 fusion.78
  431.6 24.2 %convolution_convert_fusion = bf16[1536,3072]{1,0:T(8,128)(2,1)} fusion(bf16[2048,1536]{1,0:T(8,128)(2,1)S(1)} %copy-done.125, bf16[2048,3072]{1,0:T(8,128)(2,1)} %get-tuple-element.219), kind=kOutput, calls=%fused_computation.1 | convolution fusion | flops 19332071424 | bytes 28311552 | tf_op jit(solution)/shard_map/fi,fj->ij/dot_general | solution.py:1026
  455.8 2.8 collective-permute-done.45
  459.9 3.4 add_convert_fusion.6
  465.3 15.5 %convolution_convert_fusion.5 = bf16[1536,1536]{1,0:T(8,128)(2,1)} fusion(bf16[2048,1536]{1,0:T(8,128)(2,1)} %get-tuple-element.224, bf16[2048,1536]{1,0:T(8,128)(2,1)} %get-tuple-element.225), kind=kOutput, calls=%fused_computation.6 | convolution fusion | flops 9666035712 | bytes 17301504 | tf_op jit(solution)/shard_map/fi,fj->ij/dot_general | solution.py:1026
  480.8 4.6 fusion.77
  485.4 2.9 convert_add_fusion.6
  490.9 2.8 fusion.79
  505.1 7.5 fusion.33.refs_3_
  512.6 12.2 %attend_back.2 = (bf16[512,1536]{1,0:T(8,128)(2,1)S(1)}, f32[128,1536]{1,0:T(8,128)S(1)}, f32[128,1536]{1,0:T(8,128)S(1)}) custom-call(bf16[512,1536]{1,0:T(8,128)(2,1)} %copy-done.23, bf16[128,3072]{1,0:T(8,128)(2,1)S(1)} %copy-done.10, bf16[128,3072]{1,0:T(8,128)(2,1)S(1)} %copy-done.10, bf16[512,1536]{1,0:T(8,128)(2,1)} %fusion.33.refs_3_, ...), custom_call_target="tpu_custom_call" | custom-call | flops 4026531840 | bytes 7864320 | tf_op jit(solution)/shard_map/attend_back/pallas_call | solution.py:306
  524.8 2.8 collective-permute-done.51
  528.8 5.9 multiply_reduce_fusion
  536.3 6.1 fusion.27
  546.2 2.7 collective-permute-start.55
  548.9 6.5 collective-permute-done.53
  555.4 4.8 convolution_convert_fusion.2
  564.3 2.9 convolution_convert_fusion.3
  571.5 2.9 convolution_convert_fusion.4
  579.7 3.9 text_product.1
  583.6 2.6 add_convert_fusion.4
  591.7 4.0 fusion.44
  595.7 3.9 fusion.43
  599.6 4.0 fusion.42
  605.0 2.8 collective-permute-start.61
  611.2 72.8 %attend_back.3 = (bf16[2048,384]{1,0:T(8,128)(2,1)}, bf16[2048,384]{1,0:T(8,128)(2,1)}, bf16[2048,384]{1,0:T(8,128)(2,1)}) custom-call(bf16[2048,1152]{1,0:T(8,128)(2,1)} %get-tuple-element.188.refs_0_.refs_1_.refs_2_, bf16[2048,1152]{1,0:T(8,128)(2,1)} %get-tuple-element.188.refs_0_.refs_1_.refs_2_, ...), custom_call_target="tpu_custom_call" | custom-call | flops 64424509440 | bytes 12582912 | tf_op jit(solution)/shard_map/attend_back/pallas_call | solution.py:306
  686.6 3.6 pad_maximum_fusion.refs_4_
  691.4 13.6 %convolution_convert_fusion.1 = bf16[1536,1152]{1,0:T(8,128)(2,1)} fusion(bf16[2048,1536]{1,0:T(8,128)(2,1)} %get-tuple-element.265, bf16[2048,1152]{1,0:T(8,128)(2,1)} %pad_maximum_fusion.refs_4_), kind=kOutput, calls=%fused_computation.2 | convolution fusion | flops 7249526784 | bytes 14548992 | tf_op jit(solution)/shard_map/fi,fj->ij/dot_general | solution.py:1026
  712.8 15.8 %project_back.1 = (bf16[2048,1536]{1,0:T(8,128)(2,1)}, f32[2,1536]{1,0:T(2,128)S(1)}) custom-call(bf16[512,1536]{1,0:T(8,128)(2,1)S(1)} %bitcast.301, bf16[512,1536]{1,0:T(8,128)(2,1)} %collective-permute-done.11.refs_1_, bf16[512,1536]{1,0:T(8,128)(2,1)} %collective-permute-done.12.refs_2_, bf16[512,1536]{1,0:T(8,128)(2,1)} %pad_maximum_fusion.6.refs_3_, ...), custom_call_target="tpu_custom_call" | custom-call | flops 7247757312 | bytes 20840448 | tf_op jit(solution)/shard_map/project_back/pallas_call | solution.py:141
  742.0 4.1 convert_add_fusion.4
  750.5 5.1 collective-permute-done.71
  756.2 4.0 collective-permute-done.70
  760.8 13.8 %collective-permute-done.75 = bf16[256,1536]{1,0:T(8,128)(2,1)S(1)} collective-permute-done((bf16[256,1536]{1,0:T(8,128)(2,1)S(1)}, bf16[256,1536]{1,0:T(8,128)(2,1)S(1)}, u32[]{:S(2)}, u32[]{:S(2)}) %collective-permute-start.75) | collective-permute-done | bytes 786464 | tf_op jit(solution)/shard_map/ppermute | solution.py:953
  783.0 4.8 add_convert_fusion
  798.8 4.4 collective-permute-start.81
  805.3 7.3 collective-permute-done.84
  828.1 4.1 fusion.23
  834.8 5.7 collective-permute-done.91
  842.2 4.3 collective-permute-start.95
  (678 shorter events, 251.8 us)
Async XLA Ops:
  7.2 131.9 %all-gather.4.cloned.1.call-start = ((), (), s32[]{:S(2)}) async-start(), calls=%async_computation.5 | async-start | bytes 10616832 | tf_op jit(solution)/shard_map/all_gather | solution.py:1055
  22.1 215.9 %all-gather.6.cloned.1.call-start = ((), (), s32[]{:S(2)}) async-start(), calls=%async_computation.6 | async-start | bytes 14598144 | tf_op jit(solution)/shard_map/all_gather | solution.py:1074
  31.0 39.7 %collective-permute-start.11 = (bf16[512,1536]{1,0:T(8,128)(2,1)S(1)}, bf16[512,1536]{1,0:T(8,128)(2,1)}, u32[]{:S(2)}, u32[]{:S(2)}) collective-permute-start(bf16[512,1536]{1,0:T(8,128)(2,1)S(1)} %bitcast.298), channel_id=1, source_target_pairs={{0,1},{1,0},{2,3},{3,2},{4,5},{5,4},{6,7},{7,6},{8,9},{9,8},{10,11... | collective-permute-start | bytes 4718600 | tf_op jit(solution)/shard_map/ppermute | solution.py:953
  32.7 38.0 %collective-permute-start.12 = (bf16[512,1536]{1,0:T(8,128)(2,1)S(1)}, bf16[512,1536]{1,0:T(8,128)(2,1)}, u32[]{:S(2)}, u32[]{:S(2)}) collective-permute-start(bf16[512,1536]{1,0:T(8,128)(2,1)S(1)} %bitcast.299), channel_id=1, source_target_pairs={{0,2},{1,3},{2,0},{3,1},{4,6},{5,7},{6,4},{7,5},{8,10},{9,11},{10,... | collective-permute-start | bytes 4718600 | tf_op jit(solution)/shard_map/ppermute | solution.py:953
  70.8 262.8 %all-gather.8.cloned.1.call-start = ((), (), s32[]{:S(2)}) async-start(), calls=%async_computation.7 | async-start | bytes 10616832 | tf_op jit(solution)/shard_map/all_gather | solution.py:1114
  80.8 19.7 %collective-permute-start.15 = (bf16[256,1536]{1,0:T(8,128)(2,1)S(1)}, bf16[256,1536]{1,0:T(8,128)(2,1)}, u32[]{:S(2)}, u32[]{:S(2)}) collective-permute-start(bf16[256,1536]{1,0:T(8,128)(2,1)S(1)} %slice.354), channel_id=1, source_target_pairs={{0,1},{1,0},{2,3},{3,2},{4,5},{5,4},{6,7},{7,6},{8,9},{9,8},{10,11... | collective-permute-start | bytes 2359304 | tf_op jit(solution)/shard_map/ppermute | solution.py:953
  84.5 18.2 %collective-permute-start.16 = (bf16[256,1536]{1,0:T(8,128)(2,1)}, bf16[256,1536]{1,0:T(8,128)(2,1)}, u32[]{:S(2)}, u32[]{:S(2)}) collective-permute-start(bf16[256,1536]{1,0:T(8,128)(2,1)} %slice.355), channel_id=1, source_target_pairs={{0,2},{1,3},{2,0},{3,1},{4,6},{5,7},{6,4},{7,5},{8,10},{9,11},{10,... | collective-permute-start | bytes 2359304 | tf_op jit(solution)/shard_map/ppermute | solution.py:953
  105.7 13.0 %collective-permute-start.19 = (f32[1,9216]{1,0:T(1,128)S(1)}, f32[1,9216]{1,0:T(1,128)}, u32[]{:S(2)}, u32[]{:S(2)}) collective-permute-start(f32[1,9216]{1,0:T(1,128)S(1)} %get-tuple-element.457), channel_id=1, source_target_pairs={{0,12},{4,8},{8,4},{12,0},{16,28},{20,24},{24,20},{28,16},{1,13},{... | collective-permute-start | bytes 110600 | tf_op jit(solution)/shard_map/ppermute | solution.py:953
  136.0 28.7 %collective-permute-start.30 = (bf16[48,3072]{1,0:T(8,128)(2,1)}, bf16[48,3072]{1,0:T(8,128)(2,1)}, u32[]{:S(2)}, u32[]{:S(2)}) collective-permute-start(bf16[48,3072]{1,0:T(8,128)(2,1)} %get-tuple-element.412), channel_id=1, source_target_pairs={{0,2},{1,3},{2,0},{3,1},{4,6},{5,7},{6,4},{7,5},{8,10},{9,11},{10,... | collective-permute-start | bytes 884744 | tf_op jit(solution)/shard_map/ppermute | solution.py:953
  136.4 28.3 %collective-permute-start.31 = (bf16[48,3072]{1,0:T(8,128)(2,1)}, bf16[48,3072]{1,0:T(8,128)(2,1)}, u32[]{:S(2)}, u32[]{:S(2)}) collective-permute-start(bf16[48,3072]{1,0:T(8,128)(2,1)} %get-tuple-element.411), channel_id=1, source_target_pairs={{0,3},{1,2},{2,1},{3,0},{4,7},{5,6},{6,5},{7,4},{8,11},{9,10},{10,... | collective-permute-start | bytes 884744 | tf_op jit(solution)/shard_map/ppermute | solution.py:953
  141.3 23.5 %collective-permute-start.26 = (bf16[128,768]{0,1:T(8,128)(2,1)S(1)}, bf16[128,768]{0,1:T(8,128)(2,1)S(1)}, u32[]{:S(2)}, u32[]{:S(2)}) collective-permute-start(bf16[128,768]{0,1:T(8,128)(2,1)S(1)} %fusion.57), channel_id=1, source_target_pairs={{0,1},{1,0},{2,3},{3,2},{4,5},{5,4},{6,7},{7,6},{8,9},{9,8},{10,11... | collective-permute-start | bytes 589832 | tf_op jit(solution)/shard_map/ppermute | solution.py:953
  142.4 22.3 %collective-permute-start.27 = (bf16[128,768]{0,1:T(8,128)(2,1)S(1)}, bf16[128,768]{0,1:T(8,128)(2,1)S(1)}, u32[]{:S(2)}, u32[]{:S(2)}) collective-permute-start(bf16[128,768]{0,1:T(8,128)(2,1)S(1)} %fusion.57), channel_id=1, source_target_pairs={{0,2},{1,3},{2,0},{3,1},{4,6},{5,7},{6,4},{7,5},{8,10},{9,11},{10,... | collective-permute-start | bytes 589832 | tf_op jit(solution)/shard_map/ppermute | solution.py:953
  145.6 19.2 %collective-permute-start.28 = (bf16[128,768]{0,1:T(8,128)(2,1)S(1)}, bf16[128,768]{0,1:T(8,128)(2,1)S(1)}, u32[]{:S(2)}, u32[]{:S(2)}) collective-permute-start(bf16[128,768]{0,1:T(8,128)(2,1)S(1)} %fusion.57), channel_id=1, source_target_pairs={{0,3},{1,2},{2,1},{3,0},{4,7},{5,6},{6,5},{7,4},{8,11},{9,10},{10,... | collective-permute-start | bytes 589832 | tf_op jit(solution)/shard_map/ppermute | solution.py:953
  167.6 424.1 %reduce-scatter.6.cloned.1.call-start = ((), (), s32[]{:S(2)}) async-start(), calls=%async_computation.8 | async-start | bytes 5308416 | tf_op jit(solution)/shard_map/reduce_scatter | solution.py:1194
  206.6 16.9 %collective-permute-start.32 = (bf16[512,384]{1,0:T(8,128)(2,1)}, bf16[512,384]{1,0:T(8,128)(2,1)}, u32[]{:S(2)}, u32[]{:S(2)}) collective-permute-start(bf16[512,384]{1,0:T(8,128)(2,1)} %get-tuple-element.398), channel_id=1, source_target_pairs={{0,1},{1,0},{2,3},{3,2},{4,5},{5,4},{6,7},{7,6},{8,9},{9,8},{10,11... | collective-permute-start | bytes 1179656 | tf_op jit(solution)/shard_map/ppermute | solution.py:953
  207.6 15.9 %collective-permute-start.33 = (bf16[512,384]{1,0:T(8,128)(2,1)}, bf16[512,384]{1,0:T(8,128)(2,1)}, u32[]{:S(2)}, u32[]{:S(2)}) collective-permute-start(bf16[512,384]{1,0:T(8,128)(2,1)} %get-tuple-element.397), channel_id=1, source_target_pairs={{0,2},{1,3},{2,0},{3,1},{4,6},{5,7},{6,4},{7,5},{8,10},{9,11},{10,... | collective-permute-start | bytes 1179656 | tf_op jit(solution)/shard_map/ppermute | solution.py:953
  208.2 23.9 %collective-permute-start.34 = (bf16[512,384]{1,0:T(8,128)(2,1)}, bf16[512,384]{1,0:T(8,128)(2,1)}, u32[]{:S(2)}, u32[]{:S(2)}) collective-permute-start(bf16[512,384]{1,0:T(8,128)(2,1)} %get-tuple-element.396), channel_id=1, source_target_pairs={{0,3},{1,2},{2,1},{3,0},{4,7},{5,6},{6,5},{7,4},{8,11},{9,10},{10,... | collective-permute-start | bytes 1179656 | tf_op jit(solution)/shard_map/ppermute | solution.py:953
  246.0 36.6 %collective-permute-start.35 = (bf16[512,1536]{1,0:T(8,128)(2,1)S(1)}, bf16[512,1536]{1,0:T(8,128)(2,1)S(1)}, u32[]{:S(2)}, u32[]{:S(2)}) collective-permute-start(bf16[512,1536]{1,0:T(8,128)(2,1)S(1)} %bitcast.320), channel_id=1, source_target_pairs={{0,1},{1,0},{2,3},{3,2},{4,5},{5,4},{6,7},{7,6},{8,9},{9,8},{10,11... | collective-permute-start | bytes 4718600 | tf_op jit(solution)/shard_map/ppermute | solution.py:953
  247.1 36.4 %collective-permute-start.36 = (bf16[512,1536]{1,0:T(8,128)(2,1)S(1)}, bf16[512,1536]{1,0:T(8,128)(2,1)}, u32[]{:S(2)}, u32[]{:S(2)}) collective-permute-start(bf16[512,1536]{1,0:T(8,128)(2,1)S(1)} %bitcast.321), channel_id=1, source_target_pairs={{0,2},{1,3},{2,0},{3,1},{4,6},{5,7},{6,4},{7,5},{8,10},{9,11},{10,... | collective-permute-start | bytes 4718600 | tf_op jit(solution)/shard_map/ppermute | solution.py:953
  289.8 37.3 %collective-permute-start.38 = (bf16[512,1536]{1,0:T(8,128)(2,1)S(1)}, bf16[512,1536]{1,0:T(8,128)(2,1)S(1)}, u32[]{:S(2)}, u32[]{:S(2)}) collective-permute-start(bf16[512,1536]{1,0:T(8,128)(2,1)S(1)} %add_convert_fusion.1.refs_0_), channel_id=1, source_target_pairs={{0,2},{1,3},{2,0},{3,1},{4,6},{5,7},{6,4},{7,5},{8,10},{9,11},{10,... | collective-permute-start | bytes 4718600 | tf_op jit(solution)/shard_map/ppermute | solution.py:953
  291.8 37.9 %collective-permute-start.37 = (bf16[512,1536]{1,0:T(8,128)(2,1)S(1)}, bf16[512,1536]{1,0:T(8,128)(2,1)S(1)}, u32[]{:S(2)}, u32[]{:S(2)}) collective-permute-start(bf16[512,1536]{1,0:T(8,128)(2,1)S(1)} %add_convert_fusion.1.refs_0_), channel_id=1, source_target_pairs={{0,1},{1,0},{2,3},{3,2},{4,5},{5,4},{6,7},{7,6},{8,9},{9,8},{10,11... | collective-permute-start | bytes 4718600 | tf_op jit(solution)/shard_map/ppermute | solution.py:953
  295.8 99.0 %collective-permute-start.41 = (bf16[256,1536]{1,0:T(8,128)(2,1)}, bf16[256,1536]{1,0:T(8,128)(2,1)}, u32[]{:S(2)}, u32[]{:S(2)}) collective-permute-start(bf16[256,1536]{1,0:T(8,128)(2,1)} %slice.371), channel_id=1, source_target_pairs={{0,1},{1,0},{2,3},{3,2},{4,5},{5,4},{6,7},{7,6},{8,9},{9,8},{10,11... | collective-permute-start | bytes 2359304 | tf_op jit(solution)/shard_map/ppermute | solution.py:953
  297.5 97.3 %collective-permute-start.42 = (bf16[256,1536]{1,0:T(8,128)(2,1)}, bf16[256,1536]{1,0:T(8,128)(2,1)}, u32[]{:S(2)}, u32[]{:S(2)}) collective-permute-start(bf16[256,1536]{1,0:T(8,128)(2,1)} %slice.372), channel_id=1, source_target_pairs={{0,2},{1,3},{2,0},{3,1},{4,6},{5,7},{6,4},{7,5},{8,10},{9,11},{10,... | collective-permute-start | bytes 2359304 | tf_op jit(solution)/shard_map/ppermute | solution.py:953
  328.1 66.7 %collective-permute-start.39 = (bf16[256,1536]{1,0:T(8,128)(2,1)}, bf16[256,1536]{1,0:T(8,128)(2,1)}, u32[]{:S(2)}, u32[]{:S(2)}) collective-permute-start(bf16[256,1536]{1,0:T(8,128)(2,1)} %slice.454), channel_id=1, source_target_pairs={{0,1},{1,0},{2,3},{3,2},{4,5},{5,4},{6,7},{7,6},{8,9},{9,8},{10,11... | collective-permute-start | bytes 2359304 | tf_op jit(solution)/shard_map/ppermute | solution.py:953
  331.8 63.0 %collective-permute-start.40 = (bf16[256,1536]{1,0:T(8,128)(2,1)}, bf16[256,1536]{1,0:T(8,128)(2,1)}, u32[]{:S(2)}, u32[]{:S(2)}) collective-permute-start(bf16[256,1536]{1,0:T(8,128)(2,1)} %slice.455), channel_id=1, source_target_pairs={{0,2},{1,3},{2,0},{3,1},{4,6},{5,7},{6,4},{7,5},{8,10},{9,11},{10,... | collective-permute-start | bytes 2359304 | tf_op jit(solution)/shard_map/ppermute | solution.py:953
  424.9 30.9 %collective-permute-start.43 = (bf16[256,1536]{1,0:T(8,128)(2,1)}, bf16[256,1536]{1,0:T(8,128)(2,1)}, u32[]{:S(2)}, u32[]{:S(2)}) collective-permute-start(bf16[256,1536]{1,0:T(8,128)(2,1)} %get-tuple-element.390), channel_id=1, source_target_pairs={{0,1},{1,0},{2,3},{3,2},{4,5},{5,4},{6,7},{7,6},{8,9},{9,8},{10,11... | collective-permute-start | bytes 2359304 | tf_op jit(solution)/shard_map/ppermute | solution.py:953
  425.6 30.2 %collective-permute-start.44 = (bf16[256,1536]{1,0:T(8,128)(2,1)}, bf16[256,1536]{1,0:T(8,128)(2,1)}, u32[]{:S(2)}, u32[]{:S(2)}) collective-permute-start(bf16[256,1536]{1,0:T(8,128)(2,1)} %get-tuple-element.389), channel_id=1, source_target_pairs={{0,2},{1,3},{2,0},{3,1},{4,6},{5,7},{6,4},{7,5},{8,10},{9,11},{10,... | collective-permute-start | bytes 2359304 | tf_op jit(solution)/shard_map/ppermute | solution.py:953
  429.3 29.4 %collective-permute-start.45 = (bf16[256,1536]{1,0:T(8,128)(2,1)}, bf16[256,1536]{1,0:T(8,128)(2,1)}, u32[]{:S(2)}, u32[]{:S(2)}) collective-permute-start(bf16[256,1536]{1,0:T(8,128)(2,1)} %get-tuple-element.379), channel_id=1, source_target_pairs={{0,1},{1,0},{2,3},{3,2},{4,5},{5,4},{6,7},{7,6},{8,9},{9,8},{10,11... | collective-permute-start | bytes 2359304 | tf_op jit(solution)/shard_map/ppermute | solution.py:953
  430.0 29.9 %collective-permute-start.46 = (bf16[256,1536]{1,0:T(8,128)(2,1)}, bf16[256,1536]{1,0:T(8,128)(2,1)}, u32[]{:S(2)}, u32[]{:S(2)}) collective-permute-start(bf16[256,1536]{1,0:T(8,128)(2,1)} %get-tuple-element.378), channel_id=1, source_target_pairs={{0,2},{1,3},{2,0},{3,1},{4,6},{5,7},{6,4},{7,5},{8,10},{9,11},{10,... | collective-permute-start | bytes 2359304 | tf_op jit(solution)/shard_map/ppermute | solution.py:953
  463.2 22.1 %collective-permute-start.47 = (bf16[256,1536]{1,0:T(8,128)(2,1)}, bf16[256,1536]{1,0:T(8,128)(2,1)}, u32[]{:S(2)}, u32[]{:S(2)}) collective-permute-start(bf16[256,1536]{1,0:T(8,128)(2,1)} %get-tuple-element.377), channel_id=1, source_target_pairs={{0,2},{1,3},{2,0},{3,1},{4,6},{5,7},{6,4},{7,5},{8,10},{9,11},{10,... | collective-permute-start | bytes 2359304 | tf_op jit(solution)/shard_map/ppermute | solution.py:953
  464.7 20.6 %collective-permute-start.48 = (bf16[256,1536]{1,0:T(8,128)(2,1)}, bf16[256,1536]{1,0:T(8,128)(2,1)}, u32[]{:S(2)}, u32[]{:S(2)}) collective-permute-start(bf16[256,1536]{1,0:T(8,128)(2,1)} %get-tuple-element.376), channel_id=1, source_target_pairs={{0,1},{1,0},{2,3},{3,2},{4,5},{5,4},{6,7},{7,6},{8,9},{9,8},{10,11... | collective-permute-start | bytes 2359304 | tf_op jit(solution)/shard_map/ppermute | solution.py:953
  490.2 201.2 %reduce-scatter.8.cloned.1.call-start = ((), (), s32[]{:S(2)}) async-start(), calls=%async_computation.9 | async-start | bytes 10616832 | tf_op jit(solution)/shard_map/reduce_scatter | solution.py:1193
  490.8 237.8 %reduce-scatter.10.cloned.1.call-start = ((), (), s32[]{:S(2)}) async-start(), calls=%async_computation.10 | async-start | bytes 5308416 | tf_op jit(solution)/shard_map/reduce_scatter | solution.py:1239
  493.6 31.2 %collective-permute-start.49 = (bf16[256,1536]{1,0:T(8,128)(2,1)}, bf16[256,1536]{1,0:T(8,128)(2,1)}, u32[]{:S(2)}, u32[]{:S(2)}) collective-permute-start(bf16[256,1536]{1,0:T(8,128)(2,1)} %get-tuple-element.388), channel_id=1, source_target_pairs={{0,1},{1,0},{2,3},{3,2},{4,5},{5,4},{6,7},{7,6},{8,9},{9,8},{10,11... | collective-permute-start | bytes 2359304 | tf_op jit(solution)/shard_map/ppermute | solution.py:953
  495.1 29.7 %collective-permute-start.50 = (bf16[256,1536]{1,0:T(8,128)(2,1)}, bf16[256,1536]{1,0:T(8,128)(2,1)}, u32[]{:S(2)}, u32[]{:S(2)}) collective-permute-start(bf16[256,1536]{1,0:T(8,128)(2,1)} %get-tuple-element.387), channel_id=1, source_target_pairs={{0,2},{1,3},{2,0},{3,1},{4,6},{5,7},{6,4},{7,5},{8,10},{9,11},{10,... | collective-permute-start | bytes 2359304 | tf_op jit(solution)/shard_map/ppermute | solution.py:953
  496.9 30.8 %collective-permute-start.51 = (bf16[256,1536]{1,0:T(8,128)(2,1)S(1)}, bf16[256,1536]{1,0:T(8,128)(2,1)}, u32[]{:S(2)}, u32[]{:S(2)}) collective-permute-start(bf16[256,1536]{1,0:T(8,128)(2,1)S(1)} %slice.386), channel_id=1, source_target_pairs={{0,1},{1,0},{2,3},{3,2},{4,5},{5,4},{6,7},{7,6},{8,9},{9,8},{10,11... | collective-permute-start | bytes 2359304 | tf_op jit(solution)/shard_map/ppermute | solution.py:953
  499.7 29.1 %collective-permute-start.52 = (bf16[256,1536]{1,0:T(8,128)(2,1)}, bf16[256,1536]{1,0:T(8,128)(2,1)}, u32[]{:S(2)}, u32[]{:S(2)}) collective-permute-start(bf16[256,1536]{1,0:T(8,128)(2,1)} %slice.387), channel_id=1, source_target_pairs={{0,2},{1,3},{2,0},{3,1},{4,6},{5,7},{6,4},{7,5},{8,10},{9,11},{10,... | collective-permute-start | bytes 2359304 | tf_op jit(solution)/shard_map/ppermute | solution.py:953
  543.7 11.7 %collective-permute-start.53 = (bf16[512,384]{1,0:T(8,128)(2,1)}, bf16[512,384]{1,0:T(8,128)(2,1)}, u32[]{:S(2)}, u32[]{:S(2)}) collective-permute-start(bf16[512,384]{1,0:T(8,128)(2,1)} %get-tuple-element.386), channel_id=1, source_target_pairs={{0,1},{1,0},{2,3},{3,2},{4,5},{5,4},{6,7},{7,6},{8,9},{9,8},{10,11... | collective-permute-start | bytes 1179656 | tf_op jit(solution)/shard_map/ppermute | solution.py:953
  545.9 17.7 %collective-permute-start.54 = (bf16[512,384]{1,0:T(8,128)(2,1)S(1)}, bf16[512,384]{1,0:T(8,128)(2,1)}, u32[]{:S(2)}, u32[]{:S(2)}) collective-permute-start(bf16[512,384]{1,0:T(8,128)(2,1)S(1)} %copy-done.82), channel_id=1, source_target_pairs={{0,2},{1,3},{2,0},{3,1},{4,6},{5,7},{6,4},{7,5},{8,10},{9,11},{10,... | collective-permute-start | bytes 1179656 | tf_op jit(solution)/shard_map/ppermute | solution.py:953
  546.2 24.5 %collective-permute-start.55 = (bf16[512,384]{1,0:T(8,128)(2,1)S(1)}, bf16[512,384]{1,0:T(8,128)(2,1)S(1)}, u32[]{:S(2)}, u32[]{:S(2)}) collective-permute-start(bf16[512,384]{1,0:T(8,128)(2,1)S(1)} %copy-done.81), channel_id=1, source_target_pairs={{0,3},{1,2},{2,1},{3,0},{4,7},{5,6},{6,5},{7,4},{8,11},{9,10},{10,... | collective-permute-start | bytes 1179656 | tf_op jit(solution)/shard_map/ppermute | solution.py:953
  563.6 28.0 %collective-permute-start.58 = (bf16[4,4,48,1536]{3,2,1,0:T(8,128)(2,1)}, bf16[4,4,48,1536]{3,2,1,0:T(8,128)(2,1)}, u32[]{:S(2)}, u32[]{:S(2)}) collective-permute-start(bf16[4,4,48,1536]{3,2,1,0:T(8,128)(2,1)} %dynamic-slice_bitcast_fusion), channel_id=1, source_target_pairs={{0,4},{4,0},{8,12},{12,8},{16,20},{20,16},{24,28},{28,24},{1,5},{5... | collective-permute-start | bytes 7077896 | tf_op jit(solution)/shard_map/ppermute | solution.py:953
  570.7 21.0 %collective-permute-start.57 = (bf16[4,4,48,1536]{3,2,1,0:T(8,128)(2,1)}, bf16[4,4,48,1536]{3,2,1,0:T(8,128)(2,1)}, u32[]{:S(2)}, u32[]{:S(2)}) collective-permute-start(bf16[4,4,48,1536]{3,2,1,0:T(8,128)(2,1)} %dynamic-slice_bitcast_fusion.1), channel_id=1, source_target_pairs={{0,4},{4,0},{8,12},{12,8},{16,20},{20,16},{24,28},{28,24},{1,5},{5... | collective-permute-start | bytes 7077896 | tf_op jit(solution)/shard_map/ppermute | solution.py:953
  577.2 14.4 %collective-permute-start.56 = (bf16[4,4,48,1536]{3,2,1,0:T(8,128)(2,1)}, bf16[4,4,48,1536]{3,2,1,0:T(8,128)(2,1)}, u32[]{:S(2)}, u32[]{:S(2)}) collective-permute-start(bf16[4,4,48,1536]{3,2,1,0:T(8,128)(2,1)} %dynamic-slice_bitcast_fusion.2), channel_id=1, source_target_pairs={{0,4},{4,0},{8,12},{12,8},{16,20},{20,16},{24,28},{28,24},{1,5},{5... | collective-permute-start | bytes 7077896 | tf_op jit(solution)/shard_map/ppermute | solution.py:953
  586.2 103.9 %collective-permute-start.63 = (bf16[256,1536]{1,0:T(8,128)(2,1)}, bf16[256,1536]{1,0:T(8,128)(2,1)}, u32[]{:S(2)}, u32[]{:S(2)}) collective-permute-start(bf16[256,1536]{1,0:T(8,128)(2,1)} %add_convert_fusion.4), channel_id=1, source_target_pairs={{0,1},{1,0},{2,3},{3,2},{4,5},{5,4},{6,7},{7,6},{8,9},{9,8},{10,11... | collective-permute-start | bytes 2359304 | tf_op jit(solution)/shard_map/ppermute | solution.py:953
  589.0 101.2 %collective-permute-start.62 = (bf16[256,1536]{1,0:T(8,128)(2,1)}, bf16[256,1536]{1,0:T(8,128)(2,1)}, u32[]{:S(2)}, u32[]{:S(2)}) collective-permute-start(bf16[256,1536]{1,0:T(8,128)(2,1)} %add_convert_fusion.5), channel_id=1, source_target_pairs={{0,2},{1,3},{2,0},{3,1},{4,6},{5,7},{6,4},{7,5},{8,10},{9,11},{10,... | collective-permute-start | bytes 2359304 | tf_op jit(solution)/shard_map/ppermute | solution.py:953
  605.0 85.2 %collective-permute-start.61 = (bf16[4,3,48,1536]{3,2,1,0:T(8,128)(2,1)}, bf16[4,3,48,1536]{3,2,1,0:T(8,128)(2,1)}, u32[]{:S(2)}, u32[]{:S(2)}) collective-permute-start(bf16[4,3,48,1536]{3,2,1,0:T(8,128)(2,1)} %pad_maximum_fusion.5), channel_id=1, source_target_pairs={{0,3},{1,2},{2,1},{3,0},{4,7},{5,6},{6,5},{7,4},{8,11},{9,10},{10,... | collective-permute-start | bytes 5308424 | tf_op jit(solution)/shard_map/ppermute | solution.py:953
  607.8 168.1 %reduce-scatter.12.cloned.1.call-start = ((), (), s32[]{:S(2)}) async-start(), calls=%async_computation.11 | async-start | bytes 3981312 | tf_op jit(solution)/shard_map/reduce_scatter | solution.py:1265
  609.7 80.5 %collective-permute-start.60 = (bf16[4,3,48,1536]{3,2,1,0:T(8,128)(2,1)S(1)}, bf16[4,3,48,1536]{3,2,1,0:T(8,128)(2,1)S(1)}, u32[]{:S(2)}, u32[]{:S(2)}) collective-permute-start(bf16[4,3,48,1536]{3,2,1,0:T(8,128)(2,1)S(1)} %pad_maximum_fusion.4), channel_id=1, source_target_pairs={{0,2},{1,3},{2,0},{3,1},{4,6},{5,7},{6,4},{7,5},{8,10},{9,11},{10,... | collective-permute-start | bytes 5308424 | tf_op jit(solution)/shard_map/ppermute | solution.py:953
  610.1 81.3 %collective-permute-start.59 = (bf16[4,3,48,1536]{3,2,1,0:T(8,128)(2,1)S(1)}, bf16[4,3,48,1536]{3,2,1,0:T(8,128)(2,1)}, u32[]{:S(2)}, u32[]{:S(2)}) collective-permute-start(bf16[4,3,48,1536]{3,2,1,0:T(8,128)(2,1)S(1)} %pad_maximum_fusion.3), channel_id=1, source_target_pairs={{0,1},{1,0},{2,3},{3,2},{4,5},{5,4},{6,7},{7,6},{8,9},{9,8},{10,11... | collective-permute-start | bytes 5308424 | tf_op jit(solution)/shard_map/ppermute | solution.py:953
  705.1 145.3 %reduce-scatter.14.cloned.1.call-start = ((), (), s32[]{:S(2)}) async-start(), calls=%async_computation.12 | async-start | bytes 2211840 | tf_op jit(solution)/shard_map/reduce_scatter | solution.py:1280
  709.3 19.4 %collective-permute-start.64 = (bf16[48,3072]{1,0:T(8,128)(2,1)}, bf16[48,3072]{1,0:T(8,128)(2,1)S(1)}, u32[]{:S(2)}, u32[]{:S(2)}) collective-permute-start(bf16[48,3072]{1,0:T(8,128)(2,1)} %get-tuple-element.405), channel_id=1, source_target_pairs={{0,1},{1,0},{2,3},{3,2},{4,5},{5,4},{6,7},{7,6},{8,9},{9,8},{10,11... | collective-permute-start | bytes 884744 | tf_op jit(solution)/shard_map/ppermute | solution.py:953
  710.3 18.3 %collective-permute-start.65 = (bf16[48,3072]{1,0:T(8,128)(2,1)}, bf16[48,3072]{1,0:T(8,128)(2,1)S(1)}, u32[]{:S(2)}, u32[]{:S(2)}) collective-permute-start(bf16[48,3072]{1,0:T(8,128)(2,1)} %get-tuple-element.404), channel_id=1, source_target_pairs={{0,2},{1,3},{2,0},{3,1},{4,6},{5,7},{6,4},{7,5},{8,10},{9,11},{10,... | collective-permute-start | bytes 884744 | tf_op jit(solution)/shard_map/ppermute | solution.py:953
  712.2 16.5 %collective-permute-start.66 = (bf16[48,3072]{1,0:T(8,128)(2,1)}, bf16[48,3072]{1,0:T(8,128)(2,1)}, u32[]{:S(2)}, u32[]{:S(2)}) collective-permute-start(bf16[48,3072]{1,0:T(8,128)(2,1)} %get-tuple-element.403), channel_id=1, source_target_pairs={{0,3},{1,2},{2,1},{3,0},{4,7},{5,6},{6,5},{7,4},{8,11},{9,10},{10,... | collective-permute-start | bytes 884744 | tf_op jit(solution)/shard_map/ppermute | solution.py:953
  737.8 23.0 %collective-permute-start.73 = (bf16[256,1536]{1,0:T(8,128)(2,1)S(1)}, bf16[256,1536]{1,0:T(8,128)(2,1)}, u32[]{:S(2)}, u32[]{:S(2)}) collective-permute-start(bf16[256,1536]{1,0:T(8,128)(2,1)S(1)} %get-tuple-element.370), channel_id=1, source_target_pairs={{0,1},{1,0},{2,3},{3,2},{4,5},{5,4},{6,7},{7,6},{8,9},{9,8},{10,11... | collective-permute-start | bytes 2359304 | tf_op jit(solution)/shard_map/ppermute | solution.py:953
  739.3 21.5 %collective-permute-start.74 = (bf16[256,1536]{1,0:T(8,128)(2,1)S(1)}, bf16[256,1536]{1,0:T(8,128)(2,1)}, u32[]{:S(2)}, u32[]{:S(2)}) collective-permute-start(bf16[256,1536]{1,0:T(8,128)(2,1)S(1)} %get-tuple-element.369), channel_id=1, source_target_pairs={{0,2},{1,3},{2,0},{3,1},{4,6},{5,7},{6,4},{7,5},{8,10},{9,11},{10,... | collective-permute-start | bytes 2359304 | tf_op jit(solution)/shard_map/ppermute | solution.py:953
  740.4 34.3 %collective-permute-start.75 = (bf16[256,1536]{1,0:T(8,128)(2,1)S(1)}, bf16[256,1536]{1,0:T(8,128)(2,1)S(1)}, u32[]{:S(2)}, u32[]{:S(2)}) collective-permute-start(bf16[256,1536]{1,0:T(8,128)(2,1)S(1)} %get-tuple-element.368), channel_id=1, source_target_pairs={{0,1},{1,0},{2,3},{3,2},{4,5},{5,4},{6,7},{7,6},{8,9},{9,8},{10,11... | collective-permute-start | bytes 2359304 | tf_op jit(solution)/shard_map/ppermute | solution.py:953
  741.0 34.9 %collective-permute-start.76 = (bf16[256,1536]{1,0:T(8,128)(2,1)S(1)}, bf16[256,1536]{1,0:T(8,128)(2,1)}, u32[]{:S(2)}, u32[]{:S(2)}) collective-permute-start(bf16[256,1536]{1,0:T(8,128)(2,1)S(1)} %get-tuple-element.367), channel_id=1, source_target_pairs={{0,2},{1,3},{2,0},{3,1},{4,6},{5,7},{6,4},{7,5},{8,10},{9,11},{10,... | collective-permute-start | bytes 2359304 | tf_op jit(solution)/shard_map/ppermute | solution.py:953
  792.6 20.0 %collective-permute-start.84 = (bf16[256,1536]{1,0:T(8,128)(2,1)S(1)}, bf16[256,1536]{1,0:T(8,128)(2,1)S(1)}, u32[]{:S(2)}, u32[]{:S(2)}) collective-permute-start(bf16[256,1536]{1,0:T(8,128)(2,1)S(1)} %get-tuple-element.366), channel_id=1, source_target_pairs={{0,2},{1,3},{2,0},{3,1},{4,6},{5,7},{6,4},{7,5},{8,10},{9,11},{10,... | collective-permute-start | bytes 2359304 | tf_op jit(solution)/shard_map/ppermute | solution.py:953
  793.5 19.8 %collective-permute-start.85 = (bf16[256,1536]{1,0:T(8,128)(2,1)S(1)}, bf16[256,1536]{1,0:T(8,128)(2,1)S(1)}, u32[]{:S(2)}, u32[]{:S(2)}) collective-permute-start(bf16[256,1536]{1,0:T(8,128)(2,1)S(1)} %get-tuple-element.365), channel_id=1, source_target_pairs={{0,1},{1,0},{2,3},{3,2},{4,5},{5,4},{6,7},{7,6},{8,9},{9,8},{10,11... | collective-permute-start | bytes 2359304 | tf_op jit(solution)/shard_map/ppermute | solution.py:953
  815.2 17.9 %collective-permute-start.86 = (f32[5,48]{1,0:T(8,128)S(1)}, f32[5,48]{1,0:T(8,128)S(1)}, u32[]{:S(2)}, u32[]{:S(2)}) collective-permute-start(f32[5,48]{1,0:T(8,128)S(1)} %convolution_multiply_fusion), channel_id=1, source_target_pairs={{0,1},{1,0},{2,3},{3,2},{4,5},{5,4},{6,7},{7,6},{8,9},{9,8},{10,11... | collective-permute-start | bytes 2888 | tf_op jit(solution)/shard_map/ppermute | solution.py:953
  816.2 18.4 %collective-permute-start.87 = (f32[5,48]{1,0:T(8,128)S(1)}, f32[5,48]{1,0:T(8,128)S(1)}, u32[]{:S(2)}, u32[]{:S(2)}) collective-permute-start(f32[5,48]{1,0:T(8,128)S(1)} %convolution_multiply_fusion), channel_id=1, source_target_pairs={{0,2},{1,3},{2,0},{3,1},{4,6},{5,7},{6,4},{7,5},{8,10},{9,11},{10,... | collective-permute-start | bytes 2888 | tf_op jit(solution)/shard_map/ppermute | solution.py:953
  817.3 17.3 %collective-permute-start.88 = (f32[5,48]{1,0:T(8,128)S(1)}, f32[5,48]{1,0:T(8,128)S(1)}, u32[]{:S(2)}, u32[]{:S(2)}) collective-permute-start(f32[5,48]{1,0:T(8,128)S(1)} %convolution_multiply_fusion), channel_id=1, source_target_pairs={{0,3},{1,2},{2,1},{3,0},{4,7},{5,6},{6,5},{7,4},{8,11},{9,10},{10,... | collective-permute-start | bytes 2888 | tf_op jit(solution)/shard_map/ppermute | solution.py:953
  820.9 13.8 %collective-permute-start.89 = (bf16[48,2688]{1,0:T(8,128)(2,1)}, bf16[48,2688]{1,0:T(8,128)(2,1)S(1)}, u32[]{:S(2)}, u32[]{:S(2)}) collective-permute-start(bf16[48,2688]{1,0:T(8,128)(2,1)} %get-tuple-element.423), channel_id=1, source_target_pairs={{0,1},{1,0},{2,3},{3,2},{4,5},{5,4},{6,7},{7,6},{8,9},{9,8},{10,11... | collective-permute-start | bytes 774152 | tf_op jit(solution)/shard_map/ppermute | solution.py:953
  821.9 12.9 %collective-permute-start.90 = (bf16[48,2688]{1,0:T(8,128)(2,1)}, bf16[48,2688]{1,0:T(8,128)(2,1)S(1)}, u32[]{:S(2)}, u32[]{:S(2)}) collective-permute-start(bf16[48,2688]{1,0:T(8,128)(2,1)} %get-tuple-element.422), channel_id=1, source_target_pairs={{0,2},{1,3},{2,0},{3,1},{4,6},{5,7},{6,4},{7,5},{8,10},{9,11},{10,... | collective-permute-start | bytes 774152 | tf_op jit(solution)/shard_map/ppermute | solution.py:953
  (168 other events, 1587.0 us)
Sparse Core Ops, SparseCore 0:
  22.2 100.9 all-gather.3
  126.7 111.2 all-gather.5
  240.2 90.1 all-gather.7
  490.3 52.4 reduce-scatter.5
  545.0 97.8 reduce-scatter.7
  645.1 53.3 reduce-scatter.9
  705.2 42.0 reduce-scatter.11
  787.9 36.8 reduce-scatter.13
